TPU v7x, 512 devices: a whole 4x8x8 slice. The times are simulated.
512 devices in a mesh: space: 16 (over z_lo, x), tm: 16 (over y, core), fsdp: 2 (over z_hi).
Axes of the slice: x: 4, y: 8, z: 8 (z_hi: 2, z_lo: 4; z = z_hi * 4 + z_lo), core: 2. Of those that a mesh axis runs over, the one named last changes fastest.
Arguments:
- space_query: bfloat16 [2, 32, 1024, 1024], P('fsdp', 'tm', 'space'), may hold values from -6 to 6, as said below
- space_key: bfloat16 [2, 32, 1024, 1024], P('fsdp', 'tm', 'space'), may hold values from -6 to 6, as said below
- space_value: bfloat16 [2, 32, 1024, 1024], P('fsdp', 'tm', 'space'), may hold values from -6 to 6
- time_query: bfloat16 [2, 32, 1024, 1024], P('fsdp', 'tm', 'space'), may hold values from -6 to 6, as said below
- time_key: bfloat16 [2, 32, 1024, 1024], P('fsdp', 'tm', 'space'), may hold values from -6 to 6, as said below
- stream: bfloat16 [2, 32, 1024, 1024], P('fsdp', 'tm', 'space'), may hold values from -6 to 6
- cotangent: bfloat16 [2, 32, 1024, 1024], P('fsdp', 'tm', 'space'), may hold values from -6 to 6
- mix_weight: bfloat16 [1024, 1024], P(('space', 'tm', 'fsdp')), may hold values from -0.1875 to 0.1875
Outputs:
- grad_space_query: bfloat16 [2, 32, 1024, 1024], P('fsdp', 'tm', None, 'space')
- grad_space_key: bfloat16 [2, 32, 1024, 1024], P('fsdp', 'tm', None, 'space')
- grad_space_value: bfloat16 [2, 32, 1024, 1024], P('fsdp', 'tm', None, 'space')
- grad_time_query: bfloat16 [2, 32, 1024, 1024], P('fsdp', None, ('space', 'tm'))
- grad_time_key: bfloat16 [2, 32, 1024, 1024], P('fsdp', None, ('space', 'tm'))
- grad_stream: bfloat16 [2, 32, 1024, 1024], P('fsdp', 'tm', 'space')
- grad_mix_weight: float32 [1024, 1024], P(('space', 'tm', 'fsdp'))
Inputs may be any that keep to these rules, and one draw needn't show every extreme that they name: `space_query`: real-valued activations. `space_key`: real-valued activations. `time_query`: real-valued activations. `time_key`: real-valued activations.
All inputs are finite; a program needn't handle non-finite values.
Results may differ from a plain program's by a relative error of at most 0.012.
The roundings to bfloat16 on the way count: a program that leaves them out, or rounds other values in their place, can miss the bound.
Values may be sent and summed in bfloat16 or wider, within the bound.
No kernel may reach another device: no remote copies, remote signals or barrier semaphores. Data moves between devices by JAX's collectives and lax.ppermute only.
A program may use at most 64 MiB of HBM per device.

v0:
```python
import jax
import jax.numpy as jnp
from jax import lax
from jax.sharding import PartitionSpec as P

HD = 64


def softmax_rows(scores):
    largest = jnp.max(scores, axis=-1, keepdims=True)
    weights = jnp.exp(scores - largest)
    return weights / jnp.sum(weights, axis=-1, keepdims=True)


def time_grads(queries, key_rows, values, out_grad):
    clip_count, frames, tokens, feature = queries.shape
    head_count = feature // HD
    split_shape = (clip_count, frames, tokens, head_count, HD)
    scaling = HD ** (-0.5)
    query_heads = queries.reshape(split_shape)
    key_heads = key_rows.reshape(split_shape)
    value_heads = values.reshape(split_shape)
    grad_heads = out_grad.reshape(split_shape)
    scores = (
        jnp.einsum("bfshd,bgshd->bshfg", query_heads, key_heads, preferred_element_type=jnp.float32)
        * scaling
    )
    causal = lax.broadcasted_iota(jnp.int32, (frames, frames), 1) <= lax.broadcasted_iota(
        jnp.int32, (frames, frames), 0
    )
    scores = jnp.where(causal, scores, -jnp.inf)
    weights = softmax_rows(scores)
    rounded = weights.astype(jnp.bfloat16)
    prob_grad = jnp.einsum(
        "bfshd,bgshd->bshfg", grad_heads, value_heads, preferred_element_type=jnp.float32
    )
    row_delta = jnp.sum(weights * prob_grad, axis=-1, keepdims=True)
    score_grad = (weights * (prob_grad - row_delta) * scaling).astype(jnp.bfloat16)
    grad_query = jnp.einsum(
        "bshfg,bgshd->bfshd", score_grad, key_heads, preferred_element_type=jnp.float32
    )
    grad_key = jnp.einsum(
        "bshfg,bfshd->bgshd", score_grad, query_heads, preferred_element_type=jnp.float32
    )
    value_term = jnp.einsum(
        "bshfg,bfshd->bgshd", rounded, grad_heads, preferred_element_type=jnp.float32
    )
    grad_stream = (out_grad.astype(jnp.float32) + value_term.reshape(queries.shape)).astype(
        jnp.bfloat16
    )
    return (
        grad_query.reshape(queries.shape).astype(jnp.bfloat16),
        grad_key.reshape(queries.shape).astype(jnp.bfloat16),
        grad_stream,
    )


def space_grads(queries, key_rows, values, out_grad):
    clip_count, frames, tokens, feature = queries.shape
    head_count = feature // HD
    scaling = HD ** (-0.5)

    def frame_step(operands):
        query_frame, key_frame, value_frame, grad_frame = operands
        scores = (
            jnp.einsum("shd,thd->hst", query_frame, key_frame, preferred_element_type=jnp.float32)
            * scaling
        )
        weights = softmax_rows(scores)
        rounded = weights.astype(jnp.bfloat16)
        output = jnp.einsum(
            "hst,thd->shd", rounded, value_frame, preferred_element_type=jnp.float32
        ).astype(jnp.bfloat16)
        prob_grad = jnp.einsum(
            "shd,thd->hst", grad_frame, value_frame, preferred_element_type=jnp.float32
        )
        row_delta = jnp.sum(weights * prob_grad, axis=-1, keepdims=True)
        score_grad = (weights * (prob_grad - row_delta) * scaling).astype(jnp.bfloat16)
        grad_query = jnp.einsum(
            "hst,thd->shd", score_grad, key_frame, preferred_element_type=jnp.float32
        ).astype(jnp.bfloat16)
        grad_key = jnp.einsum(
            "hst,shd->thd", score_grad, query_frame, preferred_element_type=jnp.float32
        ).astype(jnp.bfloat16)
        grad_value = jnp.einsum(
            "hst,shd->thd", rounded, grad_frame, preferred_element_type=jnp.float32
        ).astype(jnp.bfloat16)
        return (grad_query, grad_key, grad_value, output)

    def shaped(tensor):
        return tensor.reshape(clip_count * frames, tokens, head_count, HD)

    results = lax.map(
        frame_step, (shaped(queries), shaped(key_rows), shaped(values), shaped(out_grad))
    )
    return tuple((result.reshape(queries.shape) for result in results))


def body(space_query, space_key, space_value, time_query, time_key, stream, cotangent, mix_weight):
    frame_parts = (
        lax.all_to_all(time_query, "tm", split_axis=2, concat_axis=1, tiled=True),
        lax.all_to_all(time_key, "tm", split_axis=2, concat_axis=1, tiled=True),
        lax.all_to_all(stream, "tm", split_axis=2, concat_axis=1, tiled=True),
        lax.all_to_all(cotangent, "tm", split_axis=2, concat_axis=1, tiled=True),
    )
    grad_time_query, grad_time_key, grad_frames = time_grads(
        frame_parts[0], frame_parts[1], frame_parts[2], frame_parts[3]
    )
    grad_stream = lax.all_to_all(grad_frames, "tm", split_axis=1, concat_axis=2, tiled=True)
    mix_grad = jnp.einsum(
        "bfsd,rd->bfsr",
        grad_stream,
        lax.all_gather(mix_weight, ("space", "tm", "fsdp"), axis=0, tiled=True),
        preferred_element_type=jnp.float32,
    ).astype(jnp.bfloat16)
    head_parts = (
        lax.all_to_all(space_query, "space", split_axis=3, concat_axis=2, tiled=True),
        lax.all_to_all(space_key, "space", split_axis=3, concat_axis=2, tiled=True),
        lax.all_to_all(space_value, "space", split_axis=3, concat_axis=2, tiled=True),
        lax.all_to_all(mix_grad, "space", split_axis=3, concat_axis=2, tiled=True),
    )
    grad_query, grad_key, grad_value, output = space_grads(
        head_parts[0], head_parts[1], head_parts[2], head_parts[3]
    )
    output_tokens = lax.all_to_all(output, "space", split_axis=2, concat_axis=3, tiled=True)
    flat_output = output_tokens.reshape(-1, output_tokens.shape[-1])
    flat_grad = grad_stream.reshape(-1, grad_stream.shape[-1])
    grad_mix_weight = lax.psum_scatter(
        lax.dot_general(
            flat_output, flat_grad, (((0,), (0,)), ((), ())), preferred_element_type=jnp.float32
        ),
        ("space", "tm", "fsdp"),
        scatter_dimension=0,
        tiled=True,
    )
    return (
        grad_query,
        grad_key,
        grad_value,
        grad_time_query,
        grad_time_key,
        grad_stream,
        grad_mix_weight,
    )


def solution(mesh):
    placed = (
        P("fsdp", "tm", "space", None),
        P("fsdp", "tm", "space", None),
        P("fsdp", "tm", "space", None),
        P("fsdp", "tm", "space", None),
        P("fsdp", "tm", "space", None),
        P("fsdp", "tm", "space", None),
        P("fsdp", "tm", "space", None),
        P(("space", "tm", "fsdp"), None),
    )
    return jax.shard_map(
        body,
        mesh=mesh,
        in_specs=placed,
        out_specs=(
            P("fsdp", "tm", None, "space"),
            P("fsdp", "tm", None, "space"),
            P("fsdp", "tm", None, "space"),
            P("fsdp", None, ("space", "tm"), None),
            P("fsdp", None, ("space", "tm"), None),
            P("fsdp", "tm", "space", None),
            P(("space", "tm", "fsdp"), None),
        ),
        check_vma=False,
    )
```

profile of v0, /device:TPU:1, one launch (start us, length us, event | category | flops | bytes accessed | tf_op | source)
XLA Modules:
  0.0 1421.5 jit_solution(2120005797782853892)
XLA Ops:
  7.9 1.9 copy.126
  9.8 10.2 all-to-all-start.3
  20.0 1.9 copy.128
  22.0 9.9 all-to-all-done.3
  31.9 3.4 all-to-all-start.4
  35.3 1.9 copy.124
  37.3 9.1 all-to-all-done.4
  46.4 3.4 all-to-all-start.2
  52.2 9.1 all-to-all-done.2
  61.3 8.1 all-to-all-start.1
  72.5 2.0 fusion.72
  74.5 5.5 all-to-all-done.1
  80.1 3.6 all-to-all-start
  83.7 1.7 convolution_bitcast_fusion
  87.7 5.3 all-to-all-done
  93.7 5.7 all-to-all-start.5
  100.9 10.4 all-to-all-done.5
  111.3 4.2 all-to-all-start.7
  116.3 952.8 %all-gather.3.cloned.1.call-done = bf16[512,2,1024]{2,1,0:T(2,128)(2,1)} async-done(((bf16[1,2,1024]{2,1,0:T(2,128)(2,1)}), bf16[512,2,1024]{2,1,0:T(2,128)(2,1)}) %all-gather.3.cloned.1.call-update) | async-done | bytes 2097168 | tf_op jit(solution)/shard_map/all_gather | solution.py:113
  1069.1 2.7 reshape.272
  1071.9 1.8 fusion.49
  1075.2 7.0 all-to-all-start.6
  1087.3 5.0 all-to-all-done.6
  1093.4 16.3 %while.16 = (s32[]{:T(128)}, bf16[2,1024,1,64]{1,3,2,0:T(8,128)(2,1)}, bf16[2,1024,1,64]{1,3,2,0:T(8,128)(2,1)}, bf16[2,1024,1,64]{1,3,2,0:T(8,128)(2,1)}, bf16[...) while((s32[]{:T(128)}, ...), condition=%wide.region_6.7_spmd, body=%wide.region_2.6_spmd.sunk | while | flops 831779840 | bytes 47769876 | solution.py:93
  1111.5 4.1 all-to-all-start.9
  1115.9 8.9 all-to-all-done.9
  1125.9 2.7 fusion.77
  1129.7 10.6 all-to-all-start.8
  1140.3 12.8 all-to-all-done.8
  1154.3 2.4 fusion.48
  1157.9 2.4 fusion.47
  1162.5 250.8 %all-reduce.3.cloned.1.call-done = f32[1024,1024]{1,0:T(8,128)} async-done(((f32[1024,1024]{1,0:T(8,128)}), f32[1024,1024]{1,0:T(8,128)}) %all-reduce.3.cloned.1.call-update) | async-done | bytes 4194320
  (121 shorter events, 45.1 us)
Async XLA Ops:
  7.2 62.3 %copy-start.7 = (bf16[1,2,64,1024]{3,2,1,0:T(8,128)(2,1)S(1)}, bf16[1,2,64,1024]{3,2,1,0:T(8,128)(2,1)}, u32[]{:S(2)}) copy-start(bf16[1,2,64,1024]{3,2,1,0:T(8,128)(2,1)} %param.11) | copy-start | bytes 786436
  7.2 1061.9 %all-gather.3.cloned.1.call-start = ((), (), s32[]{:S(2)}) async-start(), calls=%async_computation.10 | async-start | bytes 2101248 | tf_op jit(solution)/shard_map/all_gather | solution.py:113
  9.8 22.1 %all-to-all-start.3 = ((bf16[1,2,64,1024]{3,1,0,2:T(2,128)(2,1)}), bf16[1,2,64,1024]{3,1,0,2:T(2,128)(2,1)S(1)}, u32[]{:S(2)}, u32[]{:S(2)}) async-start(bf16[1,2,64,1024]{3,1,0,2:T(2,128)(2,1)} %copy.126), calls=%async_computation.3 | async-start | bytes 524288 | tf_op jit(solution)/shard_map/all_to_all | solution.py:101
  31.9 14.5 %all-to-all-start.4 = ((bf16[1,2,64,1024]{3,1,0,2:T(2,128)(2,1)}), bf16[1,2,64,1024]{3,1,0,2:T(2,128)(2,1)S(1)}, u32[]{:S(2)}, u32[]{:S(2)}) async-start(bf16[1,2,64,1024]{3,1,0,2:T(2,128)(2,1)} %copy.128), calls=%async_computation.4 | async-start | bytes 524288 | tf_op jit(solution)/shard_map/all_to_all | solution.py:102
  46.4 14.9 %all-to-all-start.2 = ((bf16[1,2,64,1024]{3,1,0,2:T(2,128)(2,1)}), bf16[1,2,64,1024]{3,1,0,2:T(2,128)(2,1)S(1)}, u32[]{:S(2)}, u32[]{:S(2)}) async-start(bf16[1,2,64,1024]{3,1,0,2:T(2,128)(2,1)} %copy.124), calls=%async_computation.2 | async-start | bytes 524288 | tf_op jit(solution)/shard_map/all_to_all | solution.py:104
  61.3 18.8 %all-to-all-start.1 = ((bf16[16,2,4096]{2,1,0:T(2,128)(2,1)}), bf16[16,2,4096]{2,1,0:T(2,128)(2,1)S(1)}, u32[]{:S(2)}, u32[]{:S(2)}) async-start(bf16[16,2,4096]{2,1,0:T(2,128)(2,1)} %reshape.278), calls=%async_computation.1 | async-start | bytes 524288 | tf_op jit(solution)/shard_map/all_to_all | solution.py:117
  71.4 12.3 copy-start.5
  71.9 11.8 copy-start.3
  80.1 3.7 copy-start
  80.1 12.9 all-to-all-start
  83.7 15.6 %copy-start.8 = (bf16[1,2,64,1024]{3,2,1,0:T(8,128)(2,1)S(1)}, bf16[1,2,64,1024]{3,2,1,0:T(8,128)(2,1)}, u32[]{:S(2)}) copy-start(bf16[1,2,64,1024]{3,2,1,0:T(8,128)(2,1)} %param.12) | copy-start | bytes 786436
  93.0 0.7 copy-start.1
  93.7 17.6 %all-to-all-start.5 = ((bf16[1,32,4,1024]{3,2,0,1:T(4,128)(2,1)}), bf16[1,32,4,1024]{3,2,0,1:T(4,128)(2,1)S(1)}, u32[]{:S(2)}, u32[]{:S(2)}) async-start(bf16[1,32,4,1024]{3,2,0,1:T(4,128)(2,1)} %copy.135), calls=%async_computation.5 | async-start | bytes 524288 | tf_op jit(solution)/shard_map/all_to_all | solution.py:109
  111.3 963.9 %all-to-all-start.7 = ((bf16[16,2,4096]{2,1,0:T(2,128)(2,1)}), bf16[16,2,4096]{2,1,0:T(2,128)(2,1)}, u32[]{:S(2)}, u32[]{:S(2)}) async-start(bf16[16,2,4096]{2,1,0:T(2,128)(2,1)} %reshape.282), calls=%async_computation.7 | async-start | bytes 524288 | tf_op jit(solution)/shard_map/all_to_all | solution.py:119
  1073.6 10.6 copy-start.2
  1075.2 17.2 %all-to-all-start.6 = ((bf16[16,2,4096]{2,1,0:T(2,128)(2,1)}), bf16[16,2,4096]{2,1,0:T(2,128)(2,1)S(1)}, u32[]{:S(2)}, u32[]{:S(2)}) async-start(bf16[16,2,4096]{2,1,0:T(2,128)(2,1)} %reshape.280), calls=%async_computation.6 | async-start | bytes 524288 | tf_op jit(solution)/shard_map/all_to_all | solution.py:120
  1094.9 1.0 copy-start.14
  1096.9 1.2 copy-start.15
  1098.1 1.2 copy-start.10
  1098.1 2.0 copy-start.12
  1100.1 0.7 copy-start.11
  1103.0 1.0 copy-start.14
  1105.0 1.2 copy-start.15
  1106.2 1.2 copy-start.10
  1106.2 2.0 copy-start.12
  1108.2 0.7 copy-start.11
  1111.5 13.4 all-to-all-start.9
  1115.6 297.8 %all-reduce.3.cloned.1.call-start = ((), (), s32[]{:S(2)}) async-start(), calls=%async_computation.11 | async-start | bytes 8388608
  1125.9 2.8 copy-start.9
  1128.7 25.6 %copy-start.6 = (bf16[32,4,16,64]{3,2,1,0:T(8,128)(2,1)S(1)}, bf16[32,4,16,64]{3,2,1,0:T(8,128)(2,1)}, u32[]{:S(2)}) copy-start(bf16[32,4,16,64]{3,2,1,0:T(8,128)(2,1)} %copy-done.5) | copy-start | bytes 786436
  1129.7 23.4 %all-to-all-start.8 = ((bf16[1,2,64,1024]{3,1,0,2:T(2,128)(2,1)}), bf16[1,2,64,1024]{3,1,0,2:T(2,128)(2,1)S(1)}, u32[]{:S(2)}, u32[]{:S(2)}) async-start(bf16[1,2,64,1024]{3,1,0,2:T(2,128)(2,1)} %copy.145), calls=%async_computation.8 | async-start | bytes 524288 | tf_op jit(solution)/shard_map/all_to_all | solution.py:103
  1154.3 3.6 copy-start.4
  (2 other events, 1.4 us)
Sparse Core Ops, SparseCore 0:
  10.2 1058.8 all-gather.2
  1128.8 284.4 all-reduce.2
where the time goes:
time: 1420 us
  waiting for transfers between devices  1280 us (90%)
  starting transfers between devices  60.6 us (4%)
  local copies, waits for them, and re-layouts  37.3 us (3%)
  matrix products  24.1 us (2%)
  between operations  14.5 us (1%)
    all_gather x1, waiting for transfers between devices, body(): lax.all_gather(mix_weight, ('space', 'tm', 'fsdp'), axis=0, tiled=True)  953 us
    unnamed x3, waiting for transfers between devices  252 us
  transfers between devices with their start and end apart: 12, of which 11 were waited for; matrix products, arithmetic and copies ran while one was open for 3% of the time, Pallas kernels for 0%

commit v1 on v0

v1 whole, which is shorter than its diff:
```python
import jax
import jax.numpy as jnp
from jax import lax
from jax.experimental import pallas as pl
from jax.experimental.pallas import tpu as pltpu
from jax.sharding import Mesh, PartitionSpec as P

HD = 64
SCALING = HD ** (-0.5)
TM = ("y", "c")
BF = jnp.bfloat16
F32 = jnp.float32
LIMIT = 48 * 1024 * 1024
VM = pl.BlockSpec(memory_space=pltpu.VMEM)
SM = pl.BlockSpec(memory_space=pltpu.SMEM)


def call(kernel, outs, scratch=(), smem=0, n_in=1, flops=0, moved=0, name=None):
    shapes = [jax.ShapeDtypeStruct(s, d) for s, d in outs]
    return pl.pallas_call(
        kernel,
        out_shape=shapes,
        in_specs=[SM] * smem + [VM] * n_in,
        out_specs=[VM] * len(shapes),
        scratch_shapes=list(scratch),
        compiler_params=pltpu.CompilerParams(vmem_limit_bytes=LIMIT),
        cost_estimate=pl.CostEstimate(flops=flops, bytes_accessed=moved, transcendentals=0),
        name=name,
    )


def dot(a, b, dims):
    return lax.dot_general(a, b, (dims, ((), ())), preferred_element_type=F32)


def pack_time(tq, tk, st, ct, w, o):
    refs = (tq, tk, st, ct)
    for j in range(8):
        lanes = slice(128 * j, 128 * j + 128)
        wide = [[ref[f, :, lanes].astype(F32) for f in range(2)] for ref in refs]
        for g in range(16):
            rows = slice(4 * g, 4 * g + 4)
            block = jnp.concatenate([wide[a][f][rows] for a in range(4) for f in range(2)], 0)
            o[g, 32 * j : 32 * j + 32, :] = block.astype(BF)
    own = w[...].astype(F32)
    own = jnp.concatenate([own[:, 128 * j : 128 * j + 128] for j in range(8)], 0).astype(BF)
    for g in range(16):
        o[g, 256:272, :] = own


def time_grads(r, gq, gk, gs, wo):
    row = lax.broadcasted_iota(jnp.int32, (128, 128), 0)
    col = lax.broadcasted_iota(jnp.int32, (128, 128), 1)
    allowed = ((row & 3) == (col & 3)) & (row <= col)
    first = col < 64
    zero = jnp.zeros((128, 128), BF)
    kept = []
    for j in range(8):
        block = r[:, 32 * j : 32 * j + 32, :].astype(F32)
        q, k, v, g = (block[:, 8 * a : 8 * a + 8, :].reshape(128, 128).astype(BF) for a in range(4))
        sum_q = sum_k = sum_v = None
        for h in range(2):
            own = first if h == 0 else jnp.logical_not(first)
            qh, kh, gh = (jnp.where(own, t, zero) for t in (q, k, g))
            score = dot(k, qh, ((1,), (1,))) * SCALING
            score = jnp.where(allowed, score, -jnp.inf)
            e = jnp.exp(score - jnp.max(score, axis=0, keepdims=True))
            weight = e / jnp.sum(e, axis=0, keepdims=True)
            prob = dot(v, gh, ((1,), (1,)))
            delta = jnp.sum(weight * prob, axis=0, keepdims=True)
            ds = (weight * (prob - delta) * SCALING).astype(BF)
            part_k = dot(ds, qh, ((1,), (0,)))
            part_v = dot(weight.astype(BF), gh, ((1,), (0,)))
            part_q = dot(ds, kh, ((0,), (0,)))
            sum_q = part_q if h == 0 else sum_q + part_q
            sum_k = part_k if h == 0 else sum_k + part_k
            sum_v = part_v if h == 0 else sum_v + part_v
        lanes = slice(128 * j, 128 * j + 128)
        gq[:, lanes] = sum_q.astype(BF)
        gk[:, lanes] = sum_k.astype(BF)
        kept.append((g.astype(F32) + sum_v).reshape(16, 8, 128))
        if j % 2 == 1:
            gs[:, 8 * j - 8 : 8 * j + 8, :] = jnp.concatenate(kept, 1).astype(BF)
            kept = []
    rows = r[:, 256:272, :].astype(F32)
    for j in range(8):
        wo[:, 128 * j : 128 * j + 128] = jnp.concatenate(
            [rows[g, 2 * j : 2 * j + 2, :] for g in range(16)], 0
        ).astype(BF)


def unpack_stream(r, gs, wide):
    for j in range(8):
        lanes = slice(128 * j, 128 * j + 128)
        block = r[:, 8 * j : 8 * j + 8, :].astype(F32)
        for f in range(2):
            part = jnp.concatenate([block[g, 4 * f : 4 * f + 4, :] for g in range(16)], 0).astype(BF)
            gs[f, :, lanes] = part
            for m in range(4):
                wide[m, 64 * f : 64 * f + 64, lanes] = part


def pack_space(ids, q, k, v, *outs):
    z = ids[0]
    for n in range(4):
        at = pl.multiple_of(lax.rem(z + n, 4) * 256, 256)
        for a, ref in enumerate((q, k, v)):
            turned = ref[:, pl.ds(at, 256)].T
            for x in range(4):
                outs[n][x, a, :, :] = turned[64 * x : 64 * x + 64, :]


def turn_space(ids, *refs):
    ins, outs = refs[:4], refs[4:]
    x = ids[1]
    for m in range(4):
        at = lax.rem(x + m, 4)
        for n in range(4):
            outs[m][n] = ins[n][at]


def space_forward(ids, s0, s1, s2, s3, heads, stats, o0, o1, o2, o3, buf, ot):
    z, x = ids[0], ids[1]
    for m, s in enumerate((s0, s1, s2, s3)):
        for n in range(4):
            buf[lax.rem(z + 4 - n, 4) * 4 + lax.rem(x + 4 - m, 4)] = s[n]
    for a in range(3):
        for f in range(2):
            heads[a, f] = jnp.concatenate(
                [buf[i, a, :, 64 * f : 64 * f + 64] for i in range(16)], 1
            )
    for f in range(2):
        k = heads[1, f].T
        v = heads[2, f]

        def tile(t, carry):
            at = pl.ds(pl.multiple_of(t * 256, 256), 256)
            q = heads[0, f, :, at] * jnp.asarray(SCALING, BF)
            score = dot(k, q, ((1,), (0,)))
            largest = jnp.max(score, axis=0, keepdims=True)
            e = jnp.exp(score - largest)
            inverse = 1.0 / jnp.sum(e, axis=0, keepdims=True)
            stats[f, 0:1, at] = largest
            stats[f, 1:2, at] = inverse
            weight = (e * inverse).astype(BF)
            ot[t, f] = dot(v, weight, ((1,), (0,))).astype(BF)
            return carry

        lax.fori_loop(0, 4, tile, 0)
    for n, o in enumerate((o0, o1, o2, o3)):
        at = lax.rem(z + n, 4)
        for f in range(2):
            o[:, 256 * f : 256 * f + 256] = ot[at, f]


def mix_grads(g, w0, w1, w2, w3, m0, m1, m2, m3):
    for w, m in ((w0, m0), (w1, m1), (w2, m2), (w3, m3)):
        for x in range(4):
            m[:, 128 * x : 128 * x + 128] = dot(w[...], g[x], ((1,), (1,))).astype(BF)


def weight_grads(ids, g, r0, r1, r2, r3, o, buf):
    z = ids[0]
    for n, r in enumerate((r0, r1, r2, r3)):
        buf[lax.rem(z + 4 - n, 4)] = r[...]
    left = buf[...].reshape(256, 512)
    for d in range(4):
        lanes = slice(256 * d, 256 * d + 256)
        right = jnp.concatenate(
            [g[x, 64 * f : 64 * f + 64, lanes] for f in range(2) for x in range(4)], 0
        )
        total = dot(left, right, ((1,), (0,))).reshape(4, 16, 4, 256)
        for y in range(16):
            o[y, :, lanes] = jnp.concatenate([total[n, y] for n in range(4)], 0).astype(BF)


def space_backward(ids, heads, stats, m0, m1, m2, m3, gq, gk, gv, buf, got, ds_all, w_all):
    z = ids[0]
    for n, m in enumerate((m0, m1, m2, m3)):
        buf[lax.rem(z + n, 4)] = m[...]
    scale = jnp.asarray(SCALING, BF)
    for f in range(2):
        got[...] = jnp.concatenate(
            [buf[n, :, 128 * x + 64 * f : 128 * x + 64 * f + 64] for n in range(4) for x in range(4)], 1
        )
        kt = heads[1, f]
        k = kt.T
        v = heads[2, f].T
        kt = kt * scale

        def tile(t, carry):
            at = pl.ds(pl.multiple_of(t * 256, 256), 256)
            q = heads[0, f, :, at] * scale
            weight = jnp.exp(dot(k, q, ((1,), (0,))) - stats[f, 0:1, at]) * stats[f, 1:2, at]
            prob = dot(v, got[:, at], ((1,), (0,)))
            delta = jnp.sum(weight * prob, axis=0, keepdims=True)
            ds = (weight * (prob - delta)).astype(BF)
            ds_all[:, at] = ds
            w_all[:, at] = weight.astype(BF)
            gq[f, at, :] = dot(kt, ds, ((1,), (0,))).T.astype(BF)
            return carry

        lax.fori_loop(0, 4, tile, 0)
        gk[f] = dot(ds_all[...], (heads[0, f] * scale).T, ((1,), (0,))).astype(BF)
        gv[f] = dot(w_all[...], got[...].T, ((1,), (0,))).astype(BF)


def shift(value, axis, by):
    return lax.ppermute(value, axis, [(i, (i + by) % 4) for i in range(4)])


def body(space_query, space_key, space_value, time_query, time_key, stream, cotangent, mix_weight):
    ids = jnp.stack([lax.axis_index("z"), lax.axis_index("x")]).astype(jnp.int32)

    packed = call(pack_time, [((16, 272, 128), BF)], n_in=5, moved=2 << 20, name="pack_time")(
        *(t.reshape(2, 64, 1024) for t in (time_query, time_key, stream, cotangent)), mix_weight
    )[0]
    frames = lax.all_to_all(packed, TM, 0, 0, tiled=True)

    sent = call(pack_space, [((4, 3, 64, 128), BF)] * 4, smem=1, n_in=3, moved=1536 << 10, name="pack_space")(
        ids, *(t.reshape(128, 1024) for t in (space_query, space_key, space_value))
    )
    along_z = [sent[0]] + [shift(sent[n], "z", n) for n in (1, 2, 3)]
    turned = call(turn_space, [((4, 3, 64, 128), BF)] * 4, smem=1, n_in=4, moved=1536 << 10, name="turn_space")(
        ids, *along_z
    )
    along_x = [turned[0]] + [shift(turned[m], "x", m) for m in (1, 2, 3)]

    grad_time_query, grad_time_key, grad_frames, own_rows = call(
        time_grads,
        [((128, 1024), BF), ((128, 1024), BF), ((16, 64, 128), BF), ((32, 1024), BF)],
        flops=1 << 30,
        moved=2 << 20,
        name="time_grads",
    )(frames)
    back = lax.all_to_all(grad_frames, TM, 0, 0, tiled=True)

    other_rows = lax.ppermute(own_rows, "f", [(0, 1), (1, 0)])
    is_first = lax.axis_index("f") == 0
    low = jnp.where(is_first, own_rows, other_rows).reshape(16, 1, 2, 1024)
    high = jnp.where(is_first, other_rows, own_rows).reshape(16, 1, 2, 1024)
    rows = jnp.concatenate([low, high], axis=1).reshape(64, 1024)
    all_rows = [rows] + [shift(rows, "z", n) for n in (1, 2, 3)]

    heads, stats, *outputs = call(
        space_forward,
        [((3, 2, 64, 1024), BF), ((2, 2, 1024), F32)] + [((64, 512), BF)] * 4,
        scratch=[pltpu.VMEM((16, 3, 64, 128), BF), pltpu.VMEM((4, 2, 64, 256), BF)],
        smem=1,
        n_in=4,
        flops=4 << 30,
        moved=2 << 20,
        name="space_forward",
    )(ids, *along_x)
    outputs = [outputs[0]] + [shift(outputs[n], "z", n) for n in (1, 2, 3)]

    grad_stream, wide = call(
        unpack_stream, [((2, 64, 1024), BF), ((4, 128, 1024), BF)], moved=1536 << 10, name="unpack_stream"
    )(back)
    gathered = lax.all_to_all(wide, "x", 0, 0, tiled=True)

    mixed = call(
        mix_grads, [((64, 512), BF)] * 4, n_in=5, flops=1 << 28, moved=2 << 20, name="mix_grads"
    )(gathered, *all_rows)
    mixed = [mixed[0]] + [shift(mixed[n], "z", -n) for n in (1, 2, 3)]

    partial = call(
        weight_grads,
        [((16, 16, 1024), BF)],
        scratch=[pltpu.VMEM((4, 64, 512), BF)],
        smem=1,
        n_in=5,
        flops=1 << 28,
        moved=2 << 20,
        name="weight_grads",
    )(ids, gathered, *outputs)[0]
    partial = lax.all_to_all(partial, TM, 0, 0, tiled=True)

    grad_query, grad_key, grad_value = call(
        space_backward,
        [((2, 1024, 64), BF)] * 3,
        scratch=[
            pltpu.VMEM((4, 64, 512), BF),
            pltpu.VMEM((64, 1024), BF),
            pltpu.VMEM((1024, 1024), BF),
            pltpu.VMEM((1024, 1024), BF),
        ],
        smem=1,
        n_in=6,
        flops=8 << 30,
        moved=4 << 20,
        name="space_backward",
    )(ids, heads, stats, *mixed)

    partial = jnp.sum(partial.astype(F32), axis=0).reshape(8, 2, 1024)
    partial = lax.all_to_all(partial, ("z", "f"), 0, 0, tiled=True)
    grad_mix_weight = jnp.sum(partial, axis=0)

    frame_shape = (1, 2, 1024, 64)
    time_shape = (1, 32, 4, 1024)
    return (
        grad_query.reshape(frame_shape),
        grad_key.reshape(frame_shape),
        grad_value.reshape(frame_shape),
        grad_time_query.reshape(time_shape),
        grad_time_key.reshape(time_shape),
        grad_stream.reshape(1, 2, 64, 1024),
        grad_mix_weight,
    )


def solution(mesh):
    fine = Mesh(mesh.devices.reshape(4, 4, 8, 2, 2), ("z", "x", "y", "c", "f"))
    tokens = P("f", TM, ("z", "x"), None)
    feature = P("f", TM, None, ("z", "x"))
    time = P("f", None, ("z", "x", "y", "c"), None)
    rows = P(("z", "x", "y", "c", "f"), None)
    return jax.shard_map(
        body,
        mesh=fine,
        in_specs=(tokens,) * 7 + (rows,),
        out_specs=(feature,) * 3 + (time,) * 2 + (tokens, rows),
        check_vma=False,
    )
```

time: 1420 us -> 188 us (0.13)
  the two profiles are of different devices: /device:TPU:1 before, /device:TPU:2 now
where the time goes in v1:
time: 188 us; the launch traced here: 187 us
  starting transfers between devices  89.8 us (48%)
  blocking collectives  37.3 us (20%)
  Pallas kernels  29.3 us (16%)
  waiting for transfers between devices  18.2 us (10%)
  local copies, waits for them, and re-layouts  9.57 us (5%)
  other arithmetic  2.02 us (1%)
    ppermute x15, starting transfers between devices, shift(): return lax.ppermute(value, axis, [(i, (i + by) % 4) for i in range(4)])  58.5 us
    all_to_all x1, blocking collectives, body(): frames = lax.all_to_all(packed, TM, 0, 0, tiled=True)  37.3 us
    ppermute x15, waiting for transfers between devices, shift(): return lax.ppermute(value, axis, [(i, (i + by) % 4) for i in range(4)])  15.5 us
    pallas_call x1, Pallas kernels, body(): call(space_backward, [((2, 1024, 64), BF)] * 3, scratch=[pltpu.VMEM((4, 6...  11.6 us
    ppermute x1, starting transfers between devices, body(): other_rows = lax.ppermute(own_rows, 'f', [(0, 1), (1, 0)])  8.5 us
    all_to_all x1, starting transfers between devices, body(): partial = lax.all_to_all(partial, ('z', 'f'), 0, 0, tiled=True)  8.37 us
    pallas_call x1, Pallas kernels, body(): call(space_forward, [((3, 2, 64, 1024), BF), ((2, 2, 1024), F32)] + [((64...  7.75 us
    unnamed x19, local copies, waits for them, and re-layouts  7.19 us
  transfers between devices with their start and end apart: 20, of which 10 were waited for; matrix products, arithmetic and copies ran while one was open for 3% of the time, Pallas kernels for 13%

profile of v1, /device:TPU:2, one launch (start us, length us, event | category | flops | bytes accessed | tf_op | source)
XLA Modules:
  0.0 187.2 jit_solution(100586134517521552)
XLA Ops:
  5.4 37.3 %all_to_all.25.r = bf16[16,272,128]{2,1,0:T(8,128)(2,1)S(1)} all-to-all(bf16[16,272,128]{2,1,0:T(8,128)(2,1)S(1)} %pack_time.1), channel_id=1, replica_groups=mesh['z'=4,'x'=4,'y'=8,'c'=2,'f'=2] {'y','c'}, dimensions={0} | all-to-all | bytes 2228224 | tf_op jit(solution)/shard_map/all_to_all | solution.py:218
  42.7 3.5 %time_grads.1 = (bf16[128,1024]{1,0:T(8,128)(2,1)S(1)}, bf16[128,1024]{1,0:T(8,128)(2,1)S(1)}, bf16[16,64,128]{2,1,0:T(8,128)(2,1)}, bf16[32,1024]{1,0:T(8,128)(2,1)S(1)}) custom-call(bf16[16,272,128]{2,1,0:T(8,128)(2,1)S(1)} %all_to_all.25.r), custom_call_target="tpu_custom_call" | custom-call | flops 1073741824 | bytes 2097152 | tf_op jit(solution)/shard_map/time_grads/pallas_call | solution.py:229
  46.2 3.5 %all-to-all-start.1 = ((bf16[16,64,128]{2,1,0:T(8,128)(2,1)}), bf16[16,64,128]{2,1,0:T(8,128)(2,1)S(1)}, u32[]{:S(2)}, u32[]{:S(2)}) async-start(bf16[16,64,128]{2,1,0:T(8,128)(2,1)} %get-tuple-element.44), calls=%async_computation.1 | async-start | bytes 524288 | tf_op jit(solution)/shard_map/all_to_all | solution.py:236
  50.7 4.3 %collective-permute-start = (bf16[4,3,64,128]{3,2,1,0:T(8,128)(2,1)S(1)}, bf16[4,3,64,128]{3,2,1,0:T(8,128)(2,1)S(1)}, u32[]{:S(2)}, u32[]{:S(2)}) collective-permute-start(bf16[4,3,64,128]{3,2,1,0:T(8,128)(2,1)S(1)} %get-tuple-element.35), channel_id=1, source_target_pairs={{0,128},{128,256},{256,384},{384,0},{1,129},{129,257},{257,385},{3... | collective-permute-start | bytes 589832 | tf_op jit(solution)/shard_map/ppermute | solution.py:209
  55.0 6.1 %collective-permute-start.1 = (bf16[4,3,64,128]{3,2,1,0:T(8,128)(2,1)S(1)}, bf16[4,3,64,128]{3,2,1,0:T(8,128)(2,1)S(1)}, u32[]{:S(2)}, u32[]{:S(2)}) collective-permute-start(bf16[4,3,64,128]{3,2,1,0:T(8,128)(2,1)S(1)} %get-tuple-element.36), channel_id=1, source_target_pairs={{0,256},{128,384},{256,0},{384,128},{1,257},{129,385},{257,1},{385... | collective-permute-start | bytes 589832 | tf_op jit(solution)/shard_map/ppermute | solution.py:209
  61.1 2.5 %collective-permute-start.2 = (bf16[4,3,64,128]{3,2,1,0:T(8,128)(2,1)S(1)}, bf16[4,3,64,128]{3,2,1,0:T(8,128)(2,1)S(1)}, u32[]{:S(2)}, u32[]{:S(2)}) collective-permute-start(bf16[4,3,64,128]{3,2,1,0:T(8,128)(2,1)S(1)} %get-tuple-element.37), channel_id=1, source_target_pairs={{0,384},{128,0},{256,128},{384,256},{1,385},{129,1},{257,129},{385... | collective-permute-start | bytes 589832 | tf_op jit(solution)/shard_map/ppermute | solution.py:209
  64.9 4.8 %all-to-all-start.2 = ((bf16[4,128,1024]{2,1,0:T(8,128)(2,1)}), bf16[4,128,1024]{2,1,0:T(8,128)(2,1)S(1)}, u32[]{:S(2)}, u32[]{:S(2)}) async-start(bf16[4,128,1024]{2,1,0:T(8,128)(2,1)} %get-tuple-element.45), calls=%async_computation.2 | async-start | bytes 2097152 | tf_op jit(solution)/shard_map/all_to_all | solution.py:260
  69.8 2.7 %collective-permute-done.1.refs_2_ = bf16[4,3,64,128]{3,2,1,0:T(8,128)(2,1)S(1)} collective-permute-done((bf16[4,3,64,128]{3,2,1,0:T(8,128)(2,1)S(1)}, bf16[4,3,64,128]{3,2,1,0:T(8,128)(2,1)S(1)}, u32[]{:S(2)}, u32[]{:S(2)}) %collective-permute-start.1) | collective-permute-done | bytes 196640 | tf_op jit(solution)/shard_map/ppermute | solution.py:209
  74.2 3.4 %collective-permute-start.3 = (bf16[4,3,64,128]{3,2,1,0:T(8,128)(2,1)S(1)}, bf16[4,3,64,128]{3,2,1,0:T(8,128)(2,1)S(1)}, u32[]{:S(2)}, u32[]{:S(2)}) collective-permute-start(bf16[4,3,64,128]{3,2,1,0:T(8,128)(2,1)S(1)} %get-tuple-element.39), channel_id=1, source_target_pairs={{0,32},{32,64},{64,96},{96,0},{1,33},{33,65},{65,97},{97,1},{2,34}... | collective-permute-start | bytes 589832 | tf_op jit(solution)/shard_map/ppermute | solution.py:209
  77.6 3.0 %collective-permute-start.4 = (bf16[4,3,64,128]{3,2,1,0:T(8,128)(2,1)S(1)}, bf16[4,3,64,128]{3,2,1,0:T(8,128)(2,1)S(1)}, u32[]{:S(2)}, u32[]{:S(2)}) collective-permute-start(bf16[4,3,64,128]{3,2,1,0:T(8,128)(2,1)S(1)} %get-tuple-element.40), channel_id=1, source_target_pairs={{0,64},{32,96},{64,0},{96,32},{1,65},{33,97},{65,1},{97,33},{2,66}... | collective-permute-start | bytes 589832 | tf_op jit(solution)/shard_map/ppermute | solution.py:209
  80.6 4.1 %collective-permute-start.5 = (bf16[4,3,64,128]{3,2,1,0:T(8,128)(2,1)S(1)}, bf16[4,3,64,128]{3,2,1,0:T(8,128)(2,1)S(1)}, u32[]{:S(2)}, u32[]{:S(2)}) collective-permute-start(bf16[4,3,64,128]{3,2,1,0:T(8,128)(2,1)S(1)} %get-tuple-element.41), channel_id=1, source_target_pairs={{0,96},{32,0},{64,32},{96,64},{1,97},{33,1},{65,33},{97,65},{2,98}... | collective-permute-start | bytes 589832 | tf_op jit(solution)/shard_map/ppermute | solution.py:209
  84.7 2.3 %collective-permute-done.3.s1 = bf16[4,3,64,128]{3,2,1,0:T(8,128)(2,1)S(1)} collective-permute-done((bf16[4,3,64,128]{3,2,1,0:T(8,128)(2,1)S(1)}, bf16[4,3,64,128]{3,2,1,0:T(8,128)(2,1)S(1)}, u32[]{:S(2)}, u32[]{:S(2)}) %collective-permute-start.3) | collective-permute-done | bytes 196640 | tf_op jit(solution)/shard_map/ppermute | solution.py:209
  87.1 1.8 collective-permute-done.4.s2
  88.9 2.5 %collective-permute-done.5.s3 = bf16[4,3,64,128]{3,2,1,0:T(8,128)(2,1)S(1)} collective-permute-done((bf16[4,3,64,128]{3,2,1,0:T(8,128)(2,1)S(1)}, bf16[4,3,64,128]{3,2,1,0:T(8,128)(2,1)S(1)}, u32[]{:S(2)}, u32[]{:S(2)}) %collective-permute-start.5) | collective-permute-done | bytes 196640 | tf_op jit(solution)/shard_map/ppermute | solution.py:209
  91.4 7.7 %space_forward.1 = (bf16[3,2,64,1024]{3,2,1,0:T(8,128)(2,1)S(1)}, f32[2,2,1024]{2,1,0:T(2,128)S(1)}, bf16[64,512]{1,0:T(8,128)(2,1)S(1)}, bf16[64,512]{1,0:T(8,1...) custom-call(s32[2]{0:T(128)S(1)} %pad_add_fusion.ids, ...), custom_call_target="tpu_custom_call" | custom-call | flops 4294967296 | bytes 2097152 | tf_op jit(solution)/shard_map/space_forward/pallas_call | solution.py:245
  99.2 5.9 %collective-permute-start.13 = (bf16[64,512]{1,0:T(8,128)(2,1)S(1)}, bf16[64,512]{1,0:T(8,128)(2,1)S(1)}, u32[]{:S(2)}, u32[]{:S(2)}) collective-permute-start(bf16[64,512]{1,0:T(8,128)(2,1)S(1)} %get-tuple-element.58), channel_id=1, source_target_pairs={{0,128},{128,256},{256,384},{384,0},{1,129},{129,257},{257,385},{3... | collective-permute-start | bytes 196616 | tf_op jit(solution)/shard_map/ppermute | solution.py:209
  105.0 3.5 %collective-permute-start.14 = (bf16[64,512]{1,0:T(8,128)(2,1)S(1)}, bf16[64,512]{1,0:T(8,128)(2,1)S(1)}, u32[]{:S(2)}, u32[]{:S(2)}) collective-permute-start(bf16[64,512]{1,0:T(8,128)(2,1)S(1)} %get-tuple-element.59), channel_id=1, source_target_pairs={{0,256},{128,384},{256,0},{384,128},{1,257},{129,385},{257,1},{385... | collective-permute-start | bytes 196616 | tf_op jit(solution)/shard_map/ppermute | solution.py:209
  108.5 2.7 %collective-permute-start.15 = (bf16[64,512]{1,0:T(8,128)(2,1)S(1)}, bf16[64,512]{1,0:T(8,128)(2,1)S(1)}, u32[]{:S(2)}, u32[]{:S(2)}) collective-permute-start(bf16[64,512]{1,0:T(8,128)(2,1)S(1)} %get-tuple-element.60), channel_id=1, source_target_pairs={{0,384},{128,0},{256,128},{384,256},{1,385},{129,1},{257,129},{385... | collective-permute-start | bytes 196616 | tf_op jit(solution)/shard_map/ppermute | solution.py:209
  111.3 1.7 collective-permute-done.14.r2
  113.0 1.7 collective-permute-done.15.r3
  114.7 1.8 weight_grads.1
  116.5 6.2 %all-to-all-start.3 = ((bf16[16,16,1024]{2,1,0:T(8,128)(2,1)}), bf16[16,16,1024]{2,1,0:T(8,128)(2,1)}, u32[]{:S(2)}, u32[]{:S(2)}) async-start(bf16[16,16,1024]{2,1,0:T(8,128)(2,1)} %weight_grads.1), calls=%async_computation.3 | async-start | bytes 1048576 | tf_op jit(solution)/shard_map/all_to_all | solution.py:277
  122.6 8.5 %collective-permute-start.6 = (bf16[32,1024]{1,0:T(8,128)(2,1)S(1)}, bf16[32,1024]{1,0:T(8,128)(2,1)S(1)}, u32[]{:S(2)}, u32[]{:S(2)}) collective-permute-start(bf16[32,1024]{1,0:T(8,128)(2,1)S(1)} %get-tuple-element.46), channel_id=1, source_target_pairs={{0,1},{1,0},{2,3},{3,2},{4,5},{5,4},{6,7},{7,6},{8,9},{9,8},{10,11... | collective-permute-start | bytes 196616 | tf_op jit(solution)/shard_map/ppermute | solution.py:238
  131.2 2.7 %collective-permute-done.6 = bf16[32,1024]{1,0:T(8,128)(2,1)S(1)} collective-permute-done((bf16[32,1024]{1,0:T(8,128)(2,1)S(1)}, bf16[32,1024]{1,0:T(8,128)(2,1)S(1)}, u32[]{:S(2)}, u32[]{:S(2)}) %collective-permute-start.6) | collective-permute-done | bytes 65568 | tf_op jit(solution)/shard_map/ppermute | solution.py:238
  134.2 2.6 %collective-permute-start.7 = (bf16[64,1024]{1,0:T(8,128)(2,1)S(1)}, bf16[64,1024]{1,0:T(8,128)(2,1)S(1)}, u32[]{:S(2)}, u32[]{:S(2)}) collective-permute-start(bf16[64,1024]{1,0:T(8,128)(2,1)S(1)} %reshape.74.w0), channel_id=1, source_target_pairs={{0,128},{128,256},{256,384},{384,0},{1,129},{129,257},{257,385},{3... | collective-permute-start | bytes 393224 | tf_op jit(solution)/shard_map/ppermute | solution.py:209
  136.8 5.1 %collective-permute-start.8 = (bf16[64,1024]{1,0:T(8,128)(2,1)S(1)}, bf16[64,1024]{1,0:T(8,128)(2,1)S(1)}, u32[]{:S(2)}, u32[]{:S(2)}) collective-permute-start(bf16[64,1024]{1,0:T(8,128)(2,1)S(1)} %reshape.74.w0), channel_id=1, source_target_pairs={{0,256},{128,384},{256,0},{384,128},{1,257},{129,385},{257,1},{385... | collective-permute-start | bytes 393224 | tf_op jit(solution)/shard_map/ppermute | solution.py:209
  141.9 4.6 %collective-permute-start.9 = (bf16[64,1024]{1,0:T(8,128)(2,1)S(1)}, bf16[64,1024]{1,0:T(8,128)(2,1)S(1)}, u32[]{:S(2)}, u32[]{:S(2)}) collective-permute-start(bf16[64,1024]{1,0:T(8,128)(2,1)S(1)} %reshape.74.w0), channel_id=1, source_target_pairs={{0,384},{128,0},{256,128},{384,256},{1,385},{129,1},{257,129},{385... | collective-permute-start | bytes 393224 | tf_op jit(solution)/shard_map/ppermute | solution.py:209
  151.2 6.4 %collective-permute-start.10 = (bf16[64,512]{1,0:T(8,128)(2,1)S(1)}, bf16[64,512]{1,0:T(8,128)(2,1)S(1)}, u32[]{:S(2)}, u32[]{:S(2)}) collective-permute-start(bf16[64,512]{1,0:T(8,128)(2,1)S(1)} %get-tuple-element.48), channel_id=1, source_target_pairs={{0,384},{128,0},{256,128},{384,256},{1,385},{129,1},{257,129},{385... | collective-permute-start | bytes 196616 | tf_op jit(solution)/shard_map/ppermute | solution.py:209
  157.7 1.9 %collective-permute-start.11 = (bf16[64,512]{1,0:T(8,128)(2,1)S(1)}, bf16[64,512]{1,0:T(8,128)(2,1)S(1)}, u32[]{:S(2)}, u32[]{:S(2)}) collective-permute-start(bf16[64,512]{1,0:T(8,128)(2,1)S(1)} %get-tuple-element.49), channel_id=1, source_target_pairs={{0,256},{128,384},{256,0},{384,128},{1,257},{129,385},{257,1},{385... | collective-permute-start | bytes 196616 | tf_op jit(solution)/shard_map/ppermute | solution.py:209
  159.6 2.5 %collective-permute-start.12 = (bf16[64,512]{1,0:T(8,128)(2,1)S(1)}, bf16[64,512]{1,0:T(8,128)(2,1)S(1)}, u32[]{:S(2)}, u32[]{:S(2)}) collective-permute-start(bf16[64,512]{1,0:T(8,128)(2,1)S(1)} %get-tuple-element.50), channel_id=1, source_target_pairs={{0,128},{128,256},{256,384},{384,0},{1,129},{129,257},{257,385},{3... | collective-permute-start | bytes 196616 | tf_op jit(solution)/shard_map/ppermute | solution.py:209
  163.9 8.4 %all-to-all-start.4 = ((f32[8,2,1024]{2,1,0:T(2,128)}), f32[8,2,1024]{2,1,0:T(2,128)S(1)}, u32[]{:S(2)}, u32[]{:S(2)}) async-start(f32[8,2,1024]{2,1,0:T(2,128)} %reshape.81), calls=%async_computation.4 | async-start | bytes 131072 | tf_op jit(solution)/shard_map/all_to_all | solution.py:296
  172.3 11.6 %space_backward.1 = (bf16[2,1024,64]{2,1,0:T(8,128)(2,1)S(1)}, bf16[2,1024,64]{2,1,0:T(8,128)(2,1)S(1)}, bf16[2,1024,64]{2,1,0:T(8,128)(2,1)S(1)}) custom-call(s32[2]{0:T(128)S(1)} %pad_add_fusion.ids, bf16[3,2,64,1024]{3,2,1,0:T(8,128)(2,1)S(1)} %get-tuple-element.42.heads, f32[2,2,1024]{2,1,0:T(2,128)S(1)} %get-tuple-element.43.stats, ...), custom_call_target="tpu_custom_call" | custom-call | flops 8589934592 | bytes 4194304 | tf_op jit(solution)/shard_map/space_backward/pallas_call | solution.py:279
  (48 shorter events, 18.9 us)
Async XLA Ops:
  0.6 1.0 copy-start
  1.6 0.9 copy-start.1
  2.5 0.9 copy-start.2
  3.5 0.9 copy-start.3
  4.4 0.7 copy-start.7
  42.7 7.2 %copy-start.4 = (bf16[1,2,64,1024]{3,2,1,0:T(8,128)(2,1)S(1)}, bf16[1,2,64,1024]{3,2,1,0:T(8,128)(2,1)}, u32[]{:S(2)}) copy-start(bf16[1,2,64,1024]{3,2,1,0:T(8,128)(2,1)} %param.8) | copy-start | bytes 786436
  42.7 7.2 %copy-start.5 = (bf16[1,2,64,1024]{3,2,1,0:T(8,128)(2,1)S(1)}, bf16[1,2,64,1024]{3,2,1,0:T(8,128)(2,1)}, u32[]{:S(2)}) copy-start(bf16[1,2,64,1024]{3,2,1,0:T(8,128)(2,1)} %param.9) | copy-start | bytes 786436
  42.7 7.2 %copy-start.6 = (bf16[1,2,64,1024]{3,2,1,0:T(8,128)(2,1)S(1)}, bf16[1,2,64,1024]{3,2,1,0:T(8,128)(2,1)}, u32[]{:S(2)}) copy-start(bf16[1,2,64,1024]{3,2,1,0:T(8,128)(2,1)} %param.10) | copy-start | bytes 786436
  46.2 17.3 %all-to-all-start.1 = ((bf16[16,64,128]{2,1,0:T(8,128)(2,1)}), bf16[16,64,128]{2,1,0:T(8,128)(2,1)S(1)}, u32[]{:S(2)}, u32[]{:S(2)}) async-start(bf16[16,64,128]{2,1,0:T(8,128)(2,1)} %get-tuple-element.44), calls=%async_computation.1 | async-start | bytes 524288 | tf_op jit(solution)/shard_map/all_to_all | solution.py:236
  50.7 19.1 %collective-permute-start = (bf16[4,3,64,128]{3,2,1,0:T(8,128)(2,1)S(1)}, bf16[4,3,64,128]{3,2,1,0:T(8,128)(2,1)S(1)}, u32[]{:S(2)}, u32[]{:S(2)}) collective-permute-start(bf16[4,3,64,128]{3,2,1,0:T(8,128)(2,1)S(1)} %get-tuple-element.35), channel_id=1, source_target_pairs={{0,128},{128,256},{256,384},{384,0},{1,129},{129,257},{257,385},{3... | collective-permute-start | bytes 589832 | tf_op jit(solution)/shard_map/ppermute | solution.py:209
  55.0 17.5 %collective-permute-start.1 = (bf16[4,3,64,128]{3,2,1,0:T(8,128)(2,1)S(1)}, bf16[4,3,64,128]{3,2,1,0:T(8,128)(2,1)S(1)}, u32[]{:S(2)}, u32[]{:S(2)}) collective-permute-start(bf16[4,3,64,128]{3,2,1,0:T(8,128)(2,1)S(1)} %get-tuple-element.36), channel_id=1, source_target_pairs={{0,256},{128,384},{256,0},{384,128},{1,257},{129,385},{257,1},{385... | collective-permute-start | bytes 589832 | tf_op jit(solution)/shard_map/ppermute | solution.py:209
  61.1 12.5 %collective-permute-start.2 = (bf16[4,3,64,128]{3,2,1,0:T(8,128)(2,1)S(1)}, bf16[4,3,64,128]{3,2,1,0:T(8,128)(2,1)S(1)}, u32[]{:S(2)}, u32[]{:S(2)}) collective-permute-start(bf16[4,3,64,128]{3,2,1,0:T(8,128)(2,1)S(1)} %get-tuple-element.37), channel_id=1, source_target_pairs={{0,384},{128,0},{256,128},{384,256},{1,385},{129,1},{257,129},{385... | collective-permute-start | bytes 589832 | tf_op jit(solution)/shard_map/ppermute | solution.py:209
  64.9 49.7 %all-to-all-start.2 = ((bf16[4,128,1024]{2,1,0:T(8,128)(2,1)}), bf16[4,128,1024]{2,1,0:T(8,128)(2,1)S(1)}, u32[]{:S(2)}, u32[]{:S(2)}) async-start(bf16[4,128,1024]{2,1,0:T(8,128)(2,1)} %get-tuple-element.45), calls=%async_computation.2 | async-start | bytes 2097152 | tf_op jit(solution)/shard_map/all_to_all | solution.py:260
  74.2 12.9 %collective-permute-start.3 = (bf16[4,3,64,128]{3,2,1,0:T(8,128)(2,1)S(1)}, bf16[4,3,64,128]{3,2,1,0:T(8,128)(2,1)S(1)}, u32[]{:S(2)}, u32[]{:S(2)}) collective-permute-start(bf16[4,3,64,128]{3,2,1,0:T(8,128)(2,1)S(1)} %get-tuple-element.39), channel_id=1, source_target_pairs={{0,32},{32,64},{64,96},{96,0},{1,33},{33,65},{65,97},{97,1},{2,34}... | collective-permute-start | bytes 589832 | tf_op jit(solution)/shard_map/ppermute | solution.py:209
  77.6 11.3 %collective-permute-start.4 = (bf16[4,3,64,128]{3,2,1,0:T(8,128)(2,1)S(1)}, bf16[4,3,64,128]{3,2,1,0:T(8,128)(2,1)S(1)}, u32[]{:S(2)}, u32[]{:S(2)}) collective-permute-start(bf16[4,3,64,128]{3,2,1,0:T(8,128)(2,1)S(1)} %get-tuple-element.40), channel_id=1, source_target_pairs={{0,64},{32,96},{64,0},{96,32},{1,65},{33,97},{65,1},{97,33},{2,66}... | collective-permute-start | bytes 589832 | tf_op jit(solution)/shard_map/ppermute | solution.py:209
  80.6 10.8 %collective-permute-start.5 = (bf16[4,3,64,128]{3,2,1,0:T(8,128)(2,1)S(1)}, bf16[4,3,64,128]{3,2,1,0:T(8,128)(2,1)S(1)}, u32[]{:S(2)}, u32[]{:S(2)}) collective-permute-start(bf16[4,3,64,128]{3,2,1,0:T(8,128)(2,1)S(1)} %get-tuple-element.41), channel_id=1, source_target_pairs={{0,96},{32,0},{64,32},{96,64},{1,97},{33,1},{65,33},{97,65},{2,98}... | collective-permute-start | bytes 589832 | tf_op jit(solution)/shard_map/ppermute | solution.py:209
  99.2 12.1 %collective-permute-start.13 = (bf16[64,512]{1,0:T(8,128)(2,1)S(1)}, bf16[64,512]{1,0:T(8,128)(2,1)S(1)}, u32[]{:S(2)}, u32[]{:S(2)}) collective-permute-start(bf16[64,512]{1,0:T(8,128)(2,1)S(1)} %get-tuple-element.58), channel_id=1, source_target_pairs={{0,128},{128,256},{256,384},{384,0},{1,129},{129,257},{257,385},{3... | collective-permute-start | bytes 196616 | tf_op jit(solution)/shard_map/ppermute | solution.py:209
  105.0 7.9 %collective-permute-start.14 = (bf16[64,512]{1,0:T(8,128)(2,1)S(1)}, bf16[64,512]{1,0:T(8,128)(2,1)S(1)}, u32[]{:S(2)}, u32[]{:S(2)}) collective-permute-start(bf16[64,512]{1,0:T(8,128)(2,1)S(1)} %get-tuple-element.59), channel_id=1, source_target_pairs={{0,256},{128,384},{256,0},{384,128},{1,257},{129,385},{257,1},{385... | collective-permute-start | bytes 196616 | tf_op jit(solution)/shard_map/ppermute | solution.py:209
  108.5 6.2 %collective-permute-start.15 = (bf16[64,512]{1,0:T(8,128)(2,1)S(1)}, bf16[64,512]{1,0:T(8,128)(2,1)S(1)}, u32[]{:S(2)}, u32[]{:S(2)}) collective-permute-start(bf16[64,512]{1,0:T(8,128)(2,1)S(1)} %get-tuple-element.60), channel_id=1, source_target_pairs={{0,384},{128,0},{256,128},{384,256},{1,385},{129,1},{257,129},{385... | collective-permute-start | bytes 196616 | tf_op jit(solution)/shard_map/ppermute | solution.py:209
  116.5 45.6 %all-to-all-start.3 = ((bf16[16,16,1024]{2,1,0:T(8,128)(2,1)}), bf16[16,16,1024]{2,1,0:T(8,128)(2,1)}, u32[]{:S(2)}, u32[]{:S(2)}) async-start(bf16[16,16,1024]{2,1,0:T(8,128)(2,1)} %weight_grads.1), calls=%async_computation.3 | async-start | bytes 1048576 | tf_op jit(solution)/shard_map/all_to_all | solution.py:277
  122.6 11.2 %collective-permute-start.6 = (bf16[32,1024]{1,0:T(8,128)(2,1)S(1)}, bf16[32,1024]{1,0:T(8,128)(2,1)S(1)}, u32[]{:S(2)}, u32[]{:S(2)}) collective-permute-start(bf16[32,1024]{1,0:T(8,128)(2,1)S(1)} %get-tuple-element.46), channel_id=1, source_target_pairs={{0,1},{1,0},{2,3},{3,2},{4,5},{5,4},{6,7},{7,6},{8,9},{9,8},{10,11... | collective-permute-start | bytes 196616 | tf_op jit(solution)/shard_map/ppermute | solution.py:238
  134.2 13.9 %collective-permute-start.7 = (bf16[64,1024]{1,0:T(8,128)(2,1)S(1)}, bf16[64,1024]{1,0:T(8,128)(2,1)S(1)}, u32[]{:S(2)}, u32[]{:S(2)}) collective-permute-start(bf16[64,1024]{1,0:T(8,128)(2,1)S(1)} %reshape.74.w0), channel_id=1, source_target_pairs={{0,128},{128,256},{256,384},{384,0},{1,129},{129,257},{257,385},{3... | collective-permute-start | bytes 393224 | tf_op jit(solution)/shard_map/ppermute | solution.py:209
  136.8 12.3 %collective-permute-start.8 = (bf16[64,1024]{1,0:T(8,128)(2,1)S(1)}, bf16[64,1024]{1,0:T(8,128)(2,1)S(1)}, u32[]{:S(2)}, u32[]{:S(2)}) collective-permute-start(bf16[64,1024]{1,0:T(8,128)(2,1)S(1)} %reshape.74.w0), channel_id=1, source_target_pairs={{0,256},{128,384},{256,0},{384,128},{1,257},{129,385},{257,1},{385... | collective-permute-start | bytes 393224 | tf_op jit(solution)/shard_map/ppermute | solution.py:209
  141.9 7.8 %collective-permute-start.9 = (bf16[64,1024]{1,0:T(8,128)(2,1)S(1)}, bf16[64,1024]{1,0:T(8,128)(2,1)S(1)}, u32[]{:S(2)}, u32[]{:S(2)}) collective-permute-start(bf16[64,1024]{1,0:T(8,128)(2,1)S(1)} %reshape.74.w0), channel_id=1, source_target_pairs={{0,384},{128,0},{256,128},{384,256},{1,385},{129,1},{257,129},{385... | collective-permute-start | bytes 393224 | tf_op jit(solution)/shard_map/ppermute | solution.py:209
  151.2 21.0 %collective-permute-start.10 = (bf16[64,512]{1,0:T(8,128)(2,1)S(1)}, bf16[64,512]{1,0:T(8,128)(2,1)S(1)}, u32[]{:S(2)}, u32[]{:S(2)}) collective-permute-start(bf16[64,512]{1,0:T(8,128)(2,1)S(1)} %get-tuple-element.48), channel_id=1, source_target_pairs={{0,384},{128,0},{256,128},{384,256},{1,385},{129,1},{257,129},{385... | collective-permute-start | bytes 196616 | tf_op jit(solution)/shard_map/ppermute | solution.py:209
  157.7 14.6 %collective-permute-start.11 = (bf16[64,512]{1,0:T(8,128)(2,1)S(1)}, bf16[64,512]{1,0:T(8,128)(2,1)S(1)}, u32[]{:S(2)}, u32[]{:S(2)}) collective-permute-start(bf16[64,512]{1,0:T(8,128)(2,1)S(1)} %get-tuple-element.49), channel_id=1, source_target_pairs={{0,256},{128,384},{256,0},{384,128},{1,257},{129,385},{257,1},{385... | collective-permute-start | bytes 196616 | tf_op jit(solution)/shard_map/ppermute | solution.py:209
  159.6 12.7 %collective-permute-start.12 = (bf16[64,512]{1,0:T(8,128)(2,1)S(1)}, bf16[64,512]{1,0:T(8,128)(2,1)S(1)}, u32[]{:S(2)}, u32[]{:S(2)}) collective-permute-start(bf16[64,512]{1,0:T(8,128)(2,1)S(1)} %get-tuple-element.50), channel_id=1, source_target_pairs={{0,128},{128,256},{256,384},{384,0},{1,129},{129,257},{257,385},{3... | collective-permute-start | bytes 196616 | tf_op jit(solution)/shard_map/ppermute | solution.py:209
  163.9 22.7 %all-to-all-start.4 = ((f32[8,2,1024]{2,1,0:T(2,128)}), f32[8,2,1024]{2,1,0:T(2,128)S(1)}, u32[]{:S(2)}, u32[]{:S(2)}) async-start(f32[8,2,1024]{2,1,0:T(2,128)} %reshape.81), calls=%async_computation.4 | async-start | bytes 131072 | tf_op jit(solution)/shard_map/all_to_all | solution.py:296

commit v2 on v1

v2 whole, which is shorter than its diff:
```python
import jax
import jax.numpy as jnp
from jax import lax
from jax.experimental import pallas as pl
from jax.experimental.pallas import tpu as pltpu
from jax.sharding import Mesh, PartitionSpec as P

HD = 64
SCALING = HD ** (-0.5)
TM = ("y", "c")
BF = jnp.bfloat16
F32 = jnp.float32
LIMIT = 48 * 1024 * 1024
WHOLE = 60 * 1024 * 1024
VM = pl.BlockSpec(memory_space=pltpu.VMEM)
SM = pl.BlockSpec(memory_space=pltpu.SMEM)
ANY = pl.BlockSpec(memory_space=pl.ANY)
HBM = pl.BlockSpec(memory_space=pltpu.HBM)


def call(kernel, outs, ins, specs=None, scratch=(), flops=0, moved=0, name=None, after=(), limit=LIMIT):
    shapes = [jax.ShapeDtypeStruct(s, d) for s, d in outs]
    specs = specs or [VM] * len(ins)
    first, count = len(ins), len(after)

    def run(*refs):
        kernel(*refs[:first], *refs[first + count :])

    return pl.pallas_call(
        run,
        out_shape=shapes,
        in_specs=list(specs) + [ANY] * count,
        out_specs=[VM] * len(shapes),
        scratch_shapes=list(scratch),
        compiler_params=pltpu.CompilerParams(vmem_limit_bytes=limit),
        cost_estimate=pl.CostEstimate(flops=flops, bytes_accessed=moved, transcendentals=0),
        name=name,
    )(*ins, *after)


def fetch(pairs, sem):
    copies = [pltpu.make_async_copy(a, b, sem.at[i]) for i, (a, b) in enumerate(pairs)]
    for copy in copies:
        copy.start()
    return copies


def dot(a, b, dims):
    return lax.dot_general(a, b, (dims, ((), ())), preferred_element_type=F32)


def pack_time(tq, tk, st, ct, w, o, buf, sem):
    pairs = [(ref.at[f], buf.at[a, f]) for a, ref in enumerate((tq, tk, st, ct)) for f in range(2)]
    for copy in fetch(pairs, sem):
        copy.wait()
    for j in range(8):
        lanes = slice(128 * j, 128 * j + 128)
        wide = [[buf[a, f, :, lanes].astype(F32) for f in range(2)] for a in range(4)]
        for g in range(16):
            rows = slice(4 * g, 4 * g + 4)
            block = jnp.concatenate([wide[a][f][rows] for a in range(4) for f in range(2)], 0)
            o[g, 32 * j : 32 * j + 32, :] = block.astype(BF)
    own = w[...].astype(F32)
    own = jnp.concatenate([own[:, 128 * j : 128 * j + 128] for j in range(8)], 0).astype(BF)
    for g in range(16):
        o[g, 256:272, :] = own


def time_grads(r, gq, gk, gs, wo):
    row = lax.broadcasted_iota(jnp.int32, (128, 128), 0)
    col = lax.broadcasted_iota(jnp.int32, (128, 128), 1)
    allowed = ((row & 3) == (col & 3)) & (row <= col)
    first = col < 64
    zero = jnp.zeros((128, 128), BF)
    kept = []
    for j in range(8):
        block = r[:, 32 * j : 32 * j + 32, :].astype(F32)
        q, k, v, g = (block[:, 8 * a : 8 * a + 8, :].reshape(128, 128).astype(BF) for a in range(4))
        sum_q = sum_k = sum_v = None
        for h in range(2):
            own = first if h == 0 else jnp.logical_not(first)
            qh, kh, gh = (jnp.where(own, t, zero) for t in (q, k, g))
            score = dot(k, qh, ((1,), (1,))) * SCALING
            score = jnp.where(allowed, score, -jnp.inf)
            e = jnp.exp(score - jnp.max(score, axis=0, keepdims=True))
            weight = e / jnp.sum(e, axis=0, keepdims=True)
            prob = dot(v, gh, ((1,), (1,)))
            delta = jnp.sum(weight * prob, axis=0, keepdims=True)
            ds = (weight * (prob - delta) * SCALING).astype(BF)
            part_k = dot(ds, qh, ((1,), (0,)))
            part_v = dot(weight.astype(BF), gh, ((1,), (0,)))
            part_q = dot(ds, kh, ((0,), (0,)))
            sum_q = part_q if h == 0 else sum_q + part_q
            sum_k = part_k if h == 0 else sum_k + part_k
            sum_v = part_v if h == 0 else sum_v + part_v
        lanes = slice(128 * j, 128 * j + 128)
        gq[:, :, lanes] = sum_q.reshape(32, 4, 128).astype(BF)
        gk[:, :, lanes] = sum_k.reshape(32, 4, 128).astype(BF)
        kept.append((g.astype(F32) + sum_v).reshape(16, 8, 128))
        if j % 2 == 1:
            gs[:, 8 * j - 8 : 8 * j + 8, :] = jnp.concatenate(kept, 1).astype(BF)
            kept = []
    rows = r[:, 256:272, :].astype(F32)
    for j in range(8):
        wo[:, 128 * j : 128 * j + 128] = jnp.concatenate(
            [rows[g, 2 * j : 2 * j + 2, :] for g in range(16)], 0
        ).astype(BF)


def unpack_stream(ids, r, own, other, s0, s1, s2, s3, gs, wide, *outs):
    for s, o in zip((s0, s1, s2, s3), outs):
        o[:, 0:512] = s[...]
    swapped = jnp.full((32, 128), ids[2], jnp.int32) == 1
    for j in range(8):
        lanes = slice(128 * j, 128 * j + 128)
        mine, theirs = own[:, lanes].astype(F32), other[:, lanes].astype(F32)
        low = jnp.where(swapped, theirs, mine)
        high = jnp.where(swapped, mine, theirs)
        pieces = [t[2 * y : 2 * y + 2] for y in range(16) for t in (low, high)]
        rows = jnp.concatenate(pieces, 0).astype(BF)
        for o in outs:
            o[:, 512 + 128 * j : 640 + 128 * j] = rows
    for j in range(8):
        lanes = slice(128 * j, 128 * j + 128)
        block = r[:, 8 * j : 8 * j + 8, :].astype(F32)
        for f in range(2):
            part = jnp.concatenate([block[g, 4 * f : 4 * f + 4, :] for g in range(16)], 0).astype(BF)
            gs[f, :, lanes] = part
            for m in range(4):
                wide[m, 64 * f : 64 * f + 64, lanes] = part


def pack_space(ids, q, k, v, o0, o1, o2, o3, buf, turned, sem):
    x = ids[1]
    copies = fetch([(ref, buf.at[a]) for a, ref in enumerate((q, k, v))], sem)
    for a in range(3):
        copies[a].wait()
        turned[...] = buf[a].T.reshape(16, 64, 128)
        for m, o in enumerate((o0, o1, o2, o3)):
            for z in range(4):
                o[z, a, :, :] = turned[z * 4 + lax.rem(x + m, 4)]


def turn_space(ids, *refs):
    ins, outs = refs[:4], refs[4:]
    z = ids[0]
    for n in range(4):
        at = lax.rem(z + n, 4)
        for m in range(4):
            outs[n][m] = ins[m][at]


def space_forward(ids, s0, s1, s2, s3, heads, stats, o0, o1, o2, o3, buf, ot):
    z, x = ids[0], ids[1]
    for n, s in enumerate((s0, s1, s2, s3)):
        for m in range(4):
            buf[lax.rem(z + 4 - n, 4) * 4 + lax.rem(x + 4 - m, 4)] = s[m]
    for a in range(3):
        for f in range(2):
            heads[a, f] = jnp.concatenate(
                [buf[i, a, :, 64 * f : 64 * f + 64] for i in range(16)], 1
            )
    for f in range(2):
        score = dot(heads[1, f].T, heads[0, f] * jnp.asarray(SCALING, BF), ((1,), (0,)))
        largest = jnp.max(score, axis=0, keepdims=True)
        e = jnp.exp(score - largest)
        inverse = 1.0 / jnp.sum(e, axis=0, keepdims=True)
        stats[f, 0:1, :] = largest
        stats[f, 1:2, :] = inverse
        result = dot(heads[2, f], (e * inverse).astype(BF), ((1,), (0,))).astype(BF)
        for n in range(4):
            ot[n, f] = result[:, 256 * n : 256 * n + 256]
    for n, o in enumerate((o0, o1, o2, o3)):
        at = lax.rem(z + n, 4)
        for f in range(2):
            o[:, 256 * f : 256 * f + 256] = ot[at, f]


def mix_grads(g, r0, r1, r2, r3, m0, m1, m2, m3):
    for r, m in ((r0, m0), (r1, m1), (r2, m2), (r3, m3)):
        w = r[:, 512:1536]
        for x in range(4):
            m[:, 128 * x : 128 * x + 128] = dot(w, g[x], ((1,), (1,))).astype(BF)


def weight_grads(ids, g, r0, r1, r2, r3, o, buf):
    z = ids[0]
    for n, r in enumerate((r0, r1, r2, r3)):
        buf[lax.rem(z + 4 - n, 4)] = r[:, 0:512]
    left = buf[...].reshape(256, 512)
    for d in range(4):
        lanes = slice(256 * d, 256 * d + 256)
        right = jnp.concatenate(
            [g[x, 64 * f : 64 * f + 64, lanes] for f in range(2) for x in range(4)], 0
        )
        total = dot(left, right, ((1,), (0,))).reshape(4, 16, 4, 256)
        for y in range(16):
            o[y, :, lanes] = jnp.concatenate([total[n, y] for n in range(4)], 0).astype(BF)


def space_backward(ids, heads, stats, m0, m1, m2, m3, gq, gk, gv, buf, got, ds_all, w_all):
    z = ids[0]
    for n, m in enumerate((m0, m1, m2, m3)):
        buf[lax.rem(z + n, 4)] = m[...]
    scale = jnp.asarray(SCALING, BF)
    for f in range(2):
        got[...] = jnp.concatenate(
            [buf[n, :, 128 * x + 64 * f : 128 * x + 64 * f + 64] for n in range(4) for x in range(4)], 1
        )
        q, k = heads[0, f] * scale, heads[1, f]
        weight = jnp.exp(dot(k.T, q, ((1,), (0,))) - stats[f, 0:1, :]) * stats[f, 1:2, :]
        prob = dot(heads[2, f].T, got[...], ((1,), (0,)))
        delta = jnp.sum(weight * prob, axis=0, keepdims=True)
        ds_all[...] = (weight * (prob - delta)).astype(BF)
        w_all[...] = weight.astype(BF)
        gq[f] = dot(k * scale, ds_all[...], ((1,), (0,))).astype(BF)
        gk[f] = dot(ds_all[...], q.T, ((1,), (0,))).T.astype(BF)
        gv[f] = dot(w_all[...], got[...].T, ((1,), (0,))).T.astype(BF)


def add_up(r, o):
    total = r[0].astype(F32)
    for i in range(1, 16):
        total = total + r[i].astype(F32)
    for i in range(8):
        o[i] = total[2 * i : 2 * i + 2]


def shift(value, axis, by):
    return lax.ppermute(value, axis, [(i, (i + by) % 4) for i in range(4)])


def body(space_query, space_key, space_value, time_query, time_key, stream, cotangent, mix_weight):
    ids = jnp.stack([lax.axis_index(a) for a in ("z", "x", "f")]).astype(jnp.int32)

    packed = call(
        pack_time,
        [((16, 272, 128), BF)],
        [t.reshape(2, 64, 1024) for t in (time_query, time_key, stream, cotangent)] + [mix_weight],
        specs=[HBM] * 4 + [VM],
        scratch=[pltpu.VMEM((4, 2, 64, 1024), BF), pltpu.SemaphoreType.DMA((8,))],
        moved=2 << 20,
        name="pack_time",
        limit=WHOLE,
    )[0]
    frames = lax.all_to_all(packed, TM, 0, 0, tiled=True)

    part = ((4, 3, 64, 128), BF)
    sent = call(
        pack_space,
        [part] * 4,
        [ids] + [t.reshape(128, 1024) for t in (space_query, space_key, space_value)],
        specs=[SM] + [HBM] * 3,
        scratch=[
            pltpu.VMEM((3, 128, 1024), BF),
            pltpu.VMEM((16, 64, 128), BF),
            pltpu.SemaphoreType.DMA((3,)),
        ],
        moved=1536 << 10,
        name="pack_space",
        after=[packed],
    )
    along_x = [sent[0]] + [shift(sent[m], "x", m) for m in (1, 2, 3)]
    turned = call(
        turn_space, [part] * 4, [ids] + along_x, specs=[SM] + [VM] * 4, moved=1536 << 10, name="turn_space"
    )
    along_z = [turned[0]] + [shift(turned[n], "z", n) for n in (1, 2, 3)]

    grad_time_query, grad_time_key, grad_frames, own_rows = call(
        time_grads,
        [((32, 4, 1024), BF), ((32, 4, 1024), BF), ((16, 64, 128), BF), ((32, 1024), BF)],
        [frames],
        flops=1 << 30,
        moved=2 << 20,
        name="time_grads",
        after=[turned[0]],
    )
    back = lax.all_to_all(grad_frames, TM, 0, 0, tiled=True)
    other_rows = lax.ppermute(own_rows, "f", [(0, 1), (1, 0)])

    heads, stats, *outputs = call(
        space_forward,
        [((3, 2, 64, 1024), BF), ((2, 2, 1024), F32)] + [((64, 512), BF)] * 4,
        [ids] + along_z,
        specs=[SM] + [VM] * 4,
        scratch=[pltpu.VMEM((16, 3, 64, 128), BF), pltpu.VMEM((4, 2, 64, 256), BF)],
        flops=4 << 30,
        moved=2 << 20,
        name="space_forward",
    )

    grad_stream, wide, *outputs = call(
        unpack_stream,
        [((2, 64, 1024), BF), ((4, 128, 1024), BF)] + [((64, 1536), BF)] * 4,
        [ids, back, own_rows, other_rows] + outputs,
        specs=[SM] + [VM] * 7,
        moved=1536 << 10,
        name="unpack_stream",
    )
    gathered = lax.all_to_all(wide, "x", 0, 0, tiled=True)
    outputs = [outputs[0]] + [shift(outputs[n], "z", n) for n in (1, 2, 3)]

    partial = call(
        weight_grads,
        [((16, 16, 1024), BF)],
        [ids, gathered] + outputs,
        specs=[SM] + [VM] * 5,
        scratch=[pltpu.VMEM((4, 64, 512), BF)],
        flops=1 << 28,
        moved=2 << 20,
        name="weight_grads",
    )[0]
    spread = lax.all_to_all(partial, TM, 0, 0, tiled=True)
    mixed = call(
        mix_grads,
        [((64, 512), BF)] * 4,
        [gathered] + outputs,
        flops=1 << 28,
        moved=2 << 20,
        name="mix_grads",
        after=[partial],
    )
    mixed = [mixed[0]] + [shift(mixed[n], "z", -n) for n in (1, 2, 3)]

    summed = call(add_up, [((8, 2, 1024), F32)], [spread], moved=1 << 19, name="add_up", after=mixed[1:])[0]
    last = lax.all_to_all(summed, ("z", "f"), 0, 0, tiled=True)
    grads = call(
        space_backward,
        [((2, 64, 1024), BF)] * 3,
        [ids, heads, stats] + mixed,
        specs=[SM] + [VM] * 6,
        scratch=[
            pltpu.VMEM((4, 64, 512), BF),
            pltpu.VMEM((64, 1024), BF),
            pltpu.VMEM((1024, 1024), BF),
            pltpu.VMEM((1024, 1024), BF),
        ],
        flops=8 << 30,
        moved=4 << 20,
        name="space_backward",
        after=[summed],
    )
    grad_mix_weight = jnp.sum(last, axis=0)

    time_shape = (1, 32, 4, 1024)
    return (
        *(g.transpose(0, 2, 1).reshape(1, 2, 1024, 64) for g in grads),
        grad_time_query.reshape(time_shape),
        grad_time_key.reshape(time_shape),
        grad_stream.reshape(1, 2, 64, 1024),
        grad_mix_weight,
    )


def solution(mesh):
    fine = Mesh(mesh.devices.reshape(4, 4, 8, 2, 2), ("z", "x", "y", "c", "f"))
    tokens = P("f", TM, ("z", "x"), None)
    feature = P("f", TM, None, ("z", "x"))
    time = P("f", None, ("z", "x", "y", "c"), None)
    rows = P(("z", "x", "y", "c", "f"), None)
    return jax.shard_map(
        body,
        mesh=fine,
        in_specs=(tokens,) * 7 + (rows,),
        out_specs=(feature,) * 3 + (time,) * 2 + (tokens, rows),
        check_vma=False,
    )
```

time: 188 us -> 138 us (0.73)
  the two profiles are of different devices: /device:TPU:2 before, /device:TPU:1 now
where the time goes in v2:
time: 138 us
  starting transfers between devices  84.4 us (61%)
  Pallas kernels  26.6 us (19%)
  waiting for transfers between devices  22.9 us (17%)
  local copies, waits for them, and re-layouts  2.04 us (1%)
    ppermute x12, starting transfers between devices, shift(): return lax.ppermute(value, axis, [(i, (i + by) % 4) for i in range(4)])  39.2 us
    pallas_call x10, Pallas kernels, call(): pl.pallas_call(run, out_shape=shapes, in_specs=list(specs) + [ANY] * coun...  26.6 us
    ppermute x12, waiting for transfers between devices, shift(): return lax.ppermute(value, axis, [(i, (i + by) % 4) for i in range(4)])  21.8 us
    all_to_all x1, starting transfers between devices, body(): frames = lax.all_to_all(packed, TM, 0, 0, tiled=True)  10.5 us
    ppermute x1, starting transfers between devices, body(): other_rows = lax.ppermute(own_rows, 'f', [(0, 1), (1, 0)])  8.85 us
    all_to_all x1, starting transfers between devices, body(): spread = lax.all_to_all(partial, TM, 0, 0, tiled=True)  7.9 us
    all_to_all x1, starting transfers between devices, body(): back = lax.all_to_all(grad_frames, TM, 0, 0, tiled=True)  7.67 us
    all_to_all x1, starting transfers between devices, body(): last = lax.all_to_all(summed, ('z', 'f'), 0, 0, tiled=True)  6.23 us
  transfers between devices with their start and end apart: 18, of which 8 were waited for; matrix products, arithmetic and copies ran while one was open for 0% of the time, Pallas kernels for 14%

profile of v2, /device:TPU:1, one launch (start us, length us, event | category | flops | bytes accessed | tf_op | source)
XLA Modules:
  0.0 137.5 jit_solution(17260024739561654393)
XLA Ops:
  0.6 3.3 %pack_time.1.refs_4_ = bf16[16,272,128]{2,1,0:T(8,128)(2,1)} custom-call(bf16[2,64,1024]{2,1,0:T(8,128)(2,1)} %bitcast.25, bf16[2,64,1024]{2,1,0:T(8,128)(2,1)} %bitcast.26, bf16[2,64,1024]{2,1,0:T(8,128)(2,1)} %bitcast.27, bf16[2,64,1024]{2,1,0:T(8,128)(2,1)} %bitcast.28, bf16[2,1024]{1,0:T(2,128)(2,1)} %refs_4_.1), custom_call_target="tpu_custom_call" | custom-call | bytes 2097152 | tf_op jit(solution)/shard_map/pack_time/pallas_call | solution.py:29
  4.0 10.5 %all-to-all-start = ((bf16[16,272,128]{2,1,0:T(8,128)(2,1)}), bf16[16,272,128]{2,1,0:T(8,128)(2,1)S(1)}, u32[]{:S(2)}, u32[]{:S(2)}) async-start(bf16[16,272,128]{2,1,0:T(8,128)(2,1)} %pack_time.1.refs_4_), calls=%async_computation | async-start | bytes 2228224 | tf_op jit(solution)/shard_map/all_to_all | solution.py:246
  14.6 1.1 pack_space.1
  15.7 1.9 %collective-permute-start = (bf16[4,3,64,128]{3,2,1,0:T(8,128)(2,1)S(1)}, bf16[4,3,64,128]{3,2,1,0:T(8,128)(2,1)S(1)}, u32[]{:S(2)}, u32[]{:S(2)}) collective-permute-start(bf16[4,3,64,128]{3,2,1,0:T(8,128)(2,1)S(1)} %get-tuple-element.39), channel_id=1, source_target_pairs={{0,32},{32,64},{64,96},{96,0},{1,33},{33,65},{65,97},{97,1},{2,34}... | collective-permute-start | bytes 589832 | tf_op jit(solution)/shard_map/ppermute | solution.py:230
  17.6 3.8 %collective-permute-start.1 = (bf16[4,3,64,128]{3,2,1,0:T(8,128)(2,1)S(1)}, bf16[4,3,64,128]{3,2,1,0:T(8,128)(2,1)S(1)}, u32[]{:S(2)}, u32[]{:S(2)}) collective-permute-start(bf16[4,3,64,128]{3,2,1,0:T(8,128)(2,1)S(1)} %get-tuple-element.40), channel_id=1, source_target_pairs={{0,64},{32,96},{64,0},{96,32},{1,65},{33,97},{65,1},{97,33},{2,66}... | collective-permute-start | bytes 589832 | tf_op jit(solution)/shard_map/ppermute | solution.py:230
  21.5 3.1 %collective-permute-start.2 = (bf16[4,3,64,128]{3,2,1,0:T(8,128)(2,1)S(1)}, bf16[4,3,64,128]{3,2,1,0:T(8,128)(2,1)S(1)}, u32[]{:S(2)}, u32[]{:S(2)}) collective-permute-start(bf16[4,3,64,128]{3,2,1,0:T(8,128)(2,1)S(1)} %get-tuple-element.41), channel_id=1, source_target_pairs={{0,96},{32,0},{64,32},{96,64},{1,97},{33,1},{65,33},{97,65},{2,98}... | collective-permute-start | bytes 589832 | tf_op jit(solution)/shard_map/ppermute | solution.py:230
  25.6 3.2 %collective-permute-done.1.refs_3_ = bf16[4,3,64,128]{3,2,1,0:T(8,128)(2,1)S(1)} collective-permute-done((bf16[4,3,64,128]{3,2,1,0:T(8,128)(2,1)S(1)}, bf16[4,3,64,128]{3,2,1,0:T(8,128)(2,1)S(1)}, u32[]{:S(2)}, u32[]{:S(2)}) %collective-permute-start.1) | collective-permute-done | bytes 196640 | tf_op jit(solution)/shard_map/ppermute | solution.py:230
  28.8 2.7 %collective-permute-done.2.refs_4_ = bf16[4,3,64,128]{3,2,1,0:T(8,128)(2,1)S(1)} collective-permute-done((bf16[4,3,64,128]{3,2,1,0:T(8,128)(2,1)S(1)}, bf16[4,3,64,128]{3,2,1,0:T(8,128)(2,1)S(1)}, u32[]{:S(2)}, u32[]{:S(2)}) %collective-permute-start.2) | collective-permute-done | bytes 196640 | tf_op jit(solution)/shard_map/ppermute | solution.py:230
  32.1 2.6 %collective-permute-start.3 = (bf16[4,3,64,128]{3,2,1,0:T(8,128)(2,1)S(1)}, bf16[4,3,64,128]{3,2,1,0:T(8,128)(2,1)S(1)}, u32[]{:S(2)}, u32[]{:S(2)}) collective-permute-start(bf16[4,3,64,128]{3,2,1,0:T(8,128)(2,1)S(1)} %get-tuple-element.43), channel_id=1, source_target_pairs={{0,128},{128,256},{256,384},{384,0},{1,129},{129,257},{257,385},{3... | collective-permute-start | bytes 589832 | tf_op jit(solution)/shard_map/ppermute | solution.py:230
  34.7 5.8 %collective-permute-start.4 = (bf16[4,3,64,128]{3,2,1,0:T(8,128)(2,1)S(1)}, bf16[4,3,64,128]{3,2,1,0:T(8,128)(2,1)S(1)}, u32[]{:S(2)}, u32[]{:S(2)}) collective-permute-start(bf16[4,3,64,128]{3,2,1,0:T(8,128)(2,1)S(1)} %get-tuple-element.44), channel_id=1, source_target_pairs={{0,256},{128,384},{256,0},{384,128},{1,257},{129,385},{257,1},{385... | collective-permute-start | bytes 589832 | tf_op jit(solution)/shard_map/ppermute | solution.py:230
  40.5 2.2 %collective-permute-start.5 = (bf16[4,3,64,128]{3,2,1,0:T(8,128)(2,1)S(1)}, bf16[4,3,64,128]{3,2,1,0:T(8,128)(2,1)S(1)}, u32[]{:S(2)}, u32[]{:S(2)}) collective-permute-start(bf16[4,3,64,128]{3,2,1,0:T(8,128)(2,1)S(1)} %get-tuple-element.45), channel_id=1, source_target_pairs={{0,384},{128,0},{256,128},{384,256},{1,385},{129,1},{257,129},{385... | collective-permute-start | bytes 589832 | tf_op jit(solution)/shard_map/ppermute | solution.py:230
  43.8 3.7 %time_grads.1 = (bf16[32,4,1024]{2,1,0:T(4,128)(2,1)}, bf16[32,4,1024]{2,1,0:T(4,128)(2,1)}, bf16[16,64,128]{2,1,0:T(8,128)(2,1)}, bf16[32,1024]{1,0:T(8,128)(2,1)S(1)}) custom-call(bf16[16,272,128]{2,1,0:T(8,128)(2,1)S(1)} %all-to-all-done.refs_0_, bf16[4,3,64,128]{3,2,1,0:T(8,128)(2,1)S(1)} %get-tuple-element.42.refs_1_), custom_call_target="tpu_custom_call" | custom-call | flops 1073741824 | bytes 2097152 | tf_op jit(solution)/shard_map/time_grads/pallas_call | solution.py:29
  47.5 7.7 %all-to-all-start.1 = ((bf16[16,64,128]{2,1,0:T(8,128)(2,1)}), bf16[16,64,128]{2,1,0:T(8,128)(2,1)S(1)}, u32[]{:S(2)}, u32[]{:S(2)}) async-start(bf16[16,64,128]{2,1,0:T(8,128)(2,1)} %get-tuple-element.48), calls=%async_computation.1 | async-start | bytes 524288 | tf_op jit(solution)/shard_map/all_to_all | solution.py:278
  55.1 8.8 %collective-permute-start.6 = (bf16[32,1024]{1,0:T(8,128)(2,1)S(1)}, bf16[32,1024]{1,0:T(8,128)(2,1)S(1)}, u32[]{:S(2)}, u32[]{:S(2)}) collective-permute-start(bf16[32,1024]{1,0:T(8,128)(2,1)S(1)} %get-tuple-element.49.refs_2_), channel_id=1, source_target_pairs={{0,1},{1,0},{2,3},{3,2},{4,5},{5,4},{6,7},{7,6},{8,9},{9,8},{10,11... | collective-permute-start | bytes 196616 | tf_op jit(solution)/shard_map/ppermute | solution.py:279
  64.0 4.0 %space_forward.1 = (bf16[3,2,64,1024]{3,2,1,0:T(8,128)(2,1)S(1)}, f32[2,2,1024]{2,1,0:T(2,128)S(1)}, bf16[64,512]{1,0:T(8,128)(2,1)S(1)}, bf16[64,512]{1,0:T(8,1...) custom-call(s32[3]{0:T(128)S(1)} %pad_add_fusion.refs_0_, ...), custom_call_target="tpu_custom_call" | custom-call | flops 4294967296 | bytes 2097152 | tf_op jit(solution)/shard_map/space_forward/pallas_call | solution.py:29
  68.9 1.9 %unpack_stream.1 = (bf16[2,64,1024]{2,1,0:T(8,128)(2,1)}, bf16[4,128,1024]{2,1,0:T(8,128)(2,1)}, bf16[64,1536]{1,0:T(8,128)(2,1)S(1)}, bf16[64,1536]{1,0:T(8,128...) custom-call(s32[3]{0:T(128)S(1)} %pad_add_fusion.refs_0_, ...), custom_call_target="tpu_custom_call" | custom-call | bytes 1572864 | tf_op jit(solution)/shard_map/unpack_stream/pallas_call | solution.py:29
  70.9 4.1 %all-to-all-start.2 = ((bf16[4,128,1024]{2,1,0:T(8,128)(2,1)}), bf16[4,128,1024]{2,1,0:T(8,128)(2,1)S(1)}, u32[]{:S(2)}, u32[]{:S(2)}) async-start(bf16[4,128,1024]{2,1,0:T(8,128)(2,1)} %get-tuple-element.54), calls=%async_computation.2 | async-start | bytes 2097152 | tf_op jit(solution)/shard_map/all_to_all | solution.py:300
  74.9 2.2 %collective-permute-start.7 = (bf16[64,1536]{1,0:T(8,128)(2,1)S(1)}, bf16[64,1536]{1,0:T(8,128)(2,1)S(1)}, u32[]{:S(2)}, u32[]{:S(2)}) collective-permute-start(bf16[64,1536]{1,0:T(8,128)(2,1)S(1)} %get-tuple-element.56), channel_id=1, source_target_pairs={{0,128},{128,256},{256,384},{384,0},{1,129},{129,257},{257,385},{3... | collective-permute-start | bytes 589832 | tf_op jit(solution)/shard_map/ppermute | solution.py:230
  77.1 2.2 %collective-permute-start.8 = (bf16[64,1536]{1,0:T(8,128)(2,1)S(1)}, bf16[64,1536]{1,0:T(8,128)(2,1)S(1)}, u32[]{:S(2)}, u32[]{:S(2)}) collective-permute-start(bf16[64,1536]{1,0:T(8,128)(2,1)S(1)} %get-tuple-element.57), channel_id=1, source_target_pairs={{0,256},{128,384},{256,0},{384,128},{1,257},{129,385},{257,1},{385... | collective-permute-start | bytes 589832 | tf_op jit(solution)/shard_map/ppermute | solution.py:230
  79.3 4.6 %collective-permute-start.9 = (bf16[64,1536]{1,0:T(8,128)(2,1)S(1)}, bf16[64,1536]{1,0:T(8,128)(2,1)S(1)}, u32[]{:S(2)}, u32[]{:S(2)}) collective-permute-start(bf16[64,1536]{1,0:T(8,128)(2,1)S(1)} %get-tuple-element.58), channel_id=1, source_target_pairs={{0,384},{128,0},{256,128},{384,256},{1,385},{129,1},{257,129},{385... | collective-permute-start | bytes 589832 | tf_op jit(solution)/shard_map/ppermute | solution.py:230
  84.4 9.5 %collective-permute-done.8.refs_4_.refs_3_ = bf16[64,1536]{1,0:T(8,128)(2,1)S(1)} collective-permute-done((bf16[64,1536]{1,0:T(8,128)(2,1)S(1)}, bf16[64,1536]{1,0:T(8,128)(2,1)S(1)}, u32[]{:S(2)}, u32[]{:S(2)}) %collective-permute-start.8) | collective-permute-done | bytes 196640 | tf_op jit(solution)/shard_map/ppermute | solution.py:230
  93.9 1.8 %weight_grads.1.refs_5_ = bf16[16,16,1024]{2,1,0:T(8,128)(2,1)} custom-call(s32[3]{0:T(128)S(1)} %pad_add_fusion.refs_0_, bf16[4,128,1024]{2,1,0:T(8,128)(2,1)S(1)} %all-to-all-done.2.refs_1_.refs_0_, bf16[64,1536]{1,0:T(8,128)(2,1)S(1)} %get-tuple-element.55.refs_2_.refs_1_, bf16[64,1536]{1,0:T(8,128)(2,1)S(1)} %collective-permute-done.7.refs_3_.refs_2_, ...), custom_call_target="tpu_custom_call" | custom-call | flops 268435456 | bytes 2097152 | tf_op jit(solution)/shard_map/weight_grads/pallas_call | solution.py:29
  95.7 7.9 %all-to-all-start.3 = ((bf16[16,16,1024]{2,1,0:T(8,128)(2,1)}), bf16[16,16,1024]{2,1,0:T(8,128)(2,1)S(1)}, u32[]{:S(2)}, u32[]{:S(2)}) async-start(bf16[16,16,1024]{2,1,0:T(8,128)(2,1)} %weight_grads.1.refs_5_), calls=%async_computation.3 | async-start | bytes 1048576 | tf_op jit(solution)/shard_map/all_to_all | solution.py:313
  103.6 1.5 %mix_grads.1 = (bf16[64,512]{1,0:T(8,128)(2,1)S(1)}, bf16[64,512]{1,0:T(8,128)(2,1)S(1)}, bf16[64,512]{1,0:T(8,128)(2,1)S(1)}, bf16[64,512]{1,0:T(8,128)(2,1)S(1)}) custom-call(bf16[4,128,1024]{2,1,0:T(8,128)(2,1)S(1)} %all-to-all-done.2.refs_1_.refs_0_, bf16[64,1536]{1,0:T(8,128)(2,1)S(1)} %get-tuple-element.55.refs_2_.refs_1_, ...), custom_call_target="tpu_custom_call" | custom-call | flops 268435456 | bytes 2097152 | tf_op jit(solution)/shard_map/mix_grads/pallas_call | solution.py:29
  105.1 5.0 %collective-permute-start.10 = (bf16[64,512]{1,0:T(8,128)(2,1)S(1)}, bf16[64,512]{1,0:T(8,128)(2,1)S(1)}, u32[]{:S(2)}, u32[]{:S(2)}) collective-permute-start(bf16[64,512]{1,0:T(8,128)(2,1)S(1)} %get-tuple-element.60), channel_id=1, source_target_pairs={{0,384},{128,0},{256,128},{384,256},{1,385},{129,1},{257,129},{385... | collective-permute-start | bytes 196616 | tf_op jit(solution)/shard_map/ppermute | solution.py:230
  110.1 4.0 %collective-permute-start.11 = (bf16[64,512]{1,0:T(8,128)(2,1)S(1)}, bf16[64,512]{1,0:T(8,128)(2,1)S(1)}, u32[]{:S(2)}, u32[]{:S(2)}) collective-permute-start(bf16[64,512]{1,0:T(8,128)(2,1)S(1)} %get-tuple-element.61), channel_id=1, source_target_pairs={{0,256},{128,384},{256,0},{384,128},{1,257},{129,385},{257,1},{385... | collective-permute-start | bytes 196616 | tf_op jit(solution)/shard_map/ppermute | solution.py:230
  114.1 1.9 %collective-permute-start.12 = (bf16[64,512]{1,0:T(8,128)(2,1)S(1)}, bf16[64,512]{1,0:T(8,128)(2,1)S(1)}, u32[]{:S(2)}, u32[]{:S(2)}) collective-permute-start(bf16[64,512]{1,0:T(8,128)(2,1)S(1)} %get-tuple-element.62), channel_id=1, source_target_pairs={{0,128},{128,256},{256,384},{384,0},{1,129},{129,257},{257,385},{3... | collective-permute-start | bytes 196616 | tf_op jit(solution)/shard_map/ppermute | solution.py:230
  116.0 1.7 %collective-permute-done.11.refs_2_.refs_5_ = bf16[64,512]{1,0:T(8,128)(2,1)S(1)} collective-permute-done((bf16[64,512]{1,0:T(8,128)(2,1)S(1)}, bf16[64,512]{1,0:T(8,128)(2,1)S(1)}, u32[]{:S(2)}, u32[]{:S(2)}) %collective-permute-start.11) | collective-permute-done | bytes 65568 | tf_op jit(solution)/shard_map/ppermute | solution.py:230
  117.8 3.1 %collective-permute-done.12.refs_3_.refs_6_ = bf16[64,512]{1,0:T(8,128)(2,1)S(1)} collective-permute-done((bf16[64,512]{1,0:T(8,128)(2,1)S(1)}, bf16[64,512]{1,0:T(8,128)(2,1)S(1)}, u32[]{:S(2)}, u32[]{:S(2)}) %collective-permute-start.12) | collective-permute-done | bytes 65568 | tf_op jit(solution)/shard_map/ppermute | solution.py:230
  121.6 6.2 %all-to-all-start.4 = ((f32[8,2,1024]{2,1,0:T(2,128)}), f32[8,2,1024]{2,1,0:T(2,128)S(1)}, u32[]{:S(2)}, u32[]{:S(2)}) async-start(f32[8,2,1024]{2,1,0:T(2,128)} %add_up.1.refs_7_), calls=%async_computation.4 | async-start | bytes 131072 | tf_op jit(solution)/shard_map/all_to_all | solution.py:326
  127.9 1.1 copy-done.5
  129.0 7.9 %space_backward.1 = (bf16[2,64,1024]{2,1,0:T(8,128)(2,1)}, bf16[2,64,1024]{2,1,0:T(8,128)(2,1)}, bf16[2,64,1024]{2,1,0:T(8,128)(2,1)}) custom-call(s32[3]{0:T(128)S(1)} %pad_add_fusion.refs_0_, bf16[3,2,64,1024]{3,2,1,0:T(8,128)(2,1)S(1)} %copy-done.5, f32[2,2,1024]{2,1,0:T(2,128)S(1)} %get-tuple-element.47.refs_2_, ...), custom_call_target="tpu_custom_call" | custom-call | flops 8589934592 | bytes 4194304 | tf_op jit(solution)/shard_map/space_backward/pallas_call | solution.py:29
  (28 shorter events, 5.6 us)
Async XLA Ops:
  3.9 10.6 %copy-start = (bf16[16,272,128]{2,1,0:T(8,128)(2,1)S(1)}, bf16[16,272,128]{2,1,0:T(8,128)(2,1)}, u32[]{:S(2)}) copy-start(bf16[16,272,128]{2,1,0:T(8,128)(2,1)} %pack_time.1.refs_4_) | copy-start | bytes 3342340
  3.9 10.6 %copy-start.1 = (bf16[1,2,64,1024]{3,2,1,0:T(8,128)(2,1)S(1)}, bf16[1,2,64,1024]{3,2,1,0:T(8,128)(2,1)}, u32[]{:S(2)}) copy-start(bf16[1,2,64,1024]{3,2,1,0:T(8,128)(2,1)} %param.8) | copy-start | bytes 786436
  3.9 10.6 %copy-start.2 = (bf16[1,2,64,1024]{3,2,1,0:T(8,128)(2,1)S(1)}, bf16[1,2,64,1024]{3,2,1,0:T(8,128)(2,1)}, u32[]{:S(2)}) copy-start(bf16[1,2,64,1024]{3,2,1,0:T(8,128)(2,1)} %param.9) | copy-start | bytes 786436
  4.0 10.6 %copy-start.3 = (bf16[1,2,64,1024]{3,2,1,0:T(8,128)(2,1)S(1)}, bf16[1,2,64,1024]{3,2,1,0:T(8,128)(2,1)}, u32[]{:S(2)}) copy-start(bf16[1,2,64,1024]{3,2,1,0:T(8,128)(2,1)} %param.10) | copy-start | bytes 786436
  4.0 39.8 %all-to-all-start = ((bf16[16,272,128]{2,1,0:T(8,128)(2,1)}), bf16[16,272,128]{2,1,0:T(8,128)(2,1)S(1)}, u32[]{:S(2)}, u32[]{:S(2)}) async-start(bf16[16,272,128]{2,1,0:T(8,128)(2,1)} %pack_time.1.refs_4_), calls=%async_computation | async-start | bytes 2228224 | tf_op jit(solution)/shard_map/all_to_all | solution.py:246
  15.7 9.9 %collective-permute-start = (bf16[4,3,64,128]{3,2,1,0:T(8,128)(2,1)S(1)}, bf16[4,3,64,128]{3,2,1,0:T(8,128)(2,1)S(1)}, u32[]{:S(2)}, u32[]{:S(2)}) collective-permute-start(bf16[4,3,64,128]{3,2,1,0:T(8,128)(2,1)S(1)} %get-tuple-element.39), channel_id=1, source_target_pairs={{0,32},{32,64},{64,96},{96,0},{1,33},{33,65},{65,97},{97,1},{2,34}... | collective-permute-start | bytes 589832 | tf_op jit(solution)/shard_map/ppermute | solution.py:230
  17.6 11.1 %collective-permute-start.1 = (bf16[4,3,64,128]{3,2,1,0:T(8,128)(2,1)S(1)}, bf16[4,3,64,128]{3,2,1,0:T(8,128)(2,1)S(1)}, u32[]{:S(2)}, u32[]{:S(2)}) collective-permute-start(bf16[4,3,64,128]{3,2,1,0:T(8,128)(2,1)S(1)} %get-tuple-element.40), channel_id=1, source_target_pairs={{0,64},{32,96},{64,0},{96,32},{1,65},{33,97},{65,1},{97,33},{2,66}... | collective-permute-start | bytes 589832 | tf_op jit(solution)/shard_map/ppermute | solution.py:230
  21.5 10.0 %collective-permute-start.2 = (bf16[4,3,64,128]{3,2,1,0:T(8,128)(2,1)S(1)}, bf16[4,3,64,128]{3,2,1,0:T(8,128)(2,1)S(1)}, u32[]{:S(2)}, u32[]{:S(2)}) collective-permute-start(bf16[4,3,64,128]{3,2,1,0:T(8,128)(2,1)S(1)} %get-tuple-element.41), channel_id=1, source_target_pairs={{0,96},{32,0},{64,32},{96,64},{1,97},{33,1},{65,33},{97,65},{2,98}... | collective-permute-start | bytes 589832 | tf_op jit(solution)/shard_map/ppermute | solution.py:230
  32.1 31.9 %collective-permute-start.3 = (bf16[4,3,64,128]{3,2,1,0:T(8,128)(2,1)S(1)}, bf16[4,3,64,128]{3,2,1,0:T(8,128)(2,1)S(1)}, u32[]{:S(2)}, u32[]{:S(2)}) collective-permute-start(bf16[4,3,64,128]{3,2,1,0:T(8,128)(2,1)S(1)} %get-tuple-element.43), channel_id=1, source_target_pairs={{0,128},{128,256},{256,384},{384,0},{1,129},{129,257},{257,385},{3... | collective-permute-start | bytes 589832 | tf_op jit(solution)/shard_map/ppermute | solution.py:230
  34.7 29.4 %collective-permute-start.4 = (bf16[4,3,64,128]{3,2,1,0:T(8,128)(2,1)S(1)}, bf16[4,3,64,128]{3,2,1,0:T(8,128)(2,1)S(1)}, u32[]{:S(2)}, u32[]{:S(2)}) collective-permute-start(bf16[4,3,64,128]{3,2,1,0:T(8,128)(2,1)S(1)} %get-tuple-element.44), channel_id=1, source_target_pairs={{0,256},{128,384},{256,0},{384,128},{1,257},{129,385},{257,1},{385... | collective-permute-start | bytes 589832 | tf_op jit(solution)/shard_map/ppermute | solution.py:230
  40.5 23.6 %collective-permute-start.5 = (bf16[4,3,64,128]{3,2,1,0:T(8,128)(2,1)S(1)}, bf16[4,3,64,128]{3,2,1,0:T(8,128)(2,1)S(1)}, u32[]{:S(2)}, u32[]{:S(2)}) collective-permute-start(bf16[4,3,64,128]{3,2,1,0:T(8,128)(2,1)S(1)} %get-tuple-element.45), channel_id=1, source_target_pairs={{0,384},{128,0},{256,128},{384,256},{1,385},{129,1},{257,129},{385... | collective-permute-start | bytes 589832 | tf_op jit(solution)/shard_map/ppermute | solution.py:230
  47.5 21.5 %all-to-all-start.1 = ((bf16[16,64,128]{2,1,0:T(8,128)(2,1)}), bf16[16,64,128]{2,1,0:T(8,128)(2,1)S(1)}, u32[]{:S(2)}, u32[]{:S(2)}) async-start(bf16[16,64,128]{2,1,0:T(8,128)(2,1)} %get-tuple-element.48), calls=%async_computation.1 | async-start | bytes 524288 | tf_op jit(solution)/shard_map/all_to_all | solution.py:278
  55.1 13.8 %collective-permute-start.6 = (bf16[32,1024]{1,0:T(8,128)(2,1)S(1)}, bf16[32,1024]{1,0:T(8,128)(2,1)S(1)}, u32[]{:S(2)}, u32[]{:S(2)}) collective-permute-start(bf16[32,1024]{1,0:T(8,128)(2,1)S(1)} %get-tuple-element.49.refs_2_), channel_id=1, source_target_pairs={{0,1},{1,0},{2,3},{3,2},{4,5},{5,4},{6,7},{7,6},{8,9},{9,8},{10,11... | collective-permute-start | bytes 196616 | tf_op jit(solution)/shard_map/ppermute | solution.py:279
  68.0 0.9 copy-start.4
  70.9 23.0 %all-to-all-start.2 = ((bf16[4,128,1024]{2,1,0:T(8,128)(2,1)}), bf16[4,128,1024]{2,1,0:T(8,128)(2,1)S(1)}, u32[]{:S(2)}, u32[]{:S(2)}) async-start(bf16[4,128,1024]{2,1,0:T(8,128)(2,1)} %get-tuple-element.54), calls=%async_computation.2 | async-start | bytes 2097152 | tf_op jit(solution)/shard_map/all_to_all | solution.py:300
  74.9 9.5 %collective-permute-start.7 = (bf16[64,1536]{1,0:T(8,128)(2,1)S(1)}, bf16[64,1536]{1,0:T(8,128)(2,1)S(1)}, u32[]{:S(2)}, u32[]{:S(2)}) collective-permute-start(bf16[64,1536]{1,0:T(8,128)(2,1)S(1)} %get-tuple-element.56), channel_id=1, source_target_pairs={{0,128},{128,256},{256,384},{384,0},{1,129},{129,257},{257,385},{3... | collective-permute-start | bytes 589832 | tf_op jit(solution)/shard_map/ppermute | solution.py:230
  77.1 16.8 %collective-permute-start.8 = (bf16[64,1536]{1,0:T(8,128)(2,1)S(1)}, bf16[64,1536]{1,0:T(8,128)(2,1)S(1)}, u32[]{:S(2)}, u32[]{:S(2)}) collective-permute-start(bf16[64,1536]{1,0:T(8,128)(2,1)S(1)} %get-tuple-element.57), channel_id=1, source_target_pairs={{0,256},{128,384},{256,0},{384,128},{1,257},{129,385},{257,1},{385... | collective-permute-start | bytes 589832 | tf_op jit(solution)/shard_map/ppermute | solution.py:230
  79.3 14.6 %collective-permute-start.9 = (bf16[64,1536]{1,0:T(8,128)(2,1)S(1)}, bf16[64,1536]{1,0:T(8,128)(2,1)S(1)}, u32[]{:S(2)}, u32[]{:S(2)}) collective-permute-start(bf16[64,1536]{1,0:T(8,128)(2,1)S(1)} %get-tuple-element.58), channel_id=1, source_target_pairs={{0,384},{128,0},{256,128},{384,256},{1,385},{129,1},{257,129},{385... | collective-permute-start | bytes 589832 | tf_op jit(solution)/shard_map/ppermute | solution.py:230
  95.7 25.2 %all-to-all-start.3 = ((bf16[16,16,1024]{2,1,0:T(8,128)(2,1)}), bf16[16,16,1024]{2,1,0:T(8,128)(2,1)S(1)}, u32[]{:S(2)}, u32[]{:S(2)}) async-start(bf16[16,16,1024]{2,1,0:T(8,128)(2,1)} %weight_grads.1.refs_5_), calls=%async_computation.3 | async-start | bytes 1048576 | tf_op jit(solution)/shard_map/all_to_all | solution.py:313
  105.1 10.9 %collective-permute-start.10 = (bf16[64,512]{1,0:T(8,128)(2,1)S(1)}, bf16[64,512]{1,0:T(8,128)(2,1)S(1)}, u32[]{:S(2)}, u32[]{:S(2)}) collective-permute-start(bf16[64,512]{1,0:T(8,128)(2,1)S(1)} %get-tuple-element.60), channel_id=1, source_target_pairs={{0,384},{128,0},{256,128},{384,256},{1,385},{129,1},{257,129},{385... | collective-permute-start | bytes 196616 | tf_op jit(solution)/shard_map/ppermute | solution.py:230
  110.1 7.6 %collective-permute-start.11 = (bf16[64,512]{1,0:T(8,128)(2,1)S(1)}, bf16[64,512]{1,0:T(8,128)(2,1)S(1)}, u32[]{:S(2)}, u32[]{:S(2)}) collective-permute-start(bf16[64,512]{1,0:T(8,128)(2,1)S(1)} %get-tuple-element.61), channel_id=1, source_target_pairs={{0,256},{128,384},{256,0},{384,128},{1,257},{129,385},{257,1},{385... | collective-permute-start | bytes 196616 | tf_op jit(solution)/shard_map/ppermute | solution.py:230
  114.1 6.8 %collective-permute-start.12 = (bf16[64,512]{1,0:T(8,128)(2,1)S(1)}, bf16[64,512]{1,0:T(8,128)(2,1)S(1)}, u32[]{:S(2)}, u32[]{:S(2)}) collective-permute-start(bf16[64,512]{1,0:T(8,128)(2,1)S(1)} %get-tuple-element.62), channel_id=1, source_target_pairs={{0,128},{128,256},{256,384},{384,0},{1,129},{129,257},{257,385},{3... | collective-permute-start | bytes 196616 | tf_op jit(solution)/shard_map/ppermute | solution.py:230
  121.6 15.3 %all-to-all-start.4 = ((f32[8,2,1024]{2,1,0:T(2,128)}), f32[8,2,1024]{2,1,0:T(2,128)S(1)}, u32[]{:S(2)}, u32[]{:S(2)}) async-start(f32[8,2,1024]{2,1,0:T(2,128)} %add_up.1.refs_7_), calls=%async_computation.4 | async-start | bytes 131072 | tf_op jit(solution)/shard_map/all_to_all | solution.py:326
  127.9 1.1 copy-start.5

commit v3 on v2

--- a/solution.py
+++ b/solution.py
@@ -10,7 +10,8 @@
 TM = ("y", "c")
 BF = jnp.bfloat16
 F32 = jnp.float32
-LIMIT = 48 * 1024 * 1024
+LIMIT = 16 * 1024 * 1024
+FRAME = 32 * 1024 * 1024
 WHOLE = 60 * 1024 * 1024
 VM = pl.BlockSpec(memory_space=pltpu.VMEM)
 SM = pl.BlockSpec(memory_space=pltpu.SMEM)
@@ -70,33 +71,33 @@
     row = lax.broadcasted_iota(jnp.int32, (128, 128), 0)
     col = lax.broadcasted_iota(jnp.int32, (128, 128), 1)
     allowed = ((row & 3) == (col & 3)) & (row <= col)
-    first = col < 64
+    bias = jnp.where(allowed, 0.0, -jnp.inf).astype(F32)
     zero = jnp.zeros((128, 128), BF)
+    scale = jnp.asarray(SCALING, BF)
+    cots, heads = [], []
+    for j in range(8):
+        block = r[:, 32 * j : 32 * j + 32, :].astype(F32)
+        q, k, v, cot = (block[:, 8 * a : 8 * a + 8, :].reshape(128, 128) for a in range(4))
+        cots.append(cot)
+        q, k, v, g = (t.astype(BF) for t in (q, k, v, cot))
+        for own in (col < 64, col >= 64):
+            qh, kh, gh = (jnp.where(own, t, zero) for t in (q, k, g))
+            heads.append((qh, k, kh, v, gh))
+    scores = [dot(k, qh * scale, ((1,), (1,))) + bias for qh, k, _, _, _ in heads]
+    probs = [dot(v, gh, ((1,), (1,))) for _, _, _, v, gh in heads]
+    exps = [jnp.exp(s - jnp.max(s, axis=0, keepdims=True)) for s in scores]
+    weights = [e * (1.0 / jnp.sum(e, axis=0, keepdims=True)) for e in exps]
+    parts_v = [dot(w.astype(BF), h[4], ((1,), (0,))) for w, h in zip(weights, heads)]
+    deltas = [jnp.sum(w * p, axis=0, keepdims=True) for w, p in zip(weights, probs)]
+    ds = [(w * (p - d) * SCALING).astype(BF) for w, p, d in zip(weights, probs, deltas)]
+    parts_k = [dot(d, h[0], ((1,), (0,))) for d, h in zip(ds, heads)]
+    parts_q = [dot(d, h[2], ((0,), (0,))) for d, h in zip(ds, heads)]
     kept = []
     for j in range(8):
-        block = r[:, 32 * j : 32 * j + 32, :].astype(F32)
-        q, k, v, g = (block[:, 8 * a : 8 * a + 8, :].reshape(128, 128).astype(BF) for a in range(4))
-        sum_q = sum_k = sum_v = None
-        for h in range(2):
-            own = first if h == 0 else jnp.logical_not(first)
-            qh, kh, gh = (jnp.where(own, t, zero) for t in (q, k, g))
-            score = dot(k, qh, ((1,), (1,))) * SCALING
-            score = jnp.where(allowed, score, -jnp.inf)
-            e = jnp.exp(score - jnp.max(score, axis=0, keepdims=True))
-            weight = e / jnp.sum(e, axis=0, keepdims=True)
-            prob = dot(v, gh, ((1,), (1,)))
-            delta = jnp.sum(weight * prob, axis=0, keepdims=True)
-            ds = (weight * (prob - delta) * SCALING).astype(BF)
-            part_k = dot(ds, qh, ((1,), (0,)))
-            part_v = dot(weight.astype(BF), gh, ((1,), (0,)))
-            part_q = dot(ds, kh, ((0,), (0,)))
-            sum_q = part_q if h == 0 else sum_q + part_q
-            sum_k = part_k if h == 0 else sum_k + part_k
-            sum_v = part_v if h == 0 else sum_v + part_v
         lanes = slice(128 * j, 128 * j + 128)
-        gq[:, :, lanes] = sum_q.reshape(32, 4, 128).astype(BF)
-        gk[:, :, lanes] = sum_k.reshape(32, 4, 128).astype(BF)
-        kept.append((g.astype(F32) + sum_v).reshape(16, 8, 128))
+        gq[:, :, lanes] = (parts_q[2 * j] + parts_q[2 * j + 1]).reshape(32, 4, 128).astype(BF)
+        gk[:, :, lanes] = (parts_k[2 * j] + parts_k[2 * j + 1]).reshape(32, 4, 128).astype(BF)
+        kept.append((cots[j] + (parts_v[2 * j] + parts_v[2 * j + 1])).reshape(16, 8, 128))
         if j % 2 == 1:
             gs[:, 8 * j - 8 : 8 * j + 8, :] = jnp.concatenate(kept, 1).astype(BF)
             kept = []
@@ -111,8 +112,8 @@
     for s, o in zip((s0, s1, s2, s3), outs):
         o[:, 0:512] = s[...]
     swapped = jnp.full((32, 128), ids[2], jnp.int32) == 1
-    for j in range(8):
-        lanes = slice(128 * j, 128 * j + 128)
+    for j in range(4):
+        lanes = pl.ds(pl.multiple_of(ids[3] * 512 + 128 * j, 128), 128)
         mine, theirs = own[:, lanes].astype(F32), other[:, lanes].astype(F32)
         low = jnp.where(swapped, theirs, mine)
         high = jnp.where(swapped, mine, theirs)
@@ -176,15 +177,19 @@
             o[:, 256 * f : 256 * f + 256] = ot[at, f]
 
 
-def mix_grads(g, r0, r1, r2, r3, m0, m1, m2, m3):
-    for r, m in ((r0, m0), (r1, m1), (r2, m2), (r3, m3)):
-        w = r[:, 512:1536]
+def mix_grads(ids, g, own, other, m0, m1, m2, m3, buf):
+    buf[ids[3]] = own[...]
+    buf[1 - ids[3]] = other[...]
+    for n, m in enumerate((m0, m1, m2, m3)):
+        w = jnp.concatenate([buf[0, n], buf[1, n]], 1)
         for x in range(4):
             m[:, 128 * x : 128 * x + 128] = dot(w, g[x], ((1,), (1,))).astype(BF)
 
 
-def weight_grads(ids, g, r0, r1, r2, r3, o, buf):
+def weight_grads(ids, g, r0, r1, r2, r3, o, held, buf):
     z = ids[0]
+    for n, r in enumerate((r0, r1, r2, r3)):
+        held[n] = r[:, 512:1024]
     for n, r in enumerate((r0, r1, r2, r3)):
         buf[lax.rem(z + 4 - n, 4)] = r[:, 0:512]
     left = buf[...].reshape(256, 512)
@@ -231,7 +236,7 @@
 
 
 def body(space_query, space_key, space_value, time_query, time_key, stream, cotangent, mix_weight):
-    ids = jnp.stack([lax.axis_index(a) for a in ("z", "x", "f")]).astype(jnp.int32)
+    ids = jnp.stack([lax.axis_index(a) for a in ("z", "x", "f", "c")]).astype(jnp.int32)
 
     packed = call(
         pack_time,
@@ -287,11 +292,12 @@
         flops=4 << 30,
         moved=2 << 20,
         name="space_forward",
+        limit=FRAME,
     )
 
     grad_stream, wide, *outputs = call(
         unpack_stream,
-        [((2, 64, 1024), BF), ((4, 128, 1024), BF)] + [((64, 1536), BF)] * 4,
+        [((2, 64, 1024), BF), ((4, 128, 1024), BF)] + [((64, 1024), BF)] * 4,
         [ids, back, own_rows, other_rows] + outputs,
         specs=[SM] + [VM] * 7,
         moved=1536 << 10,
@@ -300,29 +306,31 @@
     gathered = lax.all_to_all(wide, "x", 0, 0, tiled=True)
     outputs = [outputs[0]] + [shift(outputs[n], "z", n) for n in (1, 2, 3)]
 
-    partial = call(
+    partial, own_lanes = call(
         weight_grads,
-        [((16, 16, 1024), BF)],
+        [((16, 16, 1024), BF), ((4, 64, 512), BF)],
         [ids, gathered] + outputs,
         specs=[SM] + [VM] * 5,
         scratch=[pltpu.VMEM((4, 64, 512), BF)],
         flops=1 << 28,
         moved=2 << 20,
         name="weight_grads",
-    )[0]
+    )
+    other_lanes = lax.ppermute(own_lanes, "c", [(0, 1), (1, 0)])
     spread = lax.all_to_all(partial, TM, 0, 0, tiled=True)
     mixed = call(
         mix_grads,
         [((64, 512), BF)] * 4,
-        [gathered] + outputs,
+        [ids, gathered, own_lanes, other_lanes],
+        specs=[SM] + [VM] * 3,
+        scratch=[pltpu.VMEM((2, 4, 64, 512), BF)],
         flops=1 << 28,
         moved=2 << 20,
         name="mix_grads",
-        after=[partial],
     )
     mixed = [mixed[0]] + [shift(mixed[n], "z", -n) for n in (1, 2, 3)]
 
-    summed = call(add_up, [((8, 2, 1024), F32)], [spread], moved=1 << 19, name="add_up", after=mixed[1:])[0]
+    summed = call(add_up, [((8, 2, 1024), F32)], [spread], moved=1 << 19, name="add_up", after=mixed[:1])[0]
     last = lax.all_to_all(summed, ("z", "f"), 0, 0, tiled=True)
     grads = call(
         space_backward,
@@ -338,6 +346,7 @@
         flops=8 << 30,
         moved=4 << 20,
         name="space_backward",
+        limit=FRAME,
         after=[summed],
     )
     grad_mix_weight = jnp.sum(last, axis=0)

time: 138 us -> 131 us (0.949)
  waiting for transfers between devices: 22.9 us -> 18.1 us
    ppermute x12, waiting for transfers between devices: 21.8 us -> 12.8 us  [shift(): return lax.ppermute(value, axis, [(i, (i + by) % 4) for i in range(4)])]
    all_to_all x1, waiting for transfers between devices: 0.01 us -> 2.82 us  [body(): spread = lax.all_to_all(partial, TM, 0, 0, tiled=True)]
    ppermute x0 -> x1, starting transfers between devices: none -> 2.14 us  [body(): other_lanes = lax.ppermute(own_lanes, 'c', [(0, 1), (1, 0)])]
    ppermute x12, starting transfers between devices: 39.2 us -> 37.2 us  [shift(): return lax.ppermute(value, axis, [(i, (i + by) % 4) for i in range(4)])]
    ppermute x0 -> x1, waiting for transfers between devices: none -> 1.41 us  [body(): other_lanes = lax.ppermute(own_lanes, 'c', [(0, 1), (1, 0)])]
  transfers between devices with their start and end apart: 18 -> 19, of which waited for: 8 -> 8; matrix products, arithmetic and copies ran while one was open for 0% -> 0% of each run, Pallas kernels for 14% -> 14%
where the time goes in v3:
time: 131 us; the launch traced here: 130 us
  starting transfers between devices  83.7 us (64%)
  Pallas kernels  25.7 us (20%)
  waiting for transfers between devices  18.1 us (14%)
    ppermute x12, starting transfers between devices, shift(): return lax.ppermute(value, axis, [(i, (i + by) % 4) for i in range(4)])  37.2 us
    pallas_call x10, Pallas kernels, call(): pl.pallas_call(run, out_shape=shapes, in_specs=list(specs) + [ANY] * coun...  25.7 us
    ppermute x12, waiting for transfers between devices, shift(): return lax.ppermute(value, axis, [(i, (i + by) % 4) for i in range(4)])  12.8 us
    all_to_all x1, starting transfers between devices, body(): frames = lax.all_to_all(packed, TM, 0, 0, tiled=True)  10.5 us
    ppermute x1, starting transfers between devices, body(): other_rows = lax.ppermute(own_rows, 'f', [(0, 1), (1, 0)])  8.86 us
    all_to_all x1, starting transfers between devices, body(): spread = lax.all_to_all(partial, TM, 0, 0, tiled=True)  8.38 us
    all_to_all x1, starting transfers between devices, body(): back = lax.all_to_all(grad_frames, TM, 0, 0, tiled=True)  7.66 us
    all_to_all x1, starting transfers between devices, body(): last = lax.all_to_all(summed, ('z', 'f'), 0, 0, tiled=True)  4.92 us
  transfers between devices with their start and end apart: 19, of which 8 were waited for; matrix products, arithmetic and copies ran while one was open for 0% of the time, Pallas kernels for 14%

profile of v3, /device:TPU:1, one launch (start us, length us, event | category | flops | bytes accessed | tf_op | source)
XLA Modules:
  0.0 130.1 jit_solution(9246763743669161526)
XLA Ops:
  0.6 3.3 %pack_time.1.refs_4_ = bf16[16,272,128]{2,1,0:T(8,128)(2,1)} custom-call(bf16[2,64,1024]{2,1,0:T(8,128)(2,1)} %bitcast.26, bf16[2,64,1024]{2,1,0:T(8,128)(2,1)} %bitcast.27, bf16[2,64,1024]{2,1,0:T(8,128)(2,1)} %bitcast.28, bf16[2,64,1024]{2,1,0:T(8,128)(2,1)} %bitcast.29, bf16[2,1024]{1,0:T(2,128)(2,1)} %refs_4_.1), custom_call_target="tpu_custom_call" | custom-call | bytes 2097152 | tf_op jit(solution)/shard_map/pack_time/pallas_call | solution.py:30
  4.0 10.5 %all-to-all-start = ((bf16[16,272,128]{2,1,0:T(8,128)(2,1)}), bf16[16,272,128]{2,1,0:T(8,128)(2,1)S(1)}, u32[]{:S(2)}, u32[]{:S(2)}) async-start(bf16[16,272,128]{2,1,0:T(8,128)(2,1)} %pack_time.1.refs_4_), calls=%async_computation | async-start | bytes 2228224 | tf_op jit(solution)/shard_map/all_to_all | solution.py:251
  14.6 1.1 pack_space.1
  15.7 1.9 %collective-permute-start = (bf16[4,3,64,128]{3,2,1,0:T(8,128)(2,1)S(1)}, bf16[4,3,64,128]{3,2,1,0:T(8,128)(2,1)S(1)}, u32[]{:S(2)}, u32[]{:S(2)}) collective-permute-start(bf16[4,3,64,128]{3,2,1,0:T(8,128)(2,1)S(1)} %get-tuple-element.41), channel_id=1, source_target_pairs={{0,32},{32,64},{64,96},{96,0},{1,33},{33,65},{65,97},{97,1},{2,34}... | collective-permute-start | bytes 589832 | tf_op jit(solution)/shard_map/ppermute | solution.py:235
  17.7 3.8 %collective-permute-start.1 = (bf16[4,3,64,128]{3,2,1,0:T(8,128)(2,1)S(1)}, bf16[4,3,64,128]{3,2,1,0:T(8,128)(2,1)S(1)}, u32[]{:S(2)}, u32[]{:S(2)}) collective-permute-start(bf16[4,3,64,128]{3,2,1,0:T(8,128)(2,1)S(1)} %get-tuple-element.42), channel_id=1, source_target_pairs={{0,64},{32,96},{64,0},{96,32},{1,65},{33,97},{65,1},{97,33},{2,66}... | collective-permute-start | bytes 589832 | tf_op jit(solution)/shard_map/ppermute | solution.py:235
  21.5 3.1 %collective-permute-start.2 = (bf16[4,3,64,128]{3,2,1,0:T(8,128)(2,1)S(1)}, bf16[4,3,64,128]{3,2,1,0:T(8,128)(2,1)S(1)}, u32[]{:S(2)}, u32[]{:S(2)}) collective-permute-start(bf16[4,3,64,128]{3,2,1,0:T(8,128)(2,1)S(1)} %get-tuple-element.43), channel_id=1, source_target_pairs={{0,96},{32,0},{64,32},{96,64},{1,97},{33,1},{65,33},{97,65},{2,98}... | collective-permute-start | bytes 589832 | tf_op jit(solution)/shard_map/ppermute | solution.py:235
  25.6 3.2 %collective-permute-done.1.refs_3_ = bf16[4,3,64,128]{3,2,1,0:T(8,128)(2,1)S(1)} collective-permute-done((bf16[4,3,64,128]{3,2,1,0:T(8,128)(2,1)S(1)}, bf16[4,3,64,128]{3,2,1,0:T(8,128)(2,1)S(1)}, u32[]{:S(2)}, u32[]{:S(2)}) %collective-permute-start.1) | collective-permute-done | bytes 196640 | tf_op jit(solution)/shard_map/ppermute | solution.py:235
  28.8 2.7 %collective-permute-done.2.refs_4_ = bf16[4,3,64,128]{3,2,1,0:T(8,128)(2,1)S(1)} collective-permute-done((bf16[4,3,64,128]{3,2,1,0:T(8,128)(2,1)S(1)}, bf16[4,3,64,128]{3,2,1,0:T(8,128)(2,1)S(1)}, u32[]{:S(2)}, u32[]{:S(2)}) %collective-permute-start.2) | collective-permute-done | bytes 196640 | tf_op jit(solution)/shard_map/ppermute | solution.py:235
  32.1 2.6 %collective-permute-start.3 = (bf16[4,3,64,128]{3,2,1,0:T(8,128)(2,1)S(1)}, bf16[4,3,64,128]{3,2,1,0:T(8,128)(2,1)S(1)}, u32[]{:S(2)}, u32[]{:S(2)}) collective-permute-start(bf16[4,3,64,128]{3,2,1,0:T(8,128)(2,1)S(1)} %get-tuple-element.45), channel_id=1, source_target_pairs={{0,128},{128,256},{256,384},{384,0},{1,129},{129,257},{257,385},{3... | collective-permute-start | bytes 589832 | tf_op jit(solution)/shard_map/ppermute | solution.py:235
  34.7 5.8 %collective-permute-start.4 = (bf16[4,3,64,128]{3,2,1,0:T(8,128)(2,1)S(1)}, bf16[4,3,64,128]{3,2,1,0:T(8,128)(2,1)S(1)}, u32[]{:S(2)}, u32[]{:S(2)}) collective-permute-start(bf16[4,3,64,128]{3,2,1,0:T(8,128)(2,1)S(1)} %get-tuple-element.46), channel_id=1, source_target_pairs={{0,256},{128,384},{256,0},{384,128},{1,257},{129,385},{257,1},{385... | collective-permute-start | bytes 589832 | tf_op jit(solution)/shard_map/ppermute | solution.py:235
  40.5 2.2 %collective-permute-start.5 = (bf16[4,3,64,128]{3,2,1,0:T(8,128)(2,1)S(1)}, bf16[4,3,64,128]{3,2,1,0:T(8,128)(2,1)S(1)}, u32[]{:S(2)}, u32[]{:S(2)}) collective-permute-start(bf16[4,3,64,128]{3,2,1,0:T(8,128)(2,1)S(1)} %get-tuple-element.47), channel_id=1, source_target_pairs={{0,384},{128,0},{256,128},{384,256},{1,385},{129,1},{257,129},{385... | collective-permute-start | bytes 589832 | tf_op jit(solution)/shard_map/ppermute | solution.py:235
  43.8 2.2 %time_grads.1 = (bf16[32,4,1024]{2,1,0:T(4,128)(2,1)}, bf16[32,4,1024]{2,1,0:T(4,128)(2,1)}, bf16[16,64,128]{2,1,0:T(8,128)(2,1)}, bf16[32,1024]{1,0:T(8,128)(2,1)S(1)}) custom-call(bf16[16,272,128]{2,1,0:T(8,128)(2,1)S(1)} %all-to-all-done.refs_0_, bf16[4,3,64,128]{3,2,1,0:T(8,128)(2,1)S(1)} %get-tuple-element.44.refs_1_), custom_call_target="tpu_custom_call" | custom-call | flops 1073741824 | bytes 2097152 | tf_op jit(solution)/shard_map/time_grads/pallas_call | solution.py:30
  46.0 7.7 %all-to-all-start.1 = ((bf16[16,64,128]{2,1,0:T(8,128)(2,1)}), bf16[16,64,128]{2,1,0:T(8,128)(2,1)S(1)}, u32[]{:S(2)}, u32[]{:S(2)}) async-start(bf16[16,64,128]{2,1,0:T(8,128)(2,1)} %get-tuple-element.50), calls=%async_computation.1 | async-start | bytes 524288 | tf_op jit(solution)/shard_map/all_to_all | solution.py:283
  53.7 8.9 %collective-permute-start.6 = (bf16[32,1024]{1,0:T(8,128)(2,1)S(1)}, bf16[32,1024]{1,0:T(8,128)(2,1)S(1)}, u32[]{:S(2)}, u32[]{:S(2)}) collective-permute-start(bf16[32,1024]{1,0:T(8,128)(2,1)S(1)} %get-tuple-element.51.refs_2_), channel_id=1, source_target_pairs={{0,1},{1,0},{2,3},{3,2},{4,5},{5,4},{6,7},{7,6},{8,9},{9,8},{10,11... | collective-permute-start | bytes 196616 | tf_op jit(solution)/shard_map/ppermute | solution.py:284
  62.6 4.0 %space_forward.1 = (bf16[3,2,64,1024]{3,2,1,0:T(8,128)(2,1)S(1)}, f32[2,2,1024]{2,1,0:T(2,128)S(1)}, bf16[64,512]{1,0:T(8,128)(2,1)S(1)}, bf16[64,512]{1,0:T(8,1...) custom-call(s32[4]{0:T(128)S(1)} %pad_add_fusion.refs_0_, ...), custom_call_target="tpu_custom_call" | custom-call | flops 4294967296 | bytes 2097152 | tf_op jit(solution)/shard_map/space_forward/pallas_call | solution.py:30
  67.5 2.0 %unpack_stream.1 = (bf16[2,64,1024]{2,1,0:T(8,128)(2,1)}, bf16[4,128,1024]{2,1,0:T(8,128)(2,1)}, bf16[64,1024]{1,0:T(8,128)(2,1)S(1)}, bf16[64,1024]{1,0:T(8,128...) custom-call(s32[4]{0:T(128)S(1)} %pad_add_fusion.refs_0_, ...), custom_call_target="tpu_custom_call" | custom-call | bytes 1572864 | tf_op jit(solution)/shard_map/unpack_stream/pallas_call | solution.py:30
  69.4 4.1 %all-to-all-start.2 = ((bf16[4,128,1024]{2,1,0:T(8,128)(2,1)}), bf16[4,128,1024]{2,1,0:T(8,128)(2,1)S(1)}, u32[]{:S(2)}, u32[]{:S(2)}) async-start(bf16[4,128,1024]{2,1,0:T(8,128)(2,1)} %get-tuple-element.56), calls=%async_computation.2 | async-start | bytes 2097152 | tf_op jit(solution)/shard_map/all_to_all | solution.py:306
  73.5 2.2 %collective-permute-start.7 = (bf16[64,1024]{1,0:T(8,128)(2,1)S(1)}, bf16[64,1024]{1,0:T(8,128)(2,1)S(1)}, u32[]{:S(2)}, u32[]{:S(2)}) collective-permute-start(bf16[64,1024]{1,0:T(8,128)(2,1)S(1)} %get-tuple-element.58), channel_id=1, source_target_pairs={{0,128},{128,256},{256,384},{384,0},{1,129},{129,257},{257,385},{3... | collective-permute-start | bytes 393224 | tf_op jit(solution)/shard_map/ppermute | solution.py:235
  75.7 2.2 %collective-permute-start.8 = (bf16[64,1024]{1,0:T(8,128)(2,1)S(1)}, bf16[64,1024]{1,0:T(8,128)(2,1)S(1)}, u32[]{:S(2)}, u32[]{:S(2)}) collective-permute-start(bf16[64,1024]{1,0:T(8,128)(2,1)S(1)} %get-tuple-element.59), channel_id=1, source_target_pairs={{0,256},{128,384},{256,0},{384,128},{1,257},{129,385},{257,1},{385... | collective-permute-start | bytes 393224 | tf_op jit(solution)/shard_map/ppermute | solution.py:235
  77.9 4.6 %collective-permute-start.9 = (bf16[64,1024]{1,0:T(8,128)(2,1)S(1)}, bf16[64,1024]{1,0:T(8,128)(2,1)S(1)}, u32[]{:S(2)}, u32[]{:S(2)}) collective-permute-start(bf16[64,1024]{1,0:T(8,128)(2,1)S(1)} %get-tuple-element.60), channel_id=1, source_target_pairs={{0,384},{128,0},{256,128},{384,256},{1,385},{129,1},{257,129},{385... | collective-permute-start | bytes 393224 | tf_op jit(solution)/shard_map/ppermute | solution.py:235
  82.5 5.7 %collective-permute-done.8.refs_4_ = bf16[64,1024]{1,0:T(8,128)(2,1)S(1)} collective-permute-done((bf16[64,1024]{1,0:T(8,128)(2,1)S(1)}, bf16[64,1024]{1,0:T(8,128)(2,1)S(1)}, u32[]{:S(2)}, u32[]{:S(2)}) %collective-permute-start.8) | collective-permute-done | bytes 131104 | tf_op jit(solution)/shard_map/ppermute | solution.py:235
  88.4 1.8 %weight_grads.1 = (bf16[16,16,1024]{2,1,0:T(8,128)(2,1)}, bf16[4,64,512]{2,1,0:T(8,128)(2,1)S(1)}) custom-call(s32[4]{0:T(128)S(1)} %pad_add_fusion.refs_0_, bf16[4,128,1024]{2,1,0:T(8,128)(2,1)S(1)} %all-to-all-done.2.refs_1_, bf16[64,1024]{1,0:T(8,128)(2,1)S(1)} %get-tuple-element.57.refs_2_, bf16[64,1024]{1,0:T(8,128)(2,1)S(1)} %collective-permute-done.7.refs_3_, ...), custom_call_target="tpu_custom_call" | custom-call | flops 268435456 | bytes 2097152 | tf_op jit(solution)/shard_map/weight_grads/pallas_call | solution.py:30
  90.2 8.4 %all-to-all-start.3 = ((bf16[16,16,1024]{2,1,0:T(8,128)(2,1)}), bf16[16,16,1024]{2,1,0:T(8,128)(2,1)S(1)}, u32[]{:S(2)}, u32[]{:S(2)}) async-start(bf16[16,16,1024]{2,1,0:T(8,128)(2,1)} %get-tuple-element.66), calls=%async_computation.3 | async-start | bytes 1048576 | tf_op jit(solution)/shard_map/all_to_all | solution.py:320
  98.6 2.1 %collective-permute-start.10 = (bf16[4,64,512]{2,1,0:T(8,128)(2,1)S(1)}, bf16[4,64,512]{2,1,0:T(8,128)(2,1)S(1)}, u32[]{:S(2)}, u32[]{:S(2)}) collective-permute-start(bf16[4,64,512]{2,1,0:T(8,128)(2,1)S(1)} %get-tuple-element.61.refs_2_), channel_id=1, source_target_pairs={{0,2},{2,0},{1,3},{3,1},{4,6},{6,4},{5,7},{7,5},{8,10},{10,8},{9,1... | collective-permute-start | bytes 786440 | tf_op jit(solution)/shard_map/ppermute | solution.py:319
  100.7 1.4 %collective-permute-done.10.refs_3_ = bf16[4,64,512]{2,1,0:T(8,128)(2,1)S(1)} collective-permute-done((bf16[4,64,512]{2,1,0:T(8,128)(2,1)S(1)}, bf16[4,64,512]{2,1,0:T(8,128)(2,1)S(1)}, u32[]{:S(2)}, u32[]{:S(2)}) %collective-permute-start.10) | collective-permute-done | bytes 262176 | tf_op jit(solution)/shard_map/ppermute | solution.py:319
  102.1 2.1 %mix_grads.1 = (bf16[64,512]{1,0:T(8,128)(2,1)S(1)}, bf16[64,512]{1,0:T(8,128)(2,1)S(1)}, bf16[64,512]{1,0:T(8,128)(2,1)S(1)}, bf16[64,512]{1,0:T(8,128)(2,1)S(1)}) custom-call(s32[4]{0:T(128)S(1)} %pad_add_fusion.refs_0_, bf16[4,128,1024]{2,1,0:T(8,128)(2,1)S(1)} %all-to-all-done.2.refs_1_, bf16[4,64,512]{2,1,0:T(8,128)(2,1)S(1)} %get-tuple-element.61.refs_2_, ...), custom_call_target="tpu_custom_call" | custom-call | flops 268435456 | bytes 2097152 | tf_op jit(solution)/shard_map/mix_grads/pallas_call | solution.py:30
  104.2 3.8 %collective-permute-start.11 = (bf16[64,512]{1,0:T(8,128)(2,1)S(1)}, bf16[64,512]{1,0:T(8,128)(2,1)S(1)}, u32[]{:S(2)}, u32[]{:S(2)}) collective-permute-start(bf16[64,512]{1,0:T(8,128)(2,1)S(1)} %get-tuple-element.63), channel_id=1, source_target_pairs={{0,384},{128,0},{256,128},{384,256},{1,385},{129,1},{257,129},{385... | collective-permute-start | bytes 196616 | tf_op jit(solution)/shard_map/ppermute | solution.py:235
  108.0 3.1 %collective-permute-start.12 = (bf16[64,512]{1,0:T(8,128)(2,1)S(1)}, bf16[64,512]{1,0:T(8,128)(2,1)S(1)}, u32[]{:S(2)}, u32[]{:S(2)}) collective-permute-start(bf16[64,512]{1,0:T(8,128)(2,1)S(1)} %get-tuple-element.64), channel_id=1, source_target_pairs={{0,256},{128,384},{256,0},{384,128},{1,257},{129,385},{257,1},{385... | collective-permute-start | bytes 196616 | tf_op jit(solution)/shard_map/ppermute | solution.py:235
  111.1 1.9 %collective-permute-start.13 = (bf16[64,512]{1,0:T(8,128)(2,1)S(1)}, bf16[64,512]{1,0:T(8,128)(2,1)S(1)}, u32[]{:S(2)}, u32[]{:S(2)}) collective-permute-start(bf16[64,512]{1,0:T(8,128)(2,1)S(1)} %get-tuple-element.65), channel_id=1, source_target_pairs={{0,128},{128,256},{256,384},{384,0},{1,129},{129,257},{257,385},{3... | collective-permute-start | bytes 196616 | tf_op jit(solution)/shard_map/ppermute | solution.py:235
  113.1 2.8 %all-to-all-done.3.refs_0_ = bf16[16,16,1024]{2,1,0:T(8,128)(2,1)S(1)} async-done(((bf16[16,16,1024]{2,1,0:T(8,128)(2,1)}), bf16[16,16,1024]{2,1,0:T(8,128)(2,1)S(1)}, u32[]{:S(2)}, u32[]{:S(2)}) %all-to-all-start.3) | async-done | bytes 524320 | tf_op jit(solution)/shard_map/all_to_all | solution.py:320
  116.6 4.9 %all-to-all-start.4 = ((f32[8,2,1024]{2,1,0:T(2,128)}), f32[8,2,1024]{2,1,0:T(2,128)S(1)}, u32[]{:S(2)}, u32[]{:S(2)}) async-start(f32[8,2,1024]{2,1,0:T(2,128)} %add_up.1.refs_7_), calls=%async_computation.4 | async-start | bytes 131072 | tf_op jit(solution)/shard_map/all_to_all | solution.py:334
  121.5 7.9 %space_backward.1 = (bf16[2,64,1024]{2,1,0:T(8,128)(2,1)}, bf16[2,64,1024]{2,1,0:T(8,128)(2,1)}, bf16[2,64,1024]{2,1,0:T(8,128)(2,1)}) custom-call(s32[4]{0:T(128)S(1)} %pad_add_fusion.refs_0_, bf16[3,2,64,1024]{3,2,1,0:T(8,128)(2,1)S(1)} %copy-done.5, f32[2,2,1024]{2,1,0:T(2,128)S(1)} %get-tuple-element.49.refs_2_, ...), custom_call_target="tpu_custom_call" | custom-call | flops 8589934592 | bytes 4194304 | tf_op jit(solution)/shard_map/space_backward/pallas_call | solution.py:30
  (30 shorter events, 5.2 us)
Async XLA Ops:
  3.9 10.6 %copy-start = (bf16[16,272,128]{2,1,0:T(8,128)(2,1)S(1)}, bf16[16,272,128]{2,1,0:T(8,128)(2,1)}, u32[]{:S(2)}) copy-start(bf16[16,272,128]{2,1,0:T(8,128)(2,1)} %pack_time.1.refs_4_) | copy-start | bytes 3342340
  3.9 10.6 %copy-start.1 = (bf16[1,2,64,1024]{3,2,1,0:T(8,128)(2,1)S(1)}, bf16[1,2,64,1024]{3,2,1,0:T(8,128)(2,1)}, u32[]{:S(2)}) copy-start(bf16[1,2,64,1024]{3,2,1,0:T(8,128)(2,1)} %param.8) | copy-start | bytes 786436
  4.0 10.6 %copy-start.2 = (bf16[1,2,64,1024]{3,2,1,0:T(8,128)(2,1)S(1)}, bf16[1,2,64,1024]{3,2,1,0:T(8,128)(2,1)}, u32[]{:S(2)}) copy-start(bf16[1,2,64,1024]{3,2,1,0:T(8,128)(2,1)} %param.9) | copy-start | bytes 786436
  4.0 10.6 %copy-start.3 = (bf16[1,2,64,1024]{3,2,1,0:T(8,128)(2,1)S(1)}, bf16[1,2,64,1024]{3,2,1,0:T(8,128)(2,1)}, u32[]{:S(2)}) copy-start(bf16[1,2,64,1024]{3,2,1,0:T(8,128)(2,1)} %param.10) | copy-start | bytes 786436
  4.0 39.8 %all-to-all-start = ((bf16[16,272,128]{2,1,0:T(8,128)(2,1)}), bf16[16,272,128]{2,1,0:T(8,128)(2,1)S(1)}, u32[]{:S(2)}, u32[]{:S(2)}) async-start(bf16[16,272,128]{2,1,0:T(8,128)(2,1)} %pack_time.1.refs_4_), calls=%async_computation | async-start | bytes 2228224 | tf_op jit(solution)/shard_map/all_to_all | solution.py:251
  15.7 9.9 %collective-permute-start = (bf16[4,3,64,128]{3,2,1,0:T(8,128)(2,1)S(1)}, bf16[4,3,64,128]{3,2,1,0:T(8,128)(2,1)S(1)}, u32[]{:S(2)}, u32[]{:S(2)}) collective-permute-start(bf16[4,3,64,128]{3,2,1,0:T(8,128)(2,1)S(1)} %get-tuple-element.41), channel_id=1, source_target_pairs={{0,32},{32,64},{64,96},{96,0},{1,33},{33,65},{65,97},{97,1},{2,34}... | collective-permute-start | bytes 589832 | tf_op jit(solution)/shard_map/ppermute | solution.py:235
  17.7 11.1 %collective-permute-start.1 = (bf16[4,3,64,128]{3,2,1,0:T(8,128)(2,1)S(1)}, bf16[4,3,64,128]{3,2,1,0:T(8,128)(2,1)S(1)}, u32[]{:S(2)}, u32[]{:S(2)}) collective-permute-start(bf16[4,3,64,128]{3,2,1,0:T(8,128)(2,1)S(1)} %get-tuple-element.42), channel_id=1, source_target_pairs={{0,64},{32,96},{64,0},{96,32},{1,65},{33,97},{65,1},{97,33},{2,66}... | collective-permute-start | bytes 589832 | tf_op jit(solution)/shard_map/ppermute | solution.py:235
  21.5 10.0 %collective-permute-start.2 = (bf16[4,3,64,128]{3,2,1,0:T(8,128)(2,1)S(1)}, bf16[4,3,64,128]{3,2,1,0:T(8,128)(2,1)S(1)}, u32[]{:S(2)}, u32[]{:S(2)}) collective-permute-start(bf16[4,3,64,128]{3,2,1,0:T(8,128)(2,1)S(1)} %get-tuple-element.43), channel_id=1, source_target_pairs={{0,96},{32,0},{64,32},{96,64},{1,97},{33,1},{65,33},{97,65},{2,98}... | collective-permute-start | bytes 589832 | tf_op jit(solution)/shard_map/ppermute | solution.py:235
  32.1 30.4 %collective-permute-start.3 = (bf16[4,3,64,128]{3,2,1,0:T(8,128)(2,1)S(1)}, bf16[4,3,64,128]{3,2,1,0:T(8,128)(2,1)S(1)}, u32[]{:S(2)}, u32[]{:S(2)}) collective-permute-start(bf16[4,3,64,128]{3,2,1,0:T(8,128)(2,1)S(1)} %get-tuple-element.45), channel_id=1, source_target_pairs={{0,128},{128,256},{256,384},{384,0},{1,129},{129,257},{257,385},{3... | collective-permute-start | bytes 589832 | tf_op jit(solution)/shard_map/ppermute | solution.py:235
  34.7 27.9 %collective-permute-start.4 = (bf16[4,3,64,128]{3,2,1,0:T(8,128)(2,1)S(1)}, bf16[4,3,64,128]{3,2,1,0:T(8,128)(2,1)S(1)}, u32[]{:S(2)}, u32[]{:S(2)}) collective-permute-start(bf16[4,3,64,128]{3,2,1,0:T(8,128)(2,1)S(1)} %get-tuple-element.46), channel_id=1, source_target_pairs={{0,256},{128,384},{256,0},{384,128},{1,257},{129,385},{257,1},{385... | collective-permute-start | bytes 589832 | tf_op jit(solution)/shard_map/ppermute | solution.py:235
  40.5 22.1 %collective-permute-start.5 = (bf16[4,3,64,128]{3,2,1,0:T(8,128)(2,1)S(1)}, bf16[4,3,64,128]{3,2,1,0:T(8,128)(2,1)S(1)}, u32[]{:S(2)}, u32[]{:S(2)}) collective-permute-start(bf16[4,3,64,128]{3,2,1,0:T(8,128)(2,1)S(1)} %get-tuple-element.47), channel_id=1, source_target_pairs={{0,384},{128,0},{256,128},{384,256},{1,385},{129,1},{257,129},{385... | collective-permute-start | bytes 589832 | tf_op jit(solution)/shard_map/ppermute | solution.py:235
  46.0 21.5 %all-to-all-start.1 = ((bf16[16,64,128]{2,1,0:T(8,128)(2,1)}), bf16[16,64,128]{2,1,0:T(8,128)(2,1)S(1)}, u32[]{:S(2)}, u32[]{:S(2)}) async-start(bf16[16,64,128]{2,1,0:T(8,128)(2,1)} %get-tuple-element.50), calls=%async_computation.1 | async-start | bytes 524288 | tf_op jit(solution)/shard_map/all_to_all | solution.py:283
  53.7 13.8 %collective-permute-start.6 = (bf16[32,1024]{1,0:T(8,128)(2,1)S(1)}, bf16[32,1024]{1,0:T(8,128)(2,1)S(1)}, u32[]{:S(2)}, u32[]{:S(2)}) collective-permute-start(bf16[32,1024]{1,0:T(8,128)(2,1)S(1)} %get-tuple-element.51.refs_2_), channel_id=1, source_target_pairs={{0,1},{1,0},{2,3},{3,2},{4,5},{5,4},{6,7},{7,6},{8,9},{9,8},{10,11... | collective-permute-start | bytes 196616 | tf_op jit(solution)/shard_map/ppermute | solution.py:284
  66.5 0.9 copy-start.4
  69.4 18.9 %all-to-all-start.2 = ((bf16[4,128,1024]{2,1,0:T(8,128)(2,1)}), bf16[4,128,1024]{2,1,0:T(8,128)(2,1)S(1)}, u32[]{:S(2)}, u32[]{:S(2)}) async-start(bf16[4,128,1024]{2,1,0:T(8,128)(2,1)} %get-tuple-element.56), calls=%async_computation.2 | async-start | bytes 2097152 | tf_op jit(solution)/shard_map/all_to_all | solution.py:306
  73.5 9.0 %collective-permute-start.7 = (bf16[64,1024]{1,0:T(8,128)(2,1)S(1)}, bf16[64,1024]{1,0:T(8,128)(2,1)S(1)}, u32[]{:S(2)}, u32[]{:S(2)}) collective-permute-start(bf16[64,1024]{1,0:T(8,128)(2,1)S(1)} %get-tuple-element.58), channel_id=1, source_target_pairs={{0,128},{128,256},{256,384},{384,0},{1,129},{129,257},{257,385},{3... | collective-permute-start | bytes 393224 | tf_op jit(solution)/shard_map/ppermute | solution.py:235
  75.7 12.6 %collective-permute-start.8 = (bf16[64,1024]{1,0:T(8,128)(2,1)S(1)}, bf16[64,1024]{1,0:T(8,128)(2,1)S(1)}, u32[]{:S(2)}, u32[]{:S(2)}) collective-permute-start(bf16[64,1024]{1,0:T(8,128)(2,1)S(1)} %get-tuple-element.59), channel_id=1, source_target_pairs={{0,256},{128,384},{256,0},{384,128},{1,257},{129,385},{257,1},{385... | collective-permute-start | bytes 393224 | tf_op jit(solution)/shard_map/ppermute | solution.py:235
  77.9 10.5 %collective-permute-start.9 = (bf16[64,1024]{1,0:T(8,128)(2,1)S(1)}, bf16[64,1024]{1,0:T(8,128)(2,1)S(1)}, u32[]{:S(2)}, u32[]{:S(2)}) collective-permute-start(bf16[64,1024]{1,0:T(8,128)(2,1)S(1)} %get-tuple-element.60), channel_id=1, source_target_pairs={{0,384},{128,0},{256,128},{384,256},{1,385},{129,1},{257,129},{385... | collective-permute-start | bytes 393224 | tf_op jit(solution)/shard_map/ppermute | solution.py:235
  90.2 25.7 %all-to-all-start.3 = ((bf16[16,16,1024]{2,1,0:T(8,128)(2,1)}), bf16[16,16,1024]{2,1,0:T(8,128)(2,1)S(1)}, u32[]{:S(2)}, u32[]{:S(2)}) async-start(bf16[16,16,1024]{2,1,0:T(8,128)(2,1)} %get-tuple-element.66), calls=%async_computation.3 | async-start | bytes 1048576 | tf_op jit(solution)/shard_map/all_to_all | solution.py:320
  98.6 23.0 %copy-start.5 = (bf16[3,2,64,1024]{3,2,1,0:T(8,128)(2,1)S(1)}, bf16[3,2,64,1024]{3,2,1,0:T(8,128)(2,1)}, u32[]{:S(2)}) copy-start(bf16[3,2,64,1024]{3,2,1,0:T(8,128)(2,1)} %copy-done.4) | copy-start | bytes 2359300
  98.6 3.6 %collective-permute-start.10 = (bf16[4,64,512]{2,1,0:T(8,128)(2,1)S(1)}, bf16[4,64,512]{2,1,0:T(8,128)(2,1)S(1)}, u32[]{:S(2)}, u32[]{:S(2)}) collective-permute-start(bf16[4,64,512]{2,1,0:T(8,128)(2,1)S(1)} %get-tuple-element.61.refs_2_), channel_id=1, source_target_pairs={{0,2},{2,0},{1,3},{3,1},{4,6},{6,4},{5,7},{7,5},{8,10},{10,8},{9,1... | collective-permute-start | bytes 786440 | tf_op jit(solution)/shard_map/ppermute | solution.py:319
  104.2 17.3 %collective-permute-start.11 = (bf16[64,512]{1,0:T(8,128)(2,1)S(1)}, bf16[64,512]{1,0:T(8,128)(2,1)S(1)}, u32[]{:S(2)}, u32[]{:S(2)}) collective-permute-start(bf16[64,512]{1,0:T(8,128)(2,1)S(1)} %get-tuple-element.63), channel_id=1, source_target_pairs={{0,384},{128,0},{256,128},{384,256},{1,385},{129,1},{257,129},{385... | collective-permute-start | bytes 196616 | tf_op jit(solution)/shard_map/ppermute | solution.py:235
  108.0 13.5 %collective-permute-start.12 = (bf16[64,512]{1,0:T(8,128)(2,1)S(1)}, bf16[64,512]{1,0:T(8,128)(2,1)S(1)}, u32[]{:S(2)}, u32[]{:S(2)}) collective-permute-start(bf16[64,512]{1,0:T(8,128)(2,1)S(1)} %get-tuple-element.64), channel_id=1, source_target_pairs={{0,256},{128,384},{256,0},{384,128},{1,257},{129,385},{257,1},{385... | collective-permute-start | bytes 196616 | tf_op jit(solution)/shard_map/ppermute | solution.py:235
  111.1 10.4 %collective-permute-start.13 = (bf16[64,512]{1,0:T(8,128)(2,1)S(1)}, bf16[64,512]{1,0:T(8,128)(2,1)S(1)}, u32[]{:S(2)}, u32[]{:S(2)}) collective-permute-start(bf16[64,512]{1,0:T(8,128)(2,1)S(1)} %get-tuple-element.65), channel_id=1, source_target_pairs={{0,128},{128,256},{256,384},{384,0},{1,129},{129,257},{257,385},{3... | collective-permute-start | bytes 196616 | tf_op jit(solution)/shard_map/ppermute | solution.py:235
  116.6 12.9 %all-to-all-start.4 = ((f32[8,2,1024]{2,1,0:T(2,128)}), f32[8,2,1024]{2,1,0:T(2,128)S(1)}, u32[]{:S(2)}, u32[]{:S(2)}) async-start(f32[8,2,1024]{2,1,0:T(2,128)} %add_up.1.refs_7_), calls=%async_computation.4 | async-start | bytes 131072 | tf_op jit(solution)/shard_map/all_to_all | solution.py:334

commit v4 on v3

--- a/solution.py
+++ b/solution.py
@@ -19,7 +19,7 @@
 HBM = pl.BlockSpec(memory_space=pltpu.HBM)
 
 
-def call(kernel, outs, ins, specs=None, scratch=(), flops=0, moved=0, name=None, after=(), limit=LIMIT):
+def call(kernel, outs, ins, specs=None, scratch=(), flops=0, moved=0, name=None, after=(), limit=LIMIT, places=None):
     shapes = [jax.ShapeDtypeStruct(s, d) for s, d in outs]
     specs = specs or [VM] * len(ins)
     first, count = len(ins), len(after)
@@ -31,7 +31,7 @@
         run,
         out_shape=shapes,
         in_specs=list(specs) + [ANY] * count,
-        out_specs=[VM] * len(shapes),
+        out_specs=places or [VM] * len(shapes),
         scratch_shapes=list(scratch),
         compiler_params=pltpu.CompilerParams(vmem_limit_bytes=limit),
         cost_estimate=pl.CostEstimate(flops=flops, bytes_accessed=moved, transcendentals=0),
@@ -50,24 +50,41 @@
     return lax.dot_general(a, b, (dims, ((), ())), preferred_element_type=F32)
 
 
-def pack_time(tq, tk, st, ct, w, o, buf, sem):
-    pairs = [(ref.at[f], buf.at[a, f]) for a, ref in enumerate((tq, tk, st, ct)) for f in range(2)]
-    for copy in fetch(pairs, sem):
-        copy.wait()
-    for j in range(8):
-        lanes = slice(128 * j, 128 * j + 128)
-        wide = [[buf[a, f, :, lanes].astype(F32) for f in range(2)] for a in range(4)]
-        for g in range(16):
-            rows = slice(4 * g, 4 * g + 4)
-            block = jnp.concatenate([wide[a][f][rows] for a in range(4) for f in range(2)], 0)
-            o[g, 32 * j : 32 * j + 32, :] = block.astype(BF)
+def pack_time(tq, tk, st, ct, w, o, buf, stage, sem, out_sem):
+    copies = [
+        pltpu.make_async_copy(
+            ref.at[f, pl.ds(16 * h, 16)], buf.at[a, f, pl.ds(16 * h, 16)], sem.at[8 * h + 2 * a + f]
+        )
+        for h in range(4)
+        for a, ref in enumerate((tq, tk, st, ct))
+        for f in range(2)
+    ]
+    for copy in copies:
+        copy.start()
     own = w[...].astype(F32)
     own = jnp.concatenate([own[:, 128 * j : 128 * j + 128] for j in range(8)], 0).astype(BF)
     for g in range(16):
-        o[g, 256:272, :] = own
-
-
-def time_grads(r, gq, gk, gs, wo):
+        stage[g, 256:272, :] = own
+    results = []
+    for h in range(4):
+        for copy in copies[8 * h : 8 * h + 8]:
+            copy.wait()
+        for j in range(8):
+            lanes = slice(128 * j, 128 * j + 128)
+            wide = [[buf[a, f, 16 * h : 16 * h + 16, lanes].astype(F32) for f in range(2)] for a in range(4)]
+            for g in range(4):
+                rows = slice(4 * g, 4 * g + 4)
+                block = jnp.concatenate([wide[a][f][rows] for a in range(4) for f in range(2)], 0)
+                stage[4 * h + g, 32 * j : 32 * j + 32, :] = block.astype(BF)
+        results.append(
+            pltpu.make_async_copy(stage.at[pl.ds(4 * h, 4)], o.at[pl.ds(4 * h, 4)], out_sem.at[h])
+        )
+        results[-1].start()
+    for copy in results:
+        copy.wait()
+
+
+def time_heads(r):
     row = lax.broadcasted_iota(jnp.int32, (128, 128), 0)
     col = lax.broadcasted_iota(jnp.int32, (128, 128), 1)
     allowed = ((row & 3) == (col & 3)) & (row <= col)
@@ -84,28 +101,37 @@
             qh, kh, gh = (jnp.where(own, t, zero) for t in (q, k, g))
             heads.append((qh, k, kh, v, gh))
     scores = [dot(k, qh * scale, ((1,), (1,))) + bias for qh, k, _, _, _ in heads]
-    probs = [dot(v, gh, ((1,), (1,))) for _, _, _, v, gh in heads]
     exps = [jnp.exp(s - jnp.max(s, axis=0, keepdims=True)) for s in scores]
     weights = [e * (1.0 / jnp.sum(e, axis=0, keepdims=True)) for e in exps]
-    parts_v = [dot(w.astype(BF), h[4], ((1,), (0,))) for w, h in zip(weights, heads)]
+    return cots, heads, weights
+
+
+def time_stream(ids, r, gs, wo):
+    cots, heads, weights = time_heads(r)
+    parts = [dot(w.astype(BF), h[4], ((1,), (0,))) for w, h in zip(weights, heads)]
+    for j in range(0, 8, 2):
+        pair = [(cots[i] + (parts[2 * i] + parts[2 * i + 1])).reshape(16, 8, 128) for i in (j, j + 1)]
+        gs[:, 8 * j : 8 * j + 16, :] = jnp.concatenate(pair, 1).astype(BF)
+    rows = r[:, 256:272, :].astype(F32)
+    rows = jnp.where(jnp.full((16, 8, 128), ids[3], jnp.int32) == 1, rows[:, 8:16], rows[:, 0:8])
+    for j in range(4):
+        wo[:, 128 * j : 128 * j + 128] = jnp.concatenate(
+            [rows[g, 2 * j : 2 * j + 2, :] for g in range(16)], 0
+        ).astype(BF)
+
+
+def time_grads(r, gq, gk, token):
+    token[...] = jnp.zeros((8, 128), F32)
+    _, heads, weights = time_heads(r)
+    probs = [dot(v, gh, ((1,), (1,))) for _, _, _, v, gh in heads]
     deltas = [jnp.sum(w * p, axis=0, keepdims=True) for w, p in zip(weights, probs)]
     ds = [(w * (p - d) * SCALING).astype(BF) for w, p, d in zip(weights, probs, deltas)]
     parts_k = [dot(d, h[0], ((1,), (0,))) for d, h in zip(ds, heads)]
     parts_q = [dot(d, h[2], ((0,), (0,))) for d, h in zip(ds, heads)]
-    kept = []
     for j in range(8):
         lanes = slice(128 * j, 128 * j + 128)
         gq[:, :, lanes] = (parts_q[2 * j] + parts_q[2 * j + 1]).reshape(32, 4, 128).astype(BF)
         gk[:, :, lanes] = (parts_k[2 * j] + parts_k[2 * j + 1]).reshape(32, 4, 128).astype(BF)
-        kept.append((cots[j] + (parts_v[2 * j] + parts_v[2 * j + 1])).reshape(16, 8, 128))
-        if j % 2 == 1:
-            gs[:, 8 * j - 8 : 8 * j + 8, :] = jnp.concatenate(kept, 1).astype(BF)
-            kept = []
-    rows = r[:, 256:272, :].astype(F32)
-    for j in range(8):
-        wo[:, 128 * j : 128 * j + 128] = jnp.concatenate(
-            [rows[g, 2 * j : 2 * j + 2, :] for g in range(16)], 0
-        ).astype(BF)
 
 
 def unpack_stream(ids, r, own, other, s0, s1, s2, s3, gs, wide, *outs):
@@ -113,7 +139,7 @@
         o[:, 0:512] = s[...]
     swapped = jnp.full((32, 128), ids[2], jnp.int32) == 1
     for j in range(4):
-        lanes = pl.ds(pl.multiple_of(ids[3] * 512 + 128 * j, 128), 128)
+        lanes = slice(128 * j, 128 * j + 128)
         mine, theirs = own[:, lanes].astype(F32), other[:, lanes].astype(F32)
         low = jnp.where(swapped, theirs, mine)
         high = jnp.where(swapped, mine, theirs)
@@ -243,7 +269,13 @@
         [((16, 272, 128), BF)],
         [t.reshape(2, 64, 1024) for t in (time_query, time_key, stream, cotangent)] + [mix_weight],
         specs=[HBM] * 4 + [VM],
-        scratch=[pltpu.VMEM((4, 2, 64, 1024), BF), pltpu.SemaphoreType.DMA((8,))],
+        scratch=[
+            pltpu.VMEM((4, 2, 64, 1024), BF),
+            pltpu.VMEM((16, 272, 128), BF),
+            pltpu.SemaphoreType.DMA((32,)),
+            pltpu.SemaphoreType.DMA((4,)),
+        ],
+        places=[HBM],
         moved=2 << 20,
         name="pack_time",
         limit=WHOLE,
@@ -271,13 +303,14 @@
     )
     along_z = [turned[0]] + [shift(turned[n], "z", n) for n in (1, 2, 3)]
 
-    grad_time_query, grad_time_key, grad_frames, own_rows = call(
-        time_grads,
-        [((32, 4, 1024), BF), ((32, 4, 1024), BF), ((16, 64, 128), BF), ((32, 1024), BF)],
-        [frames],
+    grad_frames, own_rows = call(
+        time_stream,
+        [((16, 64, 128), BF), ((32, 512), BF)],
+        [ids, frames],
+        specs=[SM, VM],
         flops=1 << 30,
         moved=2 << 20,
-        name="time_grads",
+        name="time_stream",
         after=[turned[0]],
     )
     back = lax.all_to_all(grad_frames, TM, 0, 0, tiled=True)
@@ -306,6 +339,15 @@
     gathered = lax.all_to_all(wide, "x", 0, 0, tiled=True)
     outputs = [outputs[0]] + [shift(outputs[n], "z", n) for n in (1, 2, 3)]
 
+    grad_time_query, grad_time_key, token = call(
+        time_grads,
+        [((32, 4, 1024), BF)] * 2 + [((8, 128), F32)],
+        [frames],
+        flops=1 << 30,
+        moved=2 << 20,
+        name="time_grads",
+        after=[stats],
+    )
     partial, own_lanes = call(
         weight_grads,
         [((16, 16, 1024), BF), ((4, 64, 512), BF)],
@@ -315,6 +357,7 @@
         flops=1 << 28,
         moved=2 << 20,
         name="weight_grads",
+        after=[token],
     )
     other_lanes = lax.ppermute(own_lanes, "c", [(0, 1), (1, 0)])
     spread = lax.all_to_all(partial, TM, 0, 0, tiled=True)

time: 131 us -> 130 us (level)
  waiting for transfers between devices: 18.1 us -> 16.1 us
  Pallas kernels: 25.7 us -> 27.3 us
    ppermute x12, waiting for transfers between devices: 12.8 us -> 10.8 us  [shift(): return lax.ppermute(value, axis, [(i, (i + by) % 4) for i in range(4)])]
    pallas_call x10 -> x11, Pallas kernels: 25.7 us -> 27.3 us  [call(): pl.pallas_call(run, out_shape=shapes, in_specs=list(specs) + [ANY] * coun...]
  transfers between devices with their start and end apart: 19 -> 19, of which waited for: 8 -> 8; matrix products, arithmetic and copies ran while one was open for 0% -> 0% of each run, Pallas kernels for 14% -> 16%
where the time goes in v4:
time: 130 us; the launch traced here: 129 us
  starting transfers between devices  82.7 us (64%)
  Pallas kernels  27.3 us (21%)
  waiting for transfers between devices  16.1 us (12%)
    ppermute x12, starting transfers between devices, shift(): return lax.ppermute(value, axis, [(i, (i + by) % 4) for i in range(4)])  37.2 us
    pallas_call x11, Pallas kernels, call(): pl.pallas_call(run, out_shape=shapes, in_specs=list(specs) + [ANY] * coun...  27.3 us
    ppermute x12, waiting for transfers between devices, shift(): return lax.ppermute(value, axis, [(i, (i + by) % 4) for i in range(4)])  10.8 us
    all_to_all x1, starting transfers between devices, body(): frames = lax.all_to_all(packed, TM, 0, 0, tiled=True)  10.5 us
    ppermute x1, starting transfers between devices, body(): other_rows = lax.ppermute(own_rows, 'f', [(0, 1), (1, 0)])  8.86 us
    all_to_all x1, starting transfers between devices, body(): spread = lax.all_to_all(partial, TM, 0, 0, tiled=True)  8.38 us
    all_to_all x1, starting transfers between devices, body(): back = lax.all_to_all(grad_frames, TM, 0, 0, tiled=True)  7.66 us
    all_to_all x1, starting transfers between devices, body(): gathered = lax.all_to_all(wide, 'x', 0, 0, tiled=True)  4.05 us
  transfers between devices with their start and end apart: 19, of which 8 were waited for; matrix products, arithmetic and copies ran while one was open for 0% of the time, Pallas kernels for 16%

profile of v4, /device:TPU:1, one launch (start us, length us, event | category | flops | bytes accessed | tf_op | source)
XLA Modules:
  0.0 128.6 jit_solution(11175103886766507655)
XLA Ops:
  0.6 3.0 %pack_time.1.refs_4_ = bf16[16,272,128]{2,1,0:T(8,128)(2,1)} custom-call(bf16[2,64,1024]{2,1,0:T(8,128)(2,1)} %bitcast.26, bf16[2,64,1024]{2,1,0:T(8,128)(2,1)} %bitcast.27, bf16[2,64,1024]{2,1,0:T(8,128)(2,1)} %bitcast.28, bf16[2,64,1024]{2,1,0:T(8,128)(2,1)} %bitcast.29, bf16[2,1024]{1,0:T(2,128)(2,1)} %refs_4_.1), custom_call_target="tpu_custom_call" | custom-call | bytes 2097152 | tf_op jit(solution)/shard_map/pack_time/pallas_call | solution.py:30
  3.7 10.5 %all-to-all-start = ((bf16[16,272,128]{2,1,0:T(8,128)(2,1)}), bf16[16,272,128]{2,1,0:T(8,128)(2,1)S(1)}, u32[]{:S(2)}, u32[]{:S(2)}) async-start(bf16[16,272,128]{2,1,0:T(8,128)(2,1)} %pack_time.1.refs_4_), calls=%async_computation | async-start | bytes 2228224 | tf_op jit(solution)/shard_map/all_to_all | solution.py:283
  15.4 1.9 %collective-permute-start = (bf16[4,3,64,128]{3,2,1,0:T(8,128)(2,1)S(1)}, bf16[4,3,64,128]{3,2,1,0:T(8,128)(2,1)S(1)}, u32[]{:S(2)}, u32[]{:S(2)}) collective-permute-start(bf16[4,3,64,128]{3,2,1,0:T(8,128)(2,1)S(1)} %get-tuple-element.42), channel_id=1, source_target_pairs={{0,32},{32,64},{64,96},{96,0},{1,33},{33,65},{65,97},{97,1},{2,34}... | collective-permute-start | bytes 589832 | tf_op jit(solution)/shard_map/ppermute | solution.py:261
  17.3 3.8 %collective-permute-start.1 = (bf16[4,3,64,128]{3,2,1,0:T(8,128)(2,1)S(1)}, bf16[4,3,64,128]{3,2,1,0:T(8,128)(2,1)S(1)}, u32[]{:S(2)}, u32[]{:S(2)}) collective-permute-start(bf16[4,3,64,128]{3,2,1,0:T(8,128)(2,1)S(1)} %get-tuple-element.43), channel_id=1, source_target_pairs={{0,64},{32,96},{64,0},{96,32},{1,65},{33,97},{65,1},{97,33},{2,66}... | collective-permute-start | bytes 589832 | tf_op jit(solution)/shard_map/ppermute | solution.py:261
  21.2 3.1 %collective-permute-start.2 = (bf16[4,3,64,128]{3,2,1,0:T(8,128)(2,1)S(1)}, bf16[4,3,64,128]{3,2,1,0:T(8,128)(2,1)S(1)}, u32[]{:S(2)}, u32[]{:S(2)}) collective-permute-start(bf16[4,3,64,128]{3,2,1,0:T(8,128)(2,1)S(1)} %get-tuple-element.44), channel_id=1, source_target_pairs={{0,96},{32,0},{64,32},{96,64},{1,97},{33,1},{65,33},{97,65},{2,98}... | collective-permute-start | bytes 589832 | tf_op jit(solution)/shard_map/ppermute | solution.py:261
  25.3 3.2 %collective-permute-done.1.refs_3_ = bf16[4,3,64,128]{3,2,1,0:T(8,128)(2,1)S(1)} collective-permute-done((bf16[4,3,64,128]{3,2,1,0:T(8,128)(2,1)S(1)}, bf16[4,3,64,128]{3,2,1,0:T(8,128)(2,1)S(1)}, u32[]{:S(2)}, u32[]{:S(2)}) %collective-permute-start.1) | collective-permute-done | bytes 196640 | tf_op jit(solution)/shard_map/ppermute | solution.py:261
  28.5 2.7 %collective-permute-done.2.refs_4_ = bf16[4,3,64,128]{3,2,1,0:T(8,128)(2,1)S(1)} collective-permute-done((bf16[4,3,64,128]{3,2,1,0:T(8,128)(2,1)S(1)}, bf16[4,3,64,128]{3,2,1,0:T(8,128)(2,1)S(1)}, u32[]{:S(2)}, u32[]{:S(2)}) %collective-permute-start.2) | collective-permute-done | bytes 196640 | tf_op jit(solution)/shard_map/ppermute | solution.py:261
  31.8 2.6 %collective-permute-start.3 = (bf16[4,3,64,128]{3,2,1,0:T(8,128)(2,1)S(1)}, bf16[4,3,64,128]{3,2,1,0:T(8,128)(2,1)S(1)}, u32[]{:S(2)}, u32[]{:S(2)}) collective-permute-start(bf16[4,3,64,128]{3,2,1,0:T(8,128)(2,1)S(1)} %get-tuple-element.46), channel_id=1, source_target_pairs={{0,128},{128,256},{256,384},{384,0},{1,129},{129,257},{257,385},{3... | collective-permute-start | bytes 589832 | tf_op jit(solution)/shard_map/ppermute | solution.py:261
  34.4 5.8 %collective-permute-start.4 = (bf16[4,3,64,128]{3,2,1,0:T(8,128)(2,1)S(1)}, bf16[4,3,64,128]{3,2,1,0:T(8,128)(2,1)S(1)}, u32[]{:S(2)}, u32[]{:S(2)}) collective-permute-start(bf16[4,3,64,128]{3,2,1,0:T(8,128)(2,1)S(1)} %get-tuple-element.47), channel_id=1, source_target_pairs={{0,256},{128,384},{256,0},{384,128},{1,257},{129,385},{257,1},{385... | collective-permute-start | bytes 589832 | tf_op jit(solution)/shard_map/ppermute | solution.py:261
  40.2 2.2 %collective-permute-start.5 = (bf16[4,3,64,128]{3,2,1,0:T(8,128)(2,1)S(1)}, bf16[4,3,64,128]{3,2,1,0:T(8,128)(2,1)S(1)}, u32[]{:S(2)}, u32[]{:S(2)}) collective-permute-start(bf16[4,3,64,128]{3,2,1,0:T(8,128)(2,1)S(1)} %get-tuple-element.48), channel_id=1, source_target_pairs={{0,384},{128,0},{256,128},{384,256},{1,385},{129,1},{257,129},{385... | collective-permute-start | bytes 589832 | tf_op jit(solution)/shard_map/ppermute | solution.py:261
  43.5 2.0 %time_stream.1 = (bf16[16,64,128]{2,1,0:T(8,128)(2,1)}, bf16[32,512]{1,0:T(8,128)(2,1)S(1)}) custom-call(s32[4]{0:T(128)S(1)} %pad_add_fusion.refs_0_, bf16[16,272,128]{2,1,0:T(8,128)(2,1)S(1)} %all-to-all-done.refs_1_.refs_0_, bf16[4,3,64,128]{3,2,1,0:T(8,128)(2,1)S(1)} %get-tuple-element.45.refs_1_.refs_2_), custom_call_target="tpu_custom_call" | custom-call | flops 1073741824 | bytes 2097152 | tf_op jit(solution)/shard_map/time_stream/pallas_call | solution.py:30
  45.5 7.7 %all-to-all-start.1 = ((bf16[16,64,128]{2,1,0:T(8,128)(2,1)}), bf16[16,64,128]{2,1,0:T(8,128)(2,1)S(1)}, u32[]{:S(2)}, u32[]{:S(2)}) async-start(bf16[16,64,128]{2,1,0:T(8,128)(2,1)} %get-tuple-element.51), calls=%async_computation.1 | async-start | bytes 524288 | tf_op jit(solution)/shard_map/all_to_all | solution.py:316
  53.2 8.9 %collective-permute-start.6 = (bf16[32,512]{1,0:T(8,128)(2,1)S(1)}, bf16[32,512]{1,0:T(8,128)(2,1)S(1)}, u32[]{:S(2)}, u32[]{:S(2)}) collective-permute-start(bf16[32,512]{1,0:T(8,128)(2,1)S(1)} %get-tuple-element.52.refs_2_), channel_id=1, source_target_pairs={{0,1},{1,0},{2,3},{3,2},{4,5},{5,4},{6,7},{7,6},{8,9},{9,8},{10,11... | collective-permute-start | bytes 98312 | tf_op jit(solution)/shard_map/ppermute | solution.py:317
  62.1 4.0 %space_forward.1 = (bf16[3,2,64,1024]{3,2,1,0:T(8,128)(2,1)S(1)}, f32[2,2,1024]{2,1,0:T(2,128)S(1)}, bf16[64,512]{1,0:T(8,128)(2,1)S(1)}, bf16[64,512]{1,0:T(8,1...) custom-call(s32[4]{0:T(128)S(1)} %pad_add_fusion.refs_0_, ...), custom_call_target="tpu_custom_call" | custom-call | flops 4294967296 | bytes 2097152 | tf_op jit(solution)/shard_map/space_forward/pallas_call | solution.py:30
  67.0 2.0 %unpack_stream.1 = (bf16[2,64,1024]{2,1,0:T(8,128)(2,1)}, bf16[4,128,1024]{2,1,0:T(8,128)(2,1)}, bf16[64,1024]{1,0:T(8,128)(2,1)S(1)}, bf16[64,1024]{1,0:T(8,128...) custom-call(s32[4]{0:T(128)S(1)} %pad_add_fusion.refs_0_, ...), custom_call_target="tpu_custom_call" | custom-call | bytes 1572864 | tf_op jit(solution)/shard_map/unpack_stream/pallas_call | solution.py:30
  68.9 4.1 %all-to-all-start.2 = ((bf16[4,128,1024]{2,1,0:T(8,128)(2,1)}), bf16[4,128,1024]{2,1,0:T(8,128)(2,1)S(1)}, u32[]{:S(2)}, u32[]{:S(2)}) async-start(bf16[4,128,1024]{2,1,0:T(8,128)(2,1)} %get-tuple-element.57), calls=%async_computation.2 | async-start | bytes 2097152 | tf_op jit(solution)/shard_map/all_to_all | solution.py:339
  73.0 2.2 %collective-permute-start.7 = (bf16[64,1024]{1,0:T(8,128)(2,1)S(1)}, bf16[64,1024]{1,0:T(8,128)(2,1)S(1)}, u32[]{:S(2)}, u32[]{:S(2)}) collective-permute-start(bf16[64,1024]{1,0:T(8,128)(2,1)S(1)} %get-tuple-element.59), channel_id=1, source_target_pairs={{0,128},{128,256},{256,384},{384,0},{1,129},{129,257},{257,385},{3... | collective-permute-start | bytes 393224 | tf_op jit(solution)/shard_map/ppermute | solution.py:261
  75.2 2.2 %collective-permute-start.8 = (bf16[64,1024]{1,0:T(8,128)(2,1)S(1)}, bf16[64,1024]{1,0:T(8,128)(2,1)S(1)}, u32[]{:S(2)}, u32[]{:S(2)}) collective-permute-start(bf16[64,1024]{1,0:T(8,128)(2,1)S(1)} %get-tuple-element.60), channel_id=1, source_target_pairs={{0,256},{128,384},{256,0},{384,128},{1,257},{129,385},{257,1},{385... | collective-permute-start | bytes 393224 | tf_op jit(solution)/shard_map/ppermute | solution.py:261
  77.4 4.6 %collective-permute-start.9 = (bf16[64,1024]{1,0:T(8,128)(2,1)S(1)}, bf16[64,1024]{1,0:T(8,128)(2,1)S(1)}, u32[]{:S(2)}, u32[]{:S(2)}) collective-permute-start(bf16[64,1024]{1,0:T(8,128)(2,1)S(1)} %get-tuple-element.61), channel_id=1, source_target_pairs={{0,384},{128,0},{256,128},{384,256},{1,385},{129,1},{257,129},{385... | collective-permute-start | bytes 393224 | tf_op jit(solution)/shard_map/ppermute | solution.py:261
  82.0 2.0 %time_grads.1 = (bf16[32,4,1024]{2,1,0:T(4,128)(2,1)}, bf16[32,4,1024]{2,1,0:T(4,128)(2,1)}, f32[8,128]{1,0:T(8,128)S(1)}) custom-call(bf16[16,272,128]{2,1,0:T(8,128)(2,1)S(1)} %all-to-all-done.refs_1_.refs_0_, f32[2,2,1024]{2,1,0:T(2,128)S(1)} %get-tuple-element.50.refs_1_.refs_2_), custom_call_target="tpu_custom_call" | custom-call | flops 1073741824 | bytes 2097152 | tf_op jit(solution)/shard_map/time_grads/pallas_call | solution.py:30
  84.0 3.7 %collective-permute-done.8.refs_4_ = bf16[64,1024]{1,0:T(8,128)(2,1)S(1)} collective-permute-done((bf16[64,1024]{1,0:T(8,128)(2,1)S(1)}, bf16[64,1024]{1,0:T(8,128)(2,1)S(1)}, u32[]{:S(2)}, u32[]{:S(2)}) %collective-permute-start.8) | collective-permute-done | bytes 131104 | tf_op jit(solution)/shard_map/ppermute | solution.py:261
  87.9 1.8 %weight_grads.1 = (bf16[16,16,1024]{2,1,0:T(8,128)(2,1)}, bf16[4,64,512]{2,1,0:T(8,128)(2,1)S(1)}) custom-call(s32[4]{0:T(128)S(1)} %pad_add_fusion.refs_0_, bf16[4,128,1024]{2,1,0:T(8,128)(2,1)S(1)} %all-to-all-done.2.refs_1_, bf16[64,1024]{1,0:T(8,128)(2,1)S(1)} %get-tuple-element.58.refs_2_, bf16[64,1024]{1,0:T(8,128)(2,1)S(1)} %collective-permute-done.7.refs_3_, ...), custom_call_target="tpu_custom_call" | custom-call | flops 268435456 | bytes 2097152 | tf_op jit(solution)/shard_map/weight_grads/pallas_call | solution.py:30
  89.7 8.4 %all-to-all-start.3 = ((bf16[16,16,1024]{2,1,0:T(8,128)(2,1)}), bf16[16,16,1024]{2,1,0:T(8,128)(2,1)S(1)}, u32[]{:S(2)}, u32[]{:S(2)}) async-start(bf16[16,16,1024]{2,1,0:T(8,128)(2,1)} %get-tuple-element.68), calls=%async_computation.3 | async-start | bytes 1048576 | tf_op jit(solution)/shard_map/all_to_all | solution.py:363
  98.1 2.1 %collective-permute-start.10 = (bf16[4,64,512]{2,1,0:T(8,128)(2,1)S(1)}, bf16[4,64,512]{2,1,0:T(8,128)(2,1)S(1)}, u32[]{:S(2)}, u32[]{:S(2)}) collective-permute-start(bf16[4,64,512]{2,1,0:T(8,128)(2,1)S(1)} %get-tuple-element.63.refs_2_), channel_id=1, source_target_pairs={{0,2},{2,0},{1,3},{3,1},{4,6},{6,4},{5,7},{7,5},{8,10},{10,8},{9,1... | collective-permute-start | bytes 786440 | tf_op jit(solution)/shard_map/ppermute | solution.py:362
  100.2 1.4 %collective-permute-done.10.refs_3_ = bf16[4,64,512]{2,1,0:T(8,128)(2,1)S(1)} collective-permute-done((bf16[4,64,512]{2,1,0:T(8,128)(2,1)S(1)}, bf16[4,64,512]{2,1,0:T(8,128)(2,1)S(1)}, u32[]{:S(2)}, u32[]{:S(2)}) %collective-permute-start.10) | collective-permute-done | bytes 262176 | tf_op jit(solution)/shard_map/ppermute | solution.py:362
  101.6 2.1 %mix_grads.1 = (bf16[64,512]{1,0:T(8,128)(2,1)S(1)}, bf16[64,512]{1,0:T(8,128)(2,1)S(1)}, bf16[64,512]{1,0:T(8,128)(2,1)S(1)}, bf16[64,512]{1,0:T(8,128)(2,1)S(1)}) custom-call(s32[4]{0:T(128)S(1)} %pad_add_fusion.refs_0_, bf16[4,128,1024]{2,1,0:T(8,128)(2,1)S(1)} %all-to-all-done.2.refs_1_, bf16[4,64,512]{2,1,0:T(8,128)(2,1)S(1)} %get-tuple-element.63.refs_2_, ...), custom_call_target="tpu_custom_call" | custom-call | flops 268435456 | bytes 2097152 | tf_op jit(solution)/shard_map/mix_grads/pallas_call | solution.py:30
  103.7 3.8 %collective-permute-start.11 = (bf16[64,512]{1,0:T(8,128)(2,1)S(1)}, bf16[64,512]{1,0:T(8,128)(2,1)S(1)}, u32[]{:S(2)}, u32[]{:S(2)}) collective-permute-start(bf16[64,512]{1,0:T(8,128)(2,1)S(1)} %get-tuple-element.65), channel_id=1, source_target_pairs={{0,384},{128,0},{256,128},{384,256},{1,385},{129,1},{257,129},{385... | collective-permute-start | bytes 196616 | tf_op jit(solution)/shard_map/ppermute | solution.py:261
  107.5 3.1 %collective-permute-start.12 = (bf16[64,512]{1,0:T(8,128)(2,1)S(1)}, bf16[64,512]{1,0:T(8,128)(2,1)S(1)}, u32[]{:S(2)}, u32[]{:S(2)}) collective-permute-start(bf16[64,512]{1,0:T(8,128)(2,1)S(1)} %get-tuple-element.66), channel_id=1, source_target_pairs={{0,256},{128,384},{256,0},{384,128},{1,257},{129,385},{257,1},{385... | collective-permute-start | bytes 196616 | tf_op jit(solution)/shard_map/ppermute | solution.py:261
  110.6 1.9 %collective-permute-start.13 = (bf16[64,512]{1,0:T(8,128)(2,1)S(1)}, bf16[64,512]{1,0:T(8,128)(2,1)S(1)}, u32[]{:S(2)}, u32[]{:S(2)}) collective-permute-start(bf16[64,512]{1,0:T(8,128)(2,1)S(1)} %get-tuple-element.67), channel_id=1, source_target_pairs={{0,128},{128,256},{256,384},{384,0},{1,129},{129,257},{257,385},{3... | collective-permute-start | bytes 196616 | tf_op jit(solution)/shard_map/ppermute | solution.py:261
  112.6 2.8 %all-to-all-done.3.refs_0_ = bf16[16,16,1024]{2,1,0:T(8,128)(2,1)S(1)} async-done(((bf16[16,16,1024]{2,1,0:T(8,128)(2,1)}), bf16[16,16,1024]{2,1,0:T(8,128)(2,1)S(1)}, u32[]{:S(2)}, u32[]{:S(2)}) %all-to-all-start.3) | async-done | bytes 524320 | tf_op jit(solution)/shard_map/all_to_all | solution.py:363
  116.1 3.9 %all-to-all-start.4 = ((f32[8,2,1024]{2,1,0:T(2,128)}), f32[8,2,1024]{2,1,0:T(2,128)S(1)}, u32[]{:S(2)}, u32[]{:S(2)}) async-start(f32[8,2,1024]{2,1,0:T(2,128)} %add_up.1.refs_7_), calls=%async_computation.4 | async-start | bytes 131072 | tf_op jit(solution)/shard_map/all_to_all | solution.py:377
  120.0 7.9 %space_backward.1 = (bf16[2,64,1024]{2,1,0:T(8,128)(2,1)}, bf16[2,64,1024]{2,1,0:T(8,128)(2,1)}, bf16[2,64,1024]{2,1,0:T(8,128)(2,1)}) custom-call(s32[4]{0:T(128)S(1)} %pad_add_fusion.refs_0_, bf16[3,2,64,1024]{3,2,1,0:T(8,128)(2,1)S(1)} %copy-done.5, f32[2,2,1024]{2,1,0:T(2,128)S(1)} %get-tuple-element.50.refs_1_.refs_2_, ...), custom_call_target="tpu_custom_call" | custom-call | flops 8589934592 | bytes 4194304 | tf_op jit(solution)/shard_map/space_backward/pallas_call | solution.py:30
  (31 shorter events, 6.3 us)
Async XLA Ops:
  3.6 10.6 %copy-start = (bf16[16,272,128]{2,1,0:T(8,128)(2,1)S(1)}, bf16[16,272,128]{2,1,0:T(8,128)(2,1)}, u32[]{:S(2)}) copy-start(bf16[16,272,128]{2,1,0:T(8,128)(2,1)} %pack_time.1.refs_4_) | copy-start | bytes 3342340
  3.6 10.6 %copy-start.1 = (bf16[1,2,64,1024]{3,2,1,0:T(8,128)(2,1)S(1)}, bf16[1,2,64,1024]{3,2,1,0:T(8,128)(2,1)}, u32[]{:S(2)}) copy-start(bf16[1,2,64,1024]{3,2,1,0:T(8,128)(2,1)} %param.8) | copy-start | bytes 786436
  3.6 10.6 %copy-start.2 = (bf16[1,2,64,1024]{3,2,1,0:T(8,128)(2,1)S(1)}, bf16[1,2,64,1024]{3,2,1,0:T(8,128)(2,1)}, u32[]{:S(2)}) copy-start(bf16[1,2,64,1024]{3,2,1,0:T(8,128)(2,1)} %param.9) | copy-start | bytes 786436
  3.7 10.6 %copy-start.3 = (bf16[1,2,64,1024]{3,2,1,0:T(8,128)(2,1)S(1)}, bf16[1,2,64,1024]{3,2,1,0:T(8,128)(2,1)}, u32[]{:S(2)}) copy-start(bf16[1,2,64,1024]{3,2,1,0:T(8,128)(2,1)} %param.10) | copy-start | bytes 786436
  3.7 39.8 %all-to-all-start = ((bf16[16,272,128]{2,1,0:T(8,128)(2,1)}), bf16[16,272,128]{2,1,0:T(8,128)(2,1)S(1)}, u32[]{:S(2)}, u32[]{:S(2)}) async-start(bf16[16,272,128]{2,1,0:T(8,128)(2,1)} %pack_time.1.refs_4_), calls=%async_computation | async-start | bytes 2228224 | tf_op jit(solution)/shard_map/all_to_all | solution.py:283
  15.4 9.9 %collective-permute-start = (bf16[4,3,64,128]{3,2,1,0:T(8,128)(2,1)S(1)}, bf16[4,3,64,128]{3,2,1,0:T(8,128)(2,1)S(1)}, u32[]{:S(2)}, u32[]{:S(2)}) collective-permute-start(bf16[4,3,64,128]{3,2,1,0:T(8,128)(2,1)S(1)} %get-tuple-element.42), channel_id=1, source_target_pairs={{0,32},{32,64},{64,96},{96,0},{1,33},{33,65},{65,97},{97,1},{2,34}... | collective-permute-start | bytes 589832 | tf_op jit(solution)/shard_map/ppermute | solution.py:261
  17.3 11.1 %collective-permute-start.1 = (bf16[4,3,64,128]{3,2,1,0:T(8,128)(2,1)S(1)}, bf16[4,3,64,128]{3,2,1,0:T(8,128)(2,1)S(1)}, u32[]{:S(2)}, u32[]{:S(2)}) collective-permute-start(bf16[4,3,64,128]{3,2,1,0:T(8,128)(2,1)S(1)} %get-tuple-element.43), channel_id=1, source_target_pairs={{0,64},{32,96},{64,0},{96,32},{1,65},{33,97},{65,1},{97,33},{2,66}... | collective-permute-start | bytes 589832 | tf_op jit(solution)/shard_map/ppermute | solution.py:261
  21.2 10.0 %collective-permute-start.2 = (bf16[4,3,64,128]{3,2,1,0:T(8,128)(2,1)S(1)}, bf16[4,3,64,128]{3,2,1,0:T(8,128)(2,1)S(1)}, u32[]{:S(2)}, u32[]{:S(2)}) collective-permute-start(bf16[4,3,64,128]{3,2,1,0:T(8,128)(2,1)S(1)} %get-tuple-element.44), channel_id=1, source_target_pairs={{0,96},{32,0},{64,32},{96,64},{1,97},{33,1},{65,33},{97,65},{2,98}... | collective-permute-start | bytes 589832 | tf_op jit(solution)/shard_map/ppermute | solution.py:261
  31.8 30.3 %collective-permute-start.3 = (bf16[4,3,64,128]{3,2,1,0:T(8,128)(2,1)S(1)}, bf16[4,3,64,128]{3,2,1,0:T(8,128)(2,1)S(1)}, u32[]{:S(2)}, u32[]{:S(2)}) collective-permute-start(bf16[4,3,64,128]{3,2,1,0:T(8,128)(2,1)S(1)} %get-tuple-element.46), channel_id=1, source_target_pairs={{0,128},{128,256},{256,384},{384,0},{1,129},{129,257},{257,385},{3... | collective-permute-start | bytes 589832 | tf_op jit(solution)/shard_map/ppermute | solution.py:261
  34.4 27.7 %collective-permute-start.4 = (bf16[4,3,64,128]{3,2,1,0:T(8,128)(2,1)S(1)}, bf16[4,3,64,128]{3,2,1,0:T(8,128)(2,1)S(1)}, u32[]{:S(2)}, u32[]{:S(2)}) collective-permute-start(bf16[4,3,64,128]{3,2,1,0:T(8,128)(2,1)S(1)} %get-tuple-element.47), channel_id=1, source_target_pairs={{0,256},{128,384},{256,0},{384,128},{1,257},{129,385},{257,1},{385... | collective-permute-start | bytes 589832 | tf_op jit(solution)/shard_map/ppermute | solution.py:261
  40.2 21.9 %collective-permute-start.5 = (bf16[4,3,64,128]{3,2,1,0:T(8,128)(2,1)S(1)}, bf16[4,3,64,128]{3,2,1,0:T(8,128)(2,1)S(1)}, u32[]{:S(2)}, u32[]{:S(2)}) collective-permute-start(bf16[4,3,64,128]{3,2,1,0:T(8,128)(2,1)S(1)} %get-tuple-element.48), channel_id=1, source_target_pairs={{0,384},{128,0},{256,128},{384,256},{1,385},{129,1},{257,129},{385... | collective-permute-start | bytes 589832 | tf_op jit(solution)/shard_map/ppermute | solution.py:261
  45.5 21.5 %all-to-all-start.1 = ((bf16[16,64,128]{2,1,0:T(8,128)(2,1)}), bf16[16,64,128]{2,1,0:T(8,128)(2,1)S(1)}, u32[]{:S(2)}, u32[]{:S(2)}) async-start(bf16[16,64,128]{2,1,0:T(8,128)(2,1)} %get-tuple-element.51), calls=%async_computation.1 | async-start | bytes 524288 | tf_op jit(solution)/shard_map/all_to_all | solution.py:316
  53.2 13.8 %collective-permute-start.6 = (bf16[32,512]{1,0:T(8,128)(2,1)S(1)}, bf16[32,512]{1,0:T(8,128)(2,1)S(1)}, u32[]{:S(2)}, u32[]{:S(2)}) collective-permute-start(bf16[32,512]{1,0:T(8,128)(2,1)S(1)} %get-tuple-element.52.refs_2_), channel_id=1, source_target_pairs={{0,1},{1,0},{2,3},{3,2},{4,5},{5,4},{6,7},{7,6},{8,9},{9,8},{10,11... | collective-permute-start | bytes 98312 | tf_op jit(solution)/shard_map/ppermute | solution.py:317
  66.1 0.9 copy-start.4
  68.9 18.9 %all-to-all-start.2 = ((bf16[4,128,1024]{2,1,0:T(8,128)(2,1)}), bf16[4,128,1024]{2,1,0:T(8,128)(2,1)S(1)}, u32[]{:S(2)}, u32[]{:S(2)}) async-start(bf16[4,128,1024]{2,1,0:T(8,128)(2,1)} %get-tuple-element.57), calls=%async_computation.2 | async-start | bytes 2097152 | tf_op jit(solution)/shard_map/all_to_all | solution.py:339
  73.0 11.1 %collective-permute-start.7 = (bf16[64,1024]{1,0:T(8,128)(2,1)S(1)}, bf16[64,1024]{1,0:T(8,128)(2,1)S(1)}, u32[]{:S(2)}, u32[]{:S(2)}) collective-permute-start(bf16[64,1024]{1,0:T(8,128)(2,1)S(1)} %get-tuple-element.59), channel_id=1, source_target_pairs={{0,128},{128,256},{256,384},{384,0},{1,129},{129,257},{257,385},{3... | collective-permute-start | bytes 393224 | tf_op jit(solution)/shard_map/ppermute | solution.py:261
  75.2 12.6 %collective-permute-start.8 = (bf16[64,1024]{1,0:T(8,128)(2,1)S(1)}, bf16[64,1024]{1,0:T(8,128)(2,1)S(1)}, u32[]{:S(2)}, u32[]{:S(2)}) collective-permute-start(bf16[64,1024]{1,0:T(8,128)(2,1)S(1)} %get-tuple-element.60), channel_id=1, source_target_pairs={{0,256},{128,384},{256,0},{384,128},{1,257},{129,385},{257,1},{385... | collective-permute-start | bytes 393224 | tf_op jit(solution)/shard_map/ppermute | solution.py:261
  77.4 10.5 %collective-permute-start.9 = (bf16[64,1024]{1,0:T(8,128)(2,1)S(1)}, bf16[64,1024]{1,0:T(8,128)(2,1)S(1)}, u32[]{:S(2)}, u32[]{:S(2)}) collective-permute-start(bf16[64,1024]{1,0:T(8,128)(2,1)S(1)} %get-tuple-element.61), channel_id=1, source_target_pairs={{0,384},{128,0},{256,128},{384,256},{1,385},{129,1},{257,129},{385... | collective-permute-start | bytes 393224 | tf_op jit(solution)/shard_map/ppermute | solution.py:261
  89.7 25.7 %all-to-all-start.3 = ((bf16[16,16,1024]{2,1,0:T(8,128)(2,1)}), bf16[16,16,1024]{2,1,0:T(8,128)(2,1)S(1)}, u32[]{:S(2)}, u32[]{:S(2)}) async-start(bf16[16,16,1024]{2,1,0:T(8,128)(2,1)} %get-tuple-element.68), calls=%async_computation.3 | async-start | bytes 1048576 | tf_op jit(solution)/shard_map/all_to_all | solution.py:363
  98.1 22.0 %copy-start.5 = (bf16[3,2,64,1024]{3,2,1,0:T(8,128)(2,1)S(1)}, bf16[3,2,64,1024]{3,2,1,0:T(8,128)(2,1)}, u32[]{:S(2)}) copy-start(bf16[3,2,64,1024]{3,2,1,0:T(8,128)(2,1)} %copy-done.4) | copy-start | bytes 2359300
  98.1 3.6 %collective-permute-start.10 = (bf16[4,64,512]{2,1,0:T(8,128)(2,1)S(1)}, bf16[4,64,512]{2,1,0:T(8,128)(2,1)S(1)}, u32[]{:S(2)}, u32[]{:S(2)}) collective-permute-start(bf16[4,64,512]{2,1,0:T(8,128)(2,1)S(1)} %get-tuple-element.63.refs_2_), channel_id=1, source_target_pairs={{0,2},{2,0},{1,3},{3,1},{4,6},{6,4},{5,7},{7,5},{8,10},{10,8},{9,1... | collective-permute-start | bytes 786440 | tf_op jit(solution)/shard_map/ppermute | solution.py:362
  103.7 16.3 %collective-permute-start.11 = (bf16[64,512]{1,0:T(8,128)(2,1)S(1)}, bf16[64,512]{1,0:T(8,128)(2,1)S(1)}, u32[]{:S(2)}, u32[]{:S(2)}) collective-permute-start(bf16[64,512]{1,0:T(8,128)(2,1)S(1)} %get-tuple-element.65), channel_id=1, source_target_pairs={{0,384},{128,0},{256,128},{384,256},{1,385},{129,1},{257,129},{385... | collective-permute-start | bytes 196616 | tf_op jit(solution)/shard_map/ppermute | solution.py:261
  107.5 12.5 %collective-permute-start.12 = (bf16[64,512]{1,0:T(8,128)(2,1)S(1)}, bf16[64,512]{1,0:T(8,128)(2,1)S(1)}, u32[]{:S(2)}, u32[]{:S(2)}) collective-permute-start(bf16[64,512]{1,0:T(8,128)(2,1)S(1)} %get-tuple-element.66), channel_id=1, source_target_pairs={{0,256},{128,384},{256,0},{384,128},{1,257},{129,385},{257,1},{385... | collective-permute-start | bytes 196616 | tf_op jit(solution)/shard_map/ppermute | solution.py:261
  110.6 9.4 %collective-permute-start.13 = (bf16[64,512]{1,0:T(8,128)(2,1)S(1)}, bf16[64,512]{1,0:T(8,128)(2,1)S(1)}, u32[]{:S(2)}, u32[]{:S(2)}) collective-permute-start(bf16[64,512]{1,0:T(8,128)(2,1)S(1)} %get-tuple-element.67), channel_id=1, source_target_pairs={{0,128},{128,256},{256,384},{384,0},{1,129},{129,257},{257,385},{3... | collective-permute-start | bytes 196616 | tf_op jit(solution)/shard_map/ppermute | solution.py:261
  116.1 11.9 %all-to-all-start.4 = ((f32[8,2,1024]{2,1,0:T(2,128)}), f32[8,2,1024]{2,1,0:T(2,128)S(1)}, u32[]{:S(2)}, u32[]{:S(2)}) async-start(f32[8,2,1024]{2,1,0:T(2,128)} %add_up.1.refs_7_), calls=%async_computation.4 | async-start | bytes 131072 | tf_op jit(solution)/shard_map/all_to_all | solution.py:377

commit v5 on v4

--- a/solution.py
+++ b/solution.py
@@ -204,29 +204,38 @@
 
 
 def mix_grads(ids, g, own, other, m0, m1, m2, m3, buf):
-    buf[ids[3]] = own[...]
-    buf[1 - ids[3]] = other[...]
+    for n in range(4):
+        part = (slice(128 + 64 * (n // 2), 192 + 64 * (n // 2)), slice(512 * (n % 2), 512 * (n % 2) + 512))
+        buf[ids[3], n] = own[part]
+        buf[1 - ids[3], n] = other[part]
     for n, m in enumerate((m0, m1, m2, m3)):
         w = jnp.concatenate([buf[0, n], buf[1, n]], 1)
         for x in range(4):
             m[:, 128 * x : 128 * x + 128] = dot(w, g[x], ((1,), (1,))).astype(BF)
 
 
-def weight_grads(ids, g, r0, r1, r2, r3, o, held, buf):
+def weight_grads(ids, g, r0, r1, r2, r3, kept, sent, buf):
     z = ids[0]
     for n, r in enumerate((r0, r1, r2, r3)):
-        held[n] = r[:, 512:1024]
-    for n, r in enumerate((r0, r1, r2, r3)):
+        sent[128 + 64 * (n // 2) : 192 + 64 * (n // 2), 512 * (n % 2) : 512 * (n % 2) + 512] = r[:, 512:1024]
         buf[lax.rem(z + 4 - n, 4)] = r[:, 0:512]
     left = buf[...].reshape(256, 512)
+    second = jnp.full((16, 256), ids[3], jnp.int32) == 1
     for d in range(4):
         lanes = slice(256 * d, 256 * d + 256)
         right = jnp.concatenate(
             [g[x, 64 * f : 64 * f + 64, lanes] for f in range(2) for x in range(4)], 0
         )
         total = dot(left, right, ((1,), (0,))).reshape(4, 16, 4, 256)
-        for y in range(16):
-            o[y, :, lanes] = jnp.concatenate([total[n, y] for n in range(4)], 0).astype(BF)
+        for y in range(8):
+            v0, v1 = (jnp.concatenate([total[n, 2 * y + c] for n in range(4)], 0) for c in range(2))
+            kept[16 * y : 16 * y + 16, lanes] = jnp.where(second, v1, v0)
+            sent[16 * y : 16 * y + 16, lanes] = jnp.where(second, v0, v1).astype(BF)
+
+
+def add_pair(kept, got, o, token):
+    token[...] = jnp.zeros((8, 128), F32)
+    o[...] = (kept[...] + got[0:128, :].astype(F32)).astype(BF).reshape(8, 16, 1024)
 
 
 def space_backward(ids, heads, stats, m0, m1, m2, m3, gq, gk, gv, buf, got, ds_all, w_all):
@@ -251,7 +260,7 @@
 
 def add_up(r, o):
     total = r[0].astype(F32)
-    for i in range(1, 16):
+    for i in range(1, 8):
         total = total + r[i].astype(F32)
     for i in range(8):
         o[i] = total[2 * i : 2 * i + 2]
@@ -348,9 +357,9 @@
         name="time_grads",
         after=[stats],
     )
-    partial, own_lanes = call(
+    partial, sent_pair = call(
         weight_grads,
-        [((16, 16, 1024), BF), ((4, 64, 512), BF)],
+        [((128, 1024), F32), ((256, 1024), BF)],
         [ids, gathered] + outputs,
         specs=[SM] + [VM] * 5,
         scratch=[pltpu.VMEM((4, 64, 512), BF)],
@@ -359,17 +368,25 @@
         name="weight_grads",
         after=[token],
     )
-    other_lanes = lax.ppermute(own_lanes, "c", [(0, 1), (1, 0)])
-    spread = lax.all_to_all(partial, TM, 0, 0, tiled=True)
+    got_pair = lax.ppermute(sent_pair, "c", [(0, 1), (1, 0)])
+    partial, token = call(
+        add_pair,
+        [((8, 16, 1024), BF), ((8, 128), F32)],
+        [partial, got_pair],
+        moved=1 << 20,
+        name="add_pair",
+    )
+    spread = lax.all_to_all(partial, "y", 0, 0, tiled=True)
     mixed = call(
         mix_grads,
         [((64, 512), BF)] * 4,
-        [ids, gathered, own_lanes, other_lanes],
+        [ids, gathered, sent_pair, got_pair],
         specs=[SM] + [VM] * 3,
         scratch=[pltpu.VMEM((2, 4, 64, 512), BF)],
         flops=1 << 28,
         moved=2 << 20,
         name="mix_grads",
+        after=[token],
     )
     mixed = [mixed[0]] + [shift(mixed[n], "z", -n) for n in (1, 2, 3)]
 

time: 130 us -> 129 us (level)
  waiting for transfers between devices: 16.1 us -> 13.5 us
    all_to_all x1, waiting for transfers between devices: 2.8 us -> 0.15 us  [body(): spread = lax.all_to_all(partial, 'y', 0, 0, tiled=True)]
    all_to_all x1, starting transfers between devices: 8.38 us -> 6.54 us  [body(): spread = lax.all_to_all(partial, 'y', 0, 0, tiled=True)]
    ppermute x1, starting transfers between devices: 2.14 us -> 3.46 us  [body(): got_pair = lax.ppermute(sent_pair, 'c', [(0, 1), (1, 0)])]
    pallas_call x11 -> x12, Pallas kernels: 27.3 us -> 27.2 us  [call(): pl.pallas_call(run, out_shape=shapes, in_specs=list(specs) + [ANY] * coun...]
where the time goes in v5:
time: 129 us; the launch traced here: 127 us
  starting transfers between devices  82.7 us (64%)
  Pallas kernels  27.2 us (21%)
  waiting for transfers between devices  13.5 us (10%)
  local copies, waits for them, and re-layouts  2.04 us (2%)
    ppermute x12, starting transfers between devices, shift(): return lax.ppermute(value, axis, [(i, (i + by) % 4) for i in range(4)])  37.2 us
    pallas_call x12, Pallas kernels, call(): pl.pallas_call(run, out_shape=shapes, in_specs=list(specs) + [ANY] * coun...  27.2 us
    ppermute x12, waiting for transfers between devices, shift(): return lax.ppermute(value, axis, [(i, (i + by) % 4) for i in range(4)])  10.8 us
    all_to_all x1, starting transfers between devices, body(): frames = lax.all_to_all(packed, TM, 0, 0, tiled=True)  10.5 us
    ppermute x1, starting transfers between devices, body(): other_rows = lax.ppermute(own_rows, 'f', [(0, 1), (1, 0)])  8.86 us
    all_to_all x1, starting transfers between devices, body(): back = lax.all_to_all(grad_frames, TM, 0, 0, tiled=True)  7.67 us
    all_to_all x1, starting transfers between devices, body(): spread = lax.all_to_all(partial, 'y', 0, 0, tiled=True)  6.54 us
    all_to_all x1, starting transfers between devices, body(): last = lax.all_to_all(summed, ('z', 'f'), 0, 0, tiled=True)  4.39 us
  transfers between devices with their start and end apart: 19, of which 8 were waited for; matrix products, arithmetic and copies ran while one was open for 0% of the time, Pallas kernels for 16%

profile of v5, /device:TPU:1, one launch (start us, length us, event | category | flops | bytes accessed | tf_op | source)
XLA Modules:
  0.0 127.0 jit_solution(1052345039600579610)
XLA Ops:
  0.6 3.0 %pack_time.1.refs_4_ = bf16[16,272,128]{2,1,0:T(8,128)(2,1)} custom-call(bf16[2,64,1024]{2,1,0:T(8,128)(2,1)} %bitcast.26, bf16[2,64,1024]{2,1,0:T(8,128)(2,1)} %bitcast.27, bf16[2,64,1024]{2,1,0:T(8,128)(2,1)} %bitcast.28, bf16[2,64,1024]{2,1,0:T(8,128)(2,1)} %bitcast.29, bf16[2,1024]{1,0:T(2,128)(2,1)} %refs_4_.1), custom_call_target="tpu_custom_call" | custom-call | bytes 2097152 | tf_op jit(solution)/shard_map/pack_time/pallas_call | solution.py:30
  3.7 10.5 %all-to-all-start = ((bf16[16,272,128]{2,1,0:T(8,128)(2,1)}), bf16[16,272,128]{2,1,0:T(8,128)(2,1)S(1)}, u32[]{:S(2)}, u32[]{:S(2)}) async-start(bf16[16,272,128]{2,1,0:T(8,128)(2,1)} %pack_time.1.refs_4_), calls=%async_computation | async-start | bytes 2228224 | tf_op jit(solution)/shard_map/all_to_all | solution.py:292
  14.3 1.1 pack_space.1
  15.4 1.9 %collective-permute-start = (bf16[4,3,64,128]{3,2,1,0:T(8,128)(2,1)S(1)}, bf16[4,3,64,128]{3,2,1,0:T(8,128)(2,1)S(1)}, u32[]{:S(2)}, u32[]{:S(2)}) collective-permute-start(bf16[4,3,64,128]{3,2,1,0:T(8,128)(2,1)S(1)} %get-tuple-element.44), channel_id=1, source_target_pairs={{0,32},{32,64},{64,96},{96,0},{1,33},{33,65},{65,97},{97,1},{2,34}... | collective-permute-start | bytes 589832 | tf_op jit(solution)/shard_map/ppermute | solution.py:270
  17.4 3.8 %collective-permute-start.1 = (bf16[4,3,64,128]{3,2,1,0:T(8,128)(2,1)S(1)}, bf16[4,3,64,128]{3,2,1,0:T(8,128)(2,1)S(1)}, u32[]{:S(2)}, u32[]{:S(2)}) collective-permute-start(bf16[4,3,64,128]{3,2,1,0:T(8,128)(2,1)S(1)} %get-tuple-element.45), channel_id=1, source_target_pairs={{0,64},{32,96},{64,0},{96,32},{1,65},{33,97},{65,1},{97,33},{2,66}... | collective-permute-start | bytes 589832 | tf_op jit(solution)/shard_map/ppermute | solution.py:270
  21.2 3.1 %collective-permute-start.2 = (bf16[4,3,64,128]{3,2,1,0:T(8,128)(2,1)S(1)}, bf16[4,3,64,128]{3,2,1,0:T(8,128)(2,1)S(1)}, u32[]{:S(2)}, u32[]{:S(2)}) collective-permute-start(bf16[4,3,64,128]{3,2,1,0:T(8,128)(2,1)S(1)} %get-tuple-element.46), channel_id=1, source_target_pairs={{0,96},{32,0},{64,32},{96,64},{1,97},{33,1},{65,33},{97,65},{2,98}... | collective-permute-start | bytes 589832 | tf_op jit(solution)/shard_map/ppermute | solution.py:270
  25.3 3.2 %collective-permute-done.1.refs_3_ = bf16[4,3,64,128]{3,2,1,0:T(8,128)(2,1)S(1)} collective-permute-done((bf16[4,3,64,128]{3,2,1,0:T(8,128)(2,1)S(1)}, bf16[4,3,64,128]{3,2,1,0:T(8,128)(2,1)S(1)}, u32[]{:S(2)}, u32[]{:S(2)}) %collective-permute-start.1) | collective-permute-done | bytes 196640 | tf_op jit(solution)/shard_map/ppermute | solution.py:270
  28.5 2.7 %collective-permute-done.2.refs_4_ = bf16[4,3,64,128]{3,2,1,0:T(8,128)(2,1)S(1)} collective-permute-done((bf16[4,3,64,128]{3,2,1,0:T(8,128)(2,1)S(1)}, bf16[4,3,64,128]{3,2,1,0:T(8,128)(2,1)S(1)}, u32[]{:S(2)}, u32[]{:S(2)}) %collective-permute-start.2) | collective-permute-done | bytes 196640 | tf_op jit(solution)/shard_map/ppermute | solution.py:270
  31.8 2.6 %collective-permute-start.3 = (bf16[4,3,64,128]{3,2,1,0:T(8,128)(2,1)S(1)}, bf16[4,3,64,128]{3,2,1,0:T(8,128)(2,1)S(1)}, u32[]{:S(2)}, u32[]{:S(2)}) collective-permute-start(bf16[4,3,64,128]{3,2,1,0:T(8,128)(2,1)S(1)} %get-tuple-element.48), channel_id=1, source_target_pairs={{0,128},{128,256},{256,384},{384,0},{1,129},{129,257},{257,385},{3... | collective-permute-start | bytes 589832 | tf_op jit(solution)/shard_map/ppermute | solution.py:270
  34.4 5.8 %collective-permute-start.4 = (bf16[4,3,64,128]{3,2,1,0:T(8,128)(2,1)S(1)}, bf16[4,3,64,128]{3,2,1,0:T(8,128)(2,1)S(1)}, u32[]{:S(2)}, u32[]{:S(2)}) collective-permute-start(bf16[4,3,64,128]{3,2,1,0:T(8,128)(2,1)S(1)} %get-tuple-element.49), channel_id=1, source_target_pairs={{0,256},{128,384},{256,0},{384,128},{1,257},{129,385},{257,1},{385... | collective-permute-start | bytes 589832 | tf_op jit(solution)/shard_map/ppermute | solution.py:270
  40.2 2.2 %collective-permute-start.5 = (bf16[4,3,64,128]{3,2,1,0:T(8,128)(2,1)S(1)}, bf16[4,3,64,128]{3,2,1,0:T(8,128)(2,1)S(1)}, u32[]{:S(2)}, u32[]{:S(2)}) collective-permute-start(bf16[4,3,64,128]{3,2,1,0:T(8,128)(2,1)S(1)} %get-tuple-element.50), channel_id=1, source_target_pairs={{0,384},{128,0},{256,128},{384,256},{1,385},{129,1},{257,129},{385... | collective-permute-start | bytes 589832 | tf_op jit(solution)/shard_map/ppermute | solution.py:270
  43.5 2.0 %time_stream.1 = (bf16[16,64,128]{2,1,0:T(8,128)(2,1)}, bf16[32,512]{1,0:T(8,128)(2,1)S(1)}) custom-call(s32[4]{0:T(128)S(1)} %pad_add_fusion.refs_0_, bf16[16,272,128]{2,1,0:T(8,128)(2,1)S(1)} %all-to-all-done.refs_1_.refs_0_, bf16[4,3,64,128]{3,2,1,0:T(8,128)(2,1)S(1)} %get-tuple-element.47.refs_1_.refs_2_), custom_call_target="tpu_custom_call" | custom-call | flops 1073741824 | bytes 2097152 | tf_op jit(solution)/shard_map/time_stream/pallas_call | solution.py:30
  45.5 7.7 %all-to-all-start.1 = ((bf16[16,64,128]{2,1,0:T(8,128)(2,1)}), bf16[16,64,128]{2,1,0:T(8,128)(2,1)S(1)}, u32[]{:S(2)}, u32[]{:S(2)}) async-start(bf16[16,64,128]{2,1,0:T(8,128)(2,1)} %get-tuple-element.53), calls=%async_computation.1 | async-start | bytes 524288 | tf_op jit(solution)/shard_map/all_to_all | solution.py:325
  53.2 8.9 %collective-permute-start.6 = (bf16[32,512]{1,0:T(8,128)(2,1)S(1)}, bf16[32,512]{1,0:T(8,128)(2,1)S(1)}, u32[]{:S(2)}, u32[]{:S(2)}) collective-permute-start(bf16[32,512]{1,0:T(8,128)(2,1)S(1)} %get-tuple-element.54.refs_2_), channel_id=1, source_target_pairs={{0,1},{1,0},{2,3},{3,2},{4,5},{5,4},{6,7},{7,6},{8,9},{9,8},{10,11... | collective-permute-start | bytes 98312 | tf_op jit(solution)/shard_map/ppermute | solution.py:326
  62.1 4.0 %space_forward.1 = (bf16[3,2,64,1024]{3,2,1,0:T(8,128)(2,1)S(1)}, f32[2,2,1024]{2,1,0:T(2,128)S(1)}, bf16[64,512]{1,0:T(8,128)(2,1)S(1)}, bf16[64,512]{1,0:T(8,1...) custom-call(s32[4]{0:T(128)S(1)} %pad_add_fusion.refs_0_, ...), custom_call_target="tpu_custom_call" | custom-call | flops 4294967296 | bytes 2097152 | tf_op jit(solution)/shard_map/space_forward/pallas_call | solution.py:30
  67.0 1.9 %unpack_stream.1 = (bf16[2,64,1024]{2,1,0:T(8,128)(2,1)}, bf16[4,128,1024]{2,1,0:T(8,128)(2,1)}, bf16[64,1024]{1,0:T(8,128)(2,1)S(1)}, bf16[64,1024]{1,0:T(8,128...) custom-call(s32[4]{0:T(128)S(1)} %pad_add_fusion.refs_0_, ...), custom_call_target="tpu_custom_call" | custom-call | bytes 1572864 | tf_op jit(solution)/shard_map/unpack_stream/pallas_call | solution.py:30
  68.9 4.0 %all-to-all-start.2 = ((bf16[4,128,1024]{2,1,0:T(8,128)(2,1)}), bf16[4,128,1024]{2,1,0:T(8,128)(2,1)S(1)}, u32[]{:S(2)}, u32[]{:S(2)}) async-start(bf16[4,128,1024]{2,1,0:T(8,128)(2,1)} %get-tuple-element.59), calls=%async_computation.2 | async-start | bytes 2097152 | tf_op jit(solution)/shard_map/all_to_all | solution.py:348
  73.0 2.2 %collective-permute-start.7 = (bf16[64,1024]{1,0:T(8,128)(2,1)S(1)}, bf16[64,1024]{1,0:T(8,128)(2,1)S(1)}, u32[]{:S(2)}, u32[]{:S(2)}) collective-permute-start(bf16[64,1024]{1,0:T(8,128)(2,1)S(1)} %get-tuple-element.61), channel_id=1, source_target_pairs={{0,128},{128,256},{256,384},{384,0},{1,129},{129,257},{257,385},{3... | collective-permute-start | bytes 393224 | tf_op jit(solution)/shard_map/ppermute | solution.py:270
  75.2 2.2 %collective-permute-start.8 = (bf16[64,1024]{1,0:T(8,128)(2,1)S(1)}, bf16[64,1024]{1,0:T(8,128)(2,1)S(1)}, u32[]{:S(2)}, u32[]{:S(2)}) collective-permute-start(bf16[64,1024]{1,0:T(8,128)(2,1)S(1)} %get-tuple-element.62), channel_id=1, source_target_pairs={{0,256},{128,384},{256,0},{384,128},{1,257},{129,385},{257,1},{385... | collective-permute-start | bytes 393224 | tf_op jit(solution)/shard_map/ppermute | solution.py:270
  77.3 4.6 %collective-permute-start.9 = (bf16[64,1024]{1,0:T(8,128)(2,1)S(1)}, bf16[64,1024]{1,0:T(8,128)(2,1)S(1)}, u32[]{:S(2)}, u32[]{:S(2)}) collective-permute-start(bf16[64,1024]{1,0:T(8,128)(2,1)S(1)} %get-tuple-element.63), channel_id=1, source_target_pairs={{0,384},{128,0},{256,128},{384,256},{1,385},{129,1},{257,129},{385... | collective-permute-start | bytes 393224 | tf_op jit(solution)/shard_map/ppermute | solution.py:270
  82.0 2.0 %time_grads.1 = (bf16[32,4,1024]{2,1,0:T(4,128)(2,1)}, bf16[32,4,1024]{2,1,0:T(4,128)(2,1)}, f32[8,128]{1,0:T(8,128)S(1)}) custom-call(bf16[16,272,128]{2,1,0:T(8,128)(2,1)S(1)} %all-to-all-done.refs_1_.refs_0_, f32[2,2,1024]{2,1,0:T(2,128)S(1)} %get-tuple-element.52.refs_1_.refs_2_), custom_call_target="tpu_custom_call" | custom-call | flops 1073741824 | bytes 2097152 | tf_op jit(solution)/shard_map/time_grads/pallas_call | solution.py:30
  84.0 3.7 %collective-permute-done.8.refs_4_ = bf16[64,1024]{1,0:T(8,128)(2,1)S(1)} collective-permute-done((bf16[64,1024]{1,0:T(8,128)(2,1)S(1)}, bf16[64,1024]{1,0:T(8,128)(2,1)S(1)}, u32[]{:S(2)}, u32[]{:S(2)}) %collective-permute-start.8) | collective-permute-done | bytes 131104 | tf_op jit(solution)/shard_map/ppermute | solution.py:270
  88.9 3.5 %collective-permute-start.10 = (bf16[256,1024]{1,0:T(8,128)(2,1)S(1)}, bf16[256,1024]{1,0:T(8,128)(2,1)S(1)}, u32[]{:S(2)}, u32[]{:S(2)}) collective-permute-start(bf16[256,1024]{1,0:T(8,128)(2,1)S(1)} %get-tuple-element.65.refs_2_), channel_id=1, source_target_pairs={{0,2},{2,0},{1,3},{3,1},{4,6},{6,4},{5,7},{7,5},{8,10},{10,8},{9,1... | collective-permute-start | bytes 1572872 | tf_op jit(solution)/shard_map/ppermute | solution.py:371
  92.4 1.5 %collective-permute-done.10.refs_1_.refs_3_ = bf16[256,1024]{1,0:T(8,128)(2,1)S(1)} collective-permute-done((bf16[256,1024]{1,0:T(8,128)(2,1)S(1)}, bf16[256,1024]{1,0:T(8,128)(2,1)S(1)}, u32[]{:S(2)}, u32[]{:S(2)}) %collective-permute-start.10) | collective-permute-done | bytes 524320 | tf_op jit(solution)/shard_map/ppermute | solution.py:371
  94.6 6.5 %all-to-all-start.3 = ((bf16[8,16,1024]{2,1,0:T(8,128)(2,1)}), bf16[8,16,1024]{2,1,0:T(8,128)(2,1)S(1)}, u32[]{:S(2)}, u32[]{:S(2)}) async-start(bf16[8,16,1024]{2,1,0:T(8,128)(2,1)} %get-tuple-element.72), calls=%async_computation.3 | async-start | bytes 524288 | tf_op jit(solution)/shard_map/all_to_all | solution.py:379
  101.2 2.1 %mix_grads.1 = (bf16[64,512]{1,0:T(8,128)(2,1)S(1)}, bf16[64,512]{1,0:T(8,128)(2,1)S(1)}, bf16[64,512]{1,0:T(8,128)(2,1)S(1)}, bf16[64,512]{1,0:T(8,128)(2,1)S(1)}) custom-call(s32[4]{0:T(128)S(1)} %pad_add_fusion.refs_0_, bf16[4,128,1024]{2,1,0:T(8,128)(2,1)S(1)} %all-to-all-done.2.refs_1_, bf16[256,1024]{1,0:T(8,128)(2,1)S(1)} %get-tuple-element.65.refs_2_, ...), custom_call_target="tpu_custom_call" | custom-call | flops 268435456 | bytes 2097152 | tf_op jit(solution)/shard_map/mix_grads/pallas_call | solution.py:30
  103.3 3.8 %collective-permute-start.11 = (bf16[64,512]{1,0:T(8,128)(2,1)S(1)}, bf16[64,512]{1,0:T(8,128)(2,1)S(1)}, u32[]{:S(2)}, u32[]{:S(2)}) collective-permute-start(bf16[64,512]{1,0:T(8,128)(2,1)S(1)} %get-tuple-element.69), channel_id=1, source_target_pairs={{0,384},{128,0},{256,128},{384,256},{1,385},{129,1},{257,129},{385... | collective-permute-start | bytes 196616 | tf_op jit(solution)/shard_map/ppermute | solution.py:270
  107.1 3.1 %collective-permute-start.12 = (bf16[64,512]{1,0:T(8,128)(2,1)S(1)}, bf16[64,512]{1,0:T(8,128)(2,1)S(1)}, u32[]{:S(2)}, u32[]{:S(2)}) collective-permute-start(bf16[64,512]{1,0:T(8,128)(2,1)S(1)} %get-tuple-element.70), channel_id=1, source_target_pairs={{0,256},{128,384},{256,0},{384,128},{1,257},{129,385},{257,1},{385... | collective-permute-start | bytes 196616 | tf_op jit(solution)/shard_map/ppermute | solution.py:270
  110.2 1.9 %collective-permute-start.13 = (bf16[64,512]{1,0:T(8,128)(2,1)S(1)}, bf16[64,512]{1,0:T(8,128)(2,1)S(1)}, u32[]{:S(2)}, u32[]{:S(2)}) collective-permute-start(bf16[64,512]{1,0:T(8,128)(2,1)S(1)} %get-tuple-element.71), channel_id=1, source_target_pairs={{0,128},{128,256},{256,384},{384,0},{1,129},{129,257},{257,385},{3... | collective-permute-start | bytes 196616 | tf_op jit(solution)/shard_map/ppermute | solution.py:270
  112.9 4.4 %all-to-all-start.4 = ((f32[8,2,1024]{2,1,0:T(2,128)}), f32[8,2,1024]{2,1,0:T(2,128)S(1)}, u32[]{:S(2)}, u32[]{:S(2)}) async-start(f32[8,2,1024]{2,1,0:T(2,128)} %add_up.1.refs_7_), calls=%async_computation.4 | async-start | bytes 131072 | tf_op jit(solution)/shard_map/all_to_all | solution.py:394
  117.3 1.1 copy-done.5
  118.5 7.9 %space_backward.1 = (bf16[2,64,1024]{2,1,0:T(8,128)(2,1)}, bf16[2,64,1024]{2,1,0:T(8,128)(2,1)}, bf16[2,64,1024]{2,1,0:T(8,128)(2,1)}) custom-call(s32[4]{0:T(128)S(1)} %pad_add_fusion.refs_0_, bf16[3,2,64,1024]{3,2,1,0:T(8,128)(2,1)S(1)} %copy-done.5, f32[2,2,1024]{2,1,0:T(2,128)S(1)} %get-tuple-element.52.refs_1_.refs_2_, ...), custom_call_target="tpu_custom_call" | custom-call | flops 8589934592 | bytes 4194304 | tf_op jit(solution)/shard_map/space_backward/pallas_call | solution.py:30
  (32 shorter events, 7.1 us)
Async XLA Ops:
  3.6 10.6 %copy-start = (bf16[16,272,128]{2,1,0:T(8,128)(2,1)S(1)}, bf16[16,272,128]{2,1,0:T(8,128)(2,1)}, u32[]{:S(2)}) copy-start(bf16[16,272,128]{2,1,0:T(8,128)(2,1)} %pack_time.1.refs_4_) | copy-start | bytes 3342340
  3.6 10.6 %copy-start.1 = (bf16[1,2,64,1024]{3,2,1,0:T(8,128)(2,1)S(1)}, bf16[1,2,64,1024]{3,2,1,0:T(8,128)(2,1)}, u32[]{:S(2)}) copy-start(bf16[1,2,64,1024]{3,2,1,0:T(8,128)(2,1)} %param.8) | copy-start | bytes 786436
  3.7 10.6 %copy-start.2 = (bf16[1,2,64,1024]{3,2,1,0:T(8,128)(2,1)S(1)}, bf16[1,2,64,1024]{3,2,1,0:T(8,128)(2,1)}, u32[]{:S(2)}) copy-start(bf16[1,2,64,1024]{3,2,1,0:T(8,128)(2,1)} %param.9) | copy-start | bytes 786436
  3.7 10.6 %copy-start.3 = (bf16[1,2,64,1024]{3,2,1,0:T(8,128)(2,1)S(1)}, bf16[1,2,64,1024]{3,2,1,0:T(8,128)(2,1)}, u32[]{:S(2)}) copy-start(bf16[1,2,64,1024]{3,2,1,0:T(8,128)(2,1)} %param.10) | copy-start | bytes 786436
  3.7 39.8 %all-to-all-start = ((bf16[16,272,128]{2,1,0:T(8,128)(2,1)}), bf16[16,272,128]{2,1,0:T(8,128)(2,1)S(1)}, u32[]{:S(2)}, u32[]{:S(2)}) async-start(bf16[16,272,128]{2,1,0:T(8,128)(2,1)} %pack_time.1.refs_4_), calls=%async_computation | async-start | bytes 2228224 | tf_op jit(solution)/shard_map/all_to_all | solution.py:292
  15.4 9.9 %collective-permute-start = (bf16[4,3,64,128]{3,2,1,0:T(8,128)(2,1)S(1)}, bf16[4,3,64,128]{3,2,1,0:T(8,128)(2,1)S(1)}, u32[]{:S(2)}, u32[]{:S(2)}) collective-permute-start(bf16[4,3,64,128]{3,2,1,0:T(8,128)(2,1)S(1)} %get-tuple-element.44), channel_id=1, source_target_pairs={{0,32},{32,64},{64,96},{96,0},{1,33},{33,65},{65,97},{97,1},{2,34}... | collective-permute-start | bytes 589832 | tf_op jit(solution)/shard_map/ppermute | solution.py:270
  17.4 11.1 %collective-permute-start.1 = (bf16[4,3,64,128]{3,2,1,0:T(8,128)(2,1)S(1)}, bf16[4,3,64,128]{3,2,1,0:T(8,128)(2,1)S(1)}, u32[]{:S(2)}, u32[]{:S(2)}) collective-permute-start(bf16[4,3,64,128]{3,2,1,0:T(8,128)(2,1)S(1)} %get-tuple-element.45), channel_id=1, source_target_pairs={{0,64},{32,96},{64,0},{96,32},{1,65},{33,97},{65,1},{97,33},{2,66}... | collective-permute-start | bytes 589832 | tf_op jit(solution)/shard_map/ppermute | solution.py:270
  21.2 10.0 %collective-permute-start.2 = (bf16[4,3,64,128]{3,2,1,0:T(8,128)(2,1)S(1)}, bf16[4,3,64,128]{3,2,1,0:T(8,128)(2,1)S(1)}, u32[]{:S(2)}, u32[]{:S(2)}) collective-permute-start(bf16[4,3,64,128]{3,2,1,0:T(8,128)(2,1)S(1)} %get-tuple-element.46), channel_id=1, source_target_pairs={{0,96},{32,0},{64,32},{96,64},{1,97},{33,1},{65,33},{97,65},{2,98}... | collective-permute-start | bytes 589832 | tf_op jit(solution)/shard_map/ppermute | solution.py:270
  31.8 30.3 %collective-permute-start.3 = (bf16[4,3,64,128]{3,2,1,0:T(8,128)(2,1)S(1)}, bf16[4,3,64,128]{3,2,1,0:T(8,128)(2,1)S(1)}, u32[]{:S(2)}, u32[]{:S(2)}) collective-permute-start(bf16[4,3,64,128]{3,2,1,0:T(8,128)(2,1)S(1)} %get-tuple-element.48), channel_id=1, source_target_pairs={{0,128},{128,256},{256,384},{384,0},{1,129},{129,257},{257,385},{3... | collective-permute-start | bytes 589832 | tf_op jit(solution)/shard_map/ppermute | solution.py:270
  34.4 27.7 %collective-permute-start.4 = (bf16[4,3,64,128]{3,2,1,0:T(8,128)(2,1)S(1)}, bf16[4,3,64,128]{3,2,1,0:T(8,128)(2,1)S(1)}, u32[]{:S(2)}, u32[]{:S(2)}) collective-permute-start(bf16[4,3,64,128]{3,2,1,0:T(8,128)(2,1)S(1)} %get-tuple-element.49), channel_id=1, source_target_pairs={{0,256},{128,384},{256,0},{384,128},{1,257},{129,385},{257,1},{385... | collective-permute-start | bytes 589832 | tf_op jit(solution)/shard_map/ppermute | solution.py:270
  40.2 21.9 %collective-permute-start.5 = (bf16[4,3,64,128]{3,2,1,0:T(8,128)(2,1)S(1)}, bf16[4,3,64,128]{3,2,1,0:T(8,128)(2,1)S(1)}, u32[]{:S(2)}, u32[]{:S(2)}) collective-permute-start(bf16[4,3,64,128]{3,2,1,0:T(8,128)(2,1)S(1)} %get-tuple-element.50), channel_id=1, source_target_pairs={{0,384},{128,0},{256,128},{384,256},{1,385},{129,1},{257,129},{385... | collective-permute-start | bytes 589832 | tf_op jit(solution)/shard_map/ppermute | solution.py:270
  45.5 21.5 %all-to-all-start.1 = ((bf16[16,64,128]{2,1,0:T(8,128)(2,1)}), bf16[16,64,128]{2,1,0:T(8,128)(2,1)S(1)}, u32[]{:S(2)}, u32[]{:S(2)}) async-start(bf16[16,64,128]{2,1,0:T(8,128)(2,1)} %get-tuple-element.53), calls=%async_computation.1 | async-start | bytes 524288 | tf_op jit(solution)/shard_map/all_to_all | solution.py:325
  53.2 13.8 %collective-permute-start.6 = (bf16[32,512]{1,0:T(8,128)(2,1)S(1)}, bf16[32,512]{1,0:T(8,128)(2,1)S(1)}, u32[]{:S(2)}, u32[]{:S(2)}) collective-permute-start(bf16[32,512]{1,0:T(8,128)(2,1)S(1)} %get-tuple-element.54.refs_2_), channel_id=1, source_target_pairs={{0,1},{1,0},{2,3},{3,2},{4,5},{5,4},{6,7},{7,6},{8,9},{9,8},{10,11... | collective-permute-start | bytes 98312 | tf_op jit(solution)/shard_map/ppermute | solution.py:326
  66.1 0.9 copy-start.4
  68.9 18.9 %all-to-all-start.2 = ((bf16[4,128,1024]{2,1,0:T(8,128)(2,1)}), bf16[4,128,1024]{2,1,0:T(8,128)(2,1)S(1)}, u32[]{:S(2)}, u32[]{:S(2)}) async-start(bf16[4,128,1024]{2,1,0:T(8,128)(2,1)} %get-tuple-element.59), calls=%async_computation.2 | async-start | bytes 2097152 | tf_op jit(solution)/shard_map/all_to_all | solution.py:348
  73.0 11.1 %collective-permute-start.7 = (bf16[64,1024]{1,0:T(8,128)(2,1)S(1)}, bf16[64,1024]{1,0:T(8,128)(2,1)S(1)}, u32[]{:S(2)}, u32[]{:S(2)}) collective-permute-start(bf16[64,1024]{1,0:T(8,128)(2,1)S(1)} %get-tuple-element.61), channel_id=1, source_target_pairs={{0,128},{128,256},{256,384},{384,0},{1,129},{129,257},{257,385},{3... | collective-permute-start | bytes 393224 | tf_op jit(solution)/shard_map/ppermute | solution.py:270
  75.2 12.6 %collective-permute-start.8 = (bf16[64,1024]{1,0:T(8,128)(2,1)S(1)}, bf16[64,1024]{1,0:T(8,128)(2,1)S(1)}, u32[]{:S(2)}, u32[]{:S(2)}) collective-permute-start(bf16[64,1024]{1,0:T(8,128)(2,1)S(1)} %get-tuple-element.62), channel_id=1, source_target_pairs={{0,256},{128,384},{256,0},{384,128},{1,257},{129,385},{257,1},{385... | collective-permute-start | bytes 393224 | tf_op jit(solution)/shard_map/ppermute | solution.py:270
  77.3 10.5 %collective-permute-start.9 = (bf16[64,1024]{1,0:T(8,128)(2,1)S(1)}, bf16[64,1024]{1,0:T(8,128)(2,1)S(1)}, u32[]{:S(2)}, u32[]{:S(2)}) collective-permute-start(bf16[64,1024]{1,0:T(8,128)(2,1)S(1)} %get-tuple-element.63), channel_id=1, source_target_pairs={{0,384},{128,0},{256,128},{384,256},{1,385},{129,1},{257,129},{385... | collective-permute-start | bytes 393224 | tf_op jit(solution)/shard_map/ppermute | solution.py:270
  88.9 5.0 %collective-permute-start.10 = (bf16[256,1024]{1,0:T(8,128)(2,1)S(1)}, bf16[256,1024]{1,0:T(8,128)(2,1)S(1)}, u32[]{:S(2)}, u32[]{:S(2)}) collective-permute-start(bf16[256,1024]{1,0:T(8,128)(2,1)S(1)} %get-tuple-element.65.refs_2_), channel_id=1, source_target_pairs={{0,2},{2,0},{1,3},{3,1},{4,6},{6,4},{5,7},{7,5},{8,10},{10,8},{9,1... | collective-permute-start | bytes 1572872 | tf_op jit(solution)/shard_map/ppermute | solution.py:371
  94.6 17.6 %all-to-all-start.3 = ((bf16[8,16,1024]{2,1,0:T(8,128)(2,1)}), bf16[8,16,1024]{2,1,0:T(8,128)(2,1)S(1)}, u32[]{:S(2)}, u32[]{:S(2)}) async-start(bf16[8,16,1024]{2,1,0:T(8,128)(2,1)} %get-tuple-element.72), calls=%async_computation.3 | async-start | bytes 524288 | tf_op jit(solution)/shard_map/all_to_all | solution.py:379
  103.3 14.1 %collective-permute-start.11 = (bf16[64,512]{1,0:T(8,128)(2,1)S(1)}, bf16[64,512]{1,0:T(8,128)(2,1)S(1)}, u32[]{:S(2)}, u32[]{:S(2)}) collective-permute-start(bf16[64,512]{1,0:T(8,128)(2,1)S(1)} %get-tuple-element.69), channel_id=1, source_target_pairs={{0,384},{128,0},{256,128},{384,256},{1,385},{129,1},{257,129},{385... | collective-permute-start | bytes 196616 | tf_op jit(solution)/shard_map/ppermute | solution.py:270
  107.1 10.3 %collective-permute-start.12 = (bf16[64,512]{1,0:T(8,128)(2,1)S(1)}, bf16[64,512]{1,0:T(8,128)(2,1)S(1)}, u32[]{:S(2)}, u32[]{:S(2)}) collective-permute-start(bf16[64,512]{1,0:T(8,128)(2,1)S(1)} %get-tuple-element.70), channel_id=1, source_target_pairs={{0,256},{128,384},{256,0},{384,128},{1,257},{129,385},{257,1},{385... | collective-permute-start | bytes 196616 | tf_op jit(solution)/shard_map/ppermute | solution.py:270
  110.2 7.1 %collective-permute-start.13 = (bf16[64,512]{1,0:T(8,128)(2,1)S(1)}, bf16[64,512]{1,0:T(8,128)(2,1)S(1)}, u32[]{:S(2)}, u32[]{:S(2)}) collective-permute-start(bf16[64,512]{1,0:T(8,128)(2,1)S(1)} %get-tuple-element.71), channel_id=1, source_target_pairs={{0,128},{128,256},{256,384},{384,0},{1,129},{129,257},{257,385},{3... | collective-permute-start | bytes 196616 | tf_op jit(solution)/shard_map/ppermute | solution.py:270
  112.9 13.5 %all-to-all-start.4 = ((f32[8,2,1024]{2,1,0:T(2,128)}), f32[8,2,1024]{2,1,0:T(2,128)S(1)}, u32[]{:S(2)}, u32[]{:S(2)}) async-start(f32[8,2,1024]{2,1,0:T(2,128)} %add_up.1.refs_7_), calls=%async_computation.4 | async-start | bytes 131072 | tf_op jit(solution)/shard_map/all_to_all | solution.py:394
  117.3 1.1 copy-start.5
